TPU v7x, 128 devices: a whole 4x4x4 slice. The times are simulated.
128 devices in a mesh: section: 2 (over z_lo), dp: 32 (over x, y, core), tensor: 2 (over z_hi).
Axes of the slice: x: 4, y: 4, z: 4 (z_hi: 2, z_lo: 2; z = z_hi * 2 + z_lo), core: 2. Of those that a mesh axis runs over, the one named last changes fastest.
Arguments:
- inputs: bfloat16 [2, 2048, 1536], P(None, 'dp'), may hold values from -6 to 6
- cotangent: bfloat16 [2, 2048, 1536], P(None, 'dp'), may hold values from -6 to 6
- segments: int32 [2, 2048], replicated, may hold values from 0 to 4, as said below
- routes: int32 [2, 2048, 8], P(None, 'dp'), may hold values from 0 to 15, all different within a row; in each aligned block of 64 rows (0 to 63, 64 to 127, ..., all dimensions but the last counted through in order) at most 40 rows name the same one
- norm_first: float32 [2, 1536], P('section'), may hold values from 0.5 to 1.5
- w_query: bfloat16 [2, 1536, 1536], P('section', None, 'tensor'), may hold values from -0.15625 to 0.15625
- w_key: bfloat16 [2, 1536, 512], P('section', None, 'tensor'), may hold values from -0.15625 to 0.15625
- w_value: bfloat16 [2, 1536, 512], P('section', None, 'tensor'), may hold values from -0.15625 to 0.15625
- w_out: bfloat16 [2, 1536, 1536], P('section', 'tensor'), may hold values from -1.25 to 1.25
- norm_second: float32 [2, 1536], P('section'), may hold values from 0.5 to 1.5
- w_router: bfloat16 [2, 1536, 16], P('section'), may hold values from -0.078125 to 0.078125
- w_gate: bfloat16 [2, 64, 384, 512], P('section', 'dp', None, 'tensor'), may hold values from -0.15625 to 0.15625
- w_up: bfloat16 [2, 64, 384, 512], P('section', 'dp', None, 'tensor'), may hold values from -0.15625 to 0.15625
- w_down: bfloat16 [2, 64, 512, 384], P('section', 'dp', 'tensor'), may hold values from -1 to 1
Outputs:
- layer_outputs: float32 [2, 2, 2048, 1536], P('section', None, 'dp')
- input_grads: float32 [2, 2, 2048, 1536], P('section', None, 'dp')
- grad_norm_first: float32 [2, 1536], P('section')
- grad_w_query: float32 [2, 1536, 1536], P('section', None, 'tensor')
- grad_w_key: float32 [2, 1536, 512], P('section', None, 'tensor')
- grad_w_value: float32 [2, 1536, 512], P('section', None, 'tensor')
- grad_w_out: float32 [2, 1536, 1536], P('section', 'tensor')
- grad_norm_second: float32 [2, 1536], P('section')
- grad_w_router: float32 [2, 1536, 16], P('section')
- grad_w_gate: float32 [2, 64, 384, 512], P('section', 'dp', None, 'tensor')
- grad_w_up: float32 [2, 64, 384, 512], P('section', 'dp', None, 'tensor')
- grad_w_down: float32 [2, 64, 512, 384], P('section', 'dp', 'tensor')
Inputs may be any that keep to these rules, and one draw needn't show every extreme that they name: `segments`: each micro-batch is one sequence of 2048 tokens; document ids never fall along it, and one document runs from the tokens of the first index of dp to those of the last. `routes`: each token names 8 different experts; among the rows of one index of dp in one micro-batch no expert is named more than 40 times, a bound that some block reaches.
All inputs are finite; a program needn't handle non-finite values.
Results may differ from a plain program's by a relative error of at most 0.035.
Values may be sent and summed in bfloat16 or wider, within the bound.
No kernel may reach another device: no remote copies, remote signals or barrier semaphores. Data moves between devices by JAX's collectives and lax.ppermute only.
A program may use at most 256 MiB of HBM per device.

v0:
```python
import jax
import jax.numpy as jnp
from jax import lax
from jax.sharding import PartitionSpec as P

D = 1536
HD = 64
TOPK = 8
GROUP = 8
EXPERTS = 16
MICRO = 2


EPSILON = 1e-06
SCALE = 0.125
NEGATIVE = -1e30
HIGH = lax.Precision.HIGHEST


def over_pieces(shard, axis):
    tiles = lax.all_gather(shard, axis).astype(jnp.float32)
    return tiles.sum(axis=0)


def laid_out(tiles, dim):
    tiles = jnp.moveaxis(tiles, 0, dim)
    dims = tiles.shape
    return tiles.reshape(*dims[:dim], dims[dim] * dims[dim + 1], *dims[dim + 2 :])


def sent_to_all(shard, axis):
    copies = jnp.broadcast_to(shard, (lax.axis_size(axis), *shard.shape))
    return lax.all_to_all(copies, axis, split_axis=0, concat_axis=0, tiled=True)


def gather_directly(shard, axis, dim):
    return laid_out(sent_to_all(shard, axis), dim)


def swapped(block, axis, distance):
    count = lax.axis_size(axis)
    route = []
    for low in range(count):
        high = low | 1 << distance
        if high != low and high < count:
            route += [(low, high), (high, low)]
    return lax.ppermute(block, axis, route)


def from_behind(shard, axis, by):
    size = lax.axis_size(axis)
    pairs = [(i, i + by) for i in range(size) if 0 <= i + by < size]
    return lax.ppermute(shard, axis, pairs)


def norm_apply(value, gain):
    inverse = lax.rsqrt(jnp.mean(value * value, axis=-1, keepdims=True) + EPSILON)
    return value * inverse * gain


def norm_back(value, gain, grad):
    inverse = lax.rsqrt(jnp.mean(value * value, axis=-1, keepdims=True) + EPSILON)
    scaled = grad * gain
    inner = jnp.mean(scaled * value, axis=-1, keepdims=True)
    gain_grad = jnp.sum(grad * value * inverse, axis=0)
    return (inverse * scaled - inverse * inverse * inverse * value * inner, gain_grad)


def over_rows(left, right):
    return lax.dot_general(
        left, right, (((0,), (0,)), ((), ())), preferred_element_type=jnp.float32
    )


def against(left, right):
    return lax.dot_general(
        left, right, (((1,), (1,)), ((), ())), preferred_element_type=jnp.float32
    )


def route_targets(route_rows, tok_rows, slot_rows):
    flat = route_rows.reshape(-1)
    onehot = (flat[:, None] == jnp.arange(EXPERTS, dtype=jnp.int32)[None, :]).astype(jnp.int32)
    counts = jnp.cumsum(onehot, axis=0)
    slots = jnp.sum(onehot * (counts - 1), axis=1)
    targets = flat * slot_rows + slots
    source_rows = (
        jnp.full((EXPERTS * slot_rows,), tok_rows * TOPK, jnp.int32)
        .at[targets]
        .set(jnp.arange(tok_rows * TOPK, dtype=jnp.int32))
    )
    return (targets, source_rows)


def scores_of(query, keys, allowed):
    kv_count = keys.shape[1] // HD
    grouped = query.reshape(query.shape[0], kv_count, -1, HD)
    key_heads = keys.reshape(keys.shape[0], kv_count, HD)
    scores = (
        jnp.einsum("qkgd,tkd->kgqt", grouped, key_heads, preferred_element_type=jnp.float32) * SCALE
    )
    return jnp.where(allowed[None, None], scores, NEGATIVE)


def attend_forward(query, pairs, allowed):
    scores = scores_of(query, pairs[0], allowed)
    top = jnp.max(scores, axis=-1, keepdims=True)
    raised = jnp.exp(scores - top)
    total = jnp.sum(raised, axis=-1, keepdims=True)
    weights = (raised / total).astype(jnp.bfloat16)
    kv_count = pairs.shape[2] // HD
    value_heads = pairs[1].reshape(pairs.shape[1], kv_count, HD)
    mixed = jnp.einsum("kgqt,tkd->qkgd", weights, value_heads, preferred_element_type=jnp.float32)
    return (mixed.reshape(query.shape).astype(jnp.bfloat16), top + jnp.log(total))


def attend_backward(query, pairs, allowed, log_total, grad_mixed):
    count = query.shape[0]
    kv_count = pairs.shape[2] // HD
    scores = scores_of(query, pairs[0], allowed)
    weights = jnp.exp(scores - log_total)
    grouped = query.reshape(count, kv_count, -1, HD)
    grad_heads = grad_mixed.reshape(count, kv_count, -1, HD)
    key_heads = pairs[0].reshape(pairs.shape[1], kv_count, HD)
    value_heads = pairs[1].reshape(pairs.shape[1], kv_count, HD)
    grad_values = jnp.einsum(
        "kgqt,qkgd->tkd",
        weights.astype(jnp.bfloat16),
        grad_heads,
        preferred_element_type=jnp.float32,
    )
    grad_weights = jnp.einsum(
        "qkgd,tkd->kgqt", grad_heads, value_heads, preferred_element_type=jnp.float32
    )
    inner = jnp.sum(weights * grad_weights, axis=-1, keepdims=True)
    grad_scores = (weights * (grad_weights - inner)).astype(jnp.bfloat16)
    grad_query = (
        jnp.einsum("kgqt,tkd->qkgd", grad_scores, key_heads, preferred_element_type=jnp.float32)
        * SCALE
    )
    grad_keys = (
        jnp.einsum("kgqt,qkgd->tkd", grad_scores, grouped, preferred_element_type=jnp.float32)
        * SCALE
    )
    grad_pairs = jnp.stack(
        [grad_keys.reshape(pairs.shape[1], -1), grad_values.reshape(pairs.shape[1], -1)]
    )
    return (grad_query.reshape(query.shape), grad_pairs)


def remember(store, name, value, index, valid):
    if name not in store:
        store[name] = jnp.zeros((MICRO,) + value.shape, value.dtype)
    current = lax.dynamic_index_in_dim(store[name], index, 0, False)
    store[name] = lax.dynamic_update_index_in_dim(
        store[name], jnp.where(valid, value, current), index, 0
    )


def recall(store, name, index):
    return lax.dynamic_index_in_dim(store[name], index, 0, False)


def tensor_sum(value):
    return over_pieces(value.astype(jnp.bfloat16), "tensor").astype(jnp.float32)


def fetch_keys(pair):
    return gather_directly(pair, "dp", 1)


def return_keys(grad_pairs):
    return lax.psum_scatter(
        grad_pairs.astype(jnp.bfloat16), "dp", scatter_dimension=1, tiled=True
    ).astype(jnp.float32)


def bit_of(place, bit):
    return place // 2**bit % 2 == 1


def group_all(buffer):
    place = lax.axis_index("dp")
    levels = GROUP.bit_length() - 1
    blocks = buffer.reshape((2,) * levels + buffer.shape[1:])
    for bit in range(levels):
        axis = levels - 1 - bit
        upper_bit = bit_of(place, bit)
        lower_part = lax.index_in_dim(blocks, 0, axis, False)
        upper_part = lax.index_in_dim(blocks, 1, axis, False)
        kept_part = jnp.where(upper_bit, upper_part, lower_part)
        sent_part = jnp.where(upper_bit, lower_part, upper_part)
        arrived = swapped(sent_part, "dp", bit)
        blocks = jnp.stack(
            [jnp.where(upper_bit, arrived, kept_part), jnp.where(upper_bit, kept_part, arrived)],
            axis=axis,
        )
    return blocks.reshape(buffer.shape)


def replica_gather(weights, dim):
    place = lax.axis_index("dp")
    levels = (lax.axis_size("dp") // GROUP).bit_length() - 1
    base = GROUP.bit_length() - 1
    for step in range(levels):
        bit = base + step
        upper_bit = bit_of(place, bit)
        partner_part = swapped(weights, "dp", bit)
        weights = jnp.where(
            upper_bit,
            jnp.concatenate([partner_part, weights], dim),
            jnp.concatenate([weights, partner_part], dim),
        )
    return weights


def replica_scatter(grads, dim):
    place = lax.axis_index("dp")
    levels = (lax.axis_size("dp") // GROUP).bit_length() - 1
    base = GROUP.bit_length() - 1
    for step in reversed(range(levels)):
        bit = base + step
        upper_bit = bit_of(place, bit)
        half_size = grads.shape[dim] // 2
        lower_part = lax.slice_in_dim(grads, 0, half_size, axis=dim)
        upper_part = lax.slice_in_dim(grads, half_size, 2 * half_size, axis=dim)
        kept_part = jnp.where(upper_bit, upper_part, lower_part)
        sent_part = jnp.where(upper_bit, lower_part, upper_part)
        grads = kept_part + swapped(sent_part.astype(jnp.bfloat16), "dp", bit).astype(
            sent_part.dtype
        )
    return grads


def to_owners(buffer):
    return group_all(buffer)


def to_tokens(buffer):
    return group_all(buffer)


def per_device(
    inputs,
    cotangent,
    segments,
    routes,
    norm_first,
    w_query,
    w_key,
    w_value,
    w_out,
    norm_second,
    w_router,
    w_gate,
    w_up,
    w_down,
):
    sections = lax.axis_size("section")
    section = lax.axis_index("section")
    devices = lax.axis_size("dp")
    place = lax.axis_index("dp")
    tok_rows = inputs.shape[1]
    slot_rows = 5 * tok_rows // 8
    seq_length = tok_rows * devices
    gain_one = norm_first[0]
    query_local = w_query[0]
    key_local = w_key[0]
    value_local = w_value[0]
    out_local = w_out[0]
    gain_two = norm_second[0]
    router_local = w_router[0]
    both_local = replica_gather(jnp.stack([w_gate[0], w_up[0]]), 2)
    gate_local = both_local[0]
    up_local = both_local[1]
    down_local = replica_gather(w_down[0], 2)
    local_experts = gate_local.shape[0]
    ticks = MICRO + sections - 1
    query_places = place * tok_rows + jnp.arange(tok_rows, dtype=jnp.int32)
    key_places = jnp.arange(seq_length, dtype=jnp.int32)
    expert_ids = jnp.arange(EXPERTS, dtype=jnp.int32)
    blank_row = jnp.zeros((1, D), jnp.bfloat16)

    def allowed_for(labels):
        query_labels = labels[query_places]
        return (labels[None, :] == query_labels[:, None]) & (
            key_places[None, :] <= query_places[:, None]
        )

    saved = {}
    arriving = jnp.zeros((tok_rows, D), jnp.float32)
    for tick in range(ticks):
        batch = tick - section
        valid = (batch >= 0) & (batch < MICRO)
        index = jnp.clip(batch, 0, MICRO - 1)
        given = lax.dynamic_index_in_dim(inputs, index, 0, False).astype(jnp.float32)
        hidden = jnp.where(section == 0, given, arriving)
        labels = lax.dynamic_index_in_dim(segments, index, 0, False)
        route_rows = lax.dynamic_index_in_dim(routes, index, 0, False)
        activation = norm_apply(hidden, gain_one).astype(jnp.bfloat16)
        query = jnp.dot(activation, query_local, preferred_element_type=jnp.float32).astype(
            jnp.bfloat16
        )
        pair = jnp.stack(
            [
                jnp.dot(activation, key_local, preferred_element_type=jnp.float32),
                jnp.dot(activation, value_local, preferred_element_type=jnp.float32),
            ]
        ).astype(jnp.bfloat16)
        pairs = fetch_keys(pair)
        mixed, log_total = attend_forward(query, pairs, allowed_for(labels))
        middle = hidden + tensor_sum(jnp.dot(mixed, out_local, preferred_element_type=jnp.float32))
        second_input = norm_apply(middle, gain_two).astype(jnp.bfloat16)
        logits = jnp.dot(second_input, router_local, preferred_element_type=jnp.float32)
        picked = (route_rows[:, :, None] == expert_ids[None, None, :]).astype(jnp.float32)
        chosen = jnp.sum(picked * logits[:, None, :], axis=2)
        gates = jax.nn.softmax(chosen, axis=1)
        targets, source_rows = route_targets(route_rows, tok_rows, slot_rows)
        padded = jnp.concatenate([second_input, blank_row], axis=0)
        sending = padded[source_rows // TOPK].reshape(GROUP, local_experts, slot_rows, D)
        rows = to_owners(sending)
        gate_pre = jnp.einsum(
            "secd,edf->secf", rows, gate_local, preferred_element_type=jnp.float32
        )
        up_pre = jnp.einsum("secd,edf->secf", rows, up_local, preferred_element_type=jnp.float32)
        expert_middle_rows = (jax.nn.silu(gate_pre) * up_pre).astype(jnp.bfloat16)
        produced = jnp.einsum(
            "secf,efd->secd", expert_middle_rows, down_local, preferred_element_type=jnp.float32
        ).astype(jnp.bfloat16)
        gate_pre, up_pre, produced = (gate_pre, up_pre, produced)
        returned = (
            to_tokens(produced).reshape(EXPERTS * slot_rows, D)[targets].reshape(tok_rows, TOPK, D)
        )
        combined = jnp.sum(gates[:, :, None] * returned, axis=1)
        result = middle + tensor_sum(combined)
        remember(saved, "hidden", hidden, index, valid)
        remember(saved, "activation", activation, index, valid)
        remember(saved, "query", query, index, valid)
        remember(saved, "pairs", pairs, index, valid)
        remember(saved, "mixed", mixed, index, valid)
        remember(saved, "log_total", log_total, index, valid)
        remember(saved, "middle", middle, index, valid)
        remember(saved, "second_input", second_input, index, valid)
        remember(saved, "gates", gates, index, valid)
        remember(saved, "rows", rows, index, valid)
        remember(saved, "gate_pre", gate_pre, index, valid)
        remember(saved, "up_pre", up_pre, index, valid)
        remember(saved, "returned", returned, index, valid)
        remember(saved, "result", result, index, valid)
        arriving = from_behind(result.astype(jnp.bfloat16), "section", 1).astype(result.dtype)
    query_grad = jnp.zeros(query_local.shape, jnp.float32)
    key_grad = jnp.zeros(key_local.shape, jnp.float32)
    value_grad = jnp.zeros(value_local.shape, jnp.float32)
    out_grad = jnp.zeros(out_local.shape, jnp.float32)
    router_grad = jnp.zeros(router_local.shape, jnp.float32)
    gain_one_grad = jnp.zeros(gain_one.shape, jnp.float32)
    gain_two_grad = jnp.zeros(gain_two.shape, jnp.float32)
    gate_grad = jnp.zeros(gate_local.shape, jnp.float32)
    up_grad = jnp.zeros(up_local.shape, jnp.float32)
    down_grad = jnp.zeros(down_local.shape, jnp.float32)
    router_wide = router_local.astype(jnp.float32)
    backward = {}
    arriving_back = jnp.zeros((tok_rows, D), jnp.float32)
    for tick in range(ticks):
        batch = tick - (sections - 1 - section)
        valid = (batch >= 0) & (batch < MICRO)
        useful = jnp.where(valid, 1.0, 0.0).astype(jnp.float32)
        index = jnp.clip(batch, 0, MICRO - 1)
        given = lax.dynamic_index_in_dim(cotangent, index, 0, False).astype(jnp.float32)
        grad_output = jnp.where(section == sections - 1, given, arriving_back)
        labels = lax.dynamic_index_in_dim(segments, index, 0, False)
        route_rows = lax.dynamic_index_in_dim(routes, index, 0, False)
        hidden = recall(saved, "hidden", index)
        activation = recall(saved, "activation", index)
        query = recall(saved, "query", index)
        mixed = recall(saved, "mixed", index)
        log_total = recall(saved, "log_total", index)
        middle = recall(saved, "middle", index)
        second_input = recall(saved, "second_input", index)
        gates = recall(saved, "gates", index)
        rows = recall(saved, "rows", index)
        gate_pre = recall(saved, "gate_pre", index)
        up_pre = recall(saved, "up_pre", index)
        returned = recall(saved, "returned", index)
        targets, source_rows = route_targets(route_rows, tok_rows, slot_rows)
        picked = (route_rows[:, :, None] == expert_ids[None, None, :]).astype(jnp.float32)
        gate_part = jnp.sum(grad_output[:, None, :] * returned, axis=2)
        grad_routes = (
            (gates[:, :, None] * grad_output[:, None, :])
            .astype(jnp.bfloat16)
            .reshape(tok_rows * TOPK, D)
        )
        grad_sending = jnp.concatenate([grad_routes, blank_row], axis=0)[source_rows].reshape(
            GROUP, local_experts, slot_rows, D
        )
        grad_produced = to_owners(grad_sending)
        sigmoid_gate = jax.nn.sigmoid(gate_pre)
        activated = gate_pre * sigmoid_gate
        middle_rows = (activated * up_pre).astype(jnp.bfloat16)
        grad_middle_rows = jnp.einsum(
            "secd,efd->secf", grad_produced, down_local, preferred_element_type=jnp.float32
        )
        grad_gate_pre = (
            grad_middle_rows * up_pre * sigmoid_gate * (1.0 + gate_pre * (1.0 - sigmoid_gate))
        ).astype(jnp.bfloat16)
        grad_up_pre = (grad_middle_rows * activated).astype(jnp.bfloat16)
        down_grad = down_grad + useful * jnp.einsum(
            "secf,secd->efd", middle_rows, grad_produced, preferred_element_type=jnp.float32
        )
        gate_grad = gate_grad + useful * jnp.einsum(
            "secd,secf->edf", rows, grad_gate_pre, preferred_element_type=jnp.float32
        )
        up_grad = up_grad + useful * jnp.einsum(
            "secd,secf->edf", rows, grad_up_pre, preferred_element_type=jnp.float32
        )
        grad_rows = (
            jnp.einsum(
                "secf,edf->secd", grad_gate_pre, gate_local, preferred_element_type=jnp.float32
            )
            + jnp.einsum(
                "secf,edf->secd", grad_up_pre, up_local, preferred_element_type=jnp.float32
            )
        ).astype(jnp.bfloat16)
        back_rows = (
            to_tokens(grad_rows).reshape(EXPERTS * slot_rows, D)[targets].reshape(tok_rows, TOPK, D)
        )
        grad_part = jnp.sum(back_rows, axis=1, dtype=jnp.float32)
        grad_second, grad_gates = (
            lax.psum(grad_part.astype(jnp.bfloat16), "tensor").astype(jnp.float32),
            lax.psum(gate_part.astype(jnp.bfloat16), "tensor").astype(jnp.float32),
        )
        inner = jnp.sum(gates * grad_gates, axis=1, keepdims=True)
        grad_chosen = gates * (grad_gates - inner)
        grad_logits = jnp.sum(grad_chosen[:, :, None] * picked, axis=1)
        router_grad = router_grad + useful * lax.dot_general(
            second_input.astype(jnp.float32), grad_logits, (((0,), (0,)), ((), ())), precision=HIGH
        )
        grad_second = grad_second + lax.dot_general(
            grad_logits, router_wide, (((1,), (1,)), ((), ())), precision=HIGH
        )
        grad_from_norm, gain_two_part = norm_back(middle, gain_two, grad_second)
        gain_two_grad = gain_two_grad + useful * gain_two_part
        grad_middle = grad_output + grad_from_norm
        grad_branch = grad_middle.astype(jnp.bfloat16)
        out_grad = out_grad + useful * over_rows(mixed, grad_branch)
        grad_mixed = against(grad_branch, out_local).astype(jnp.bfloat16)
        pairs = recall(saved, "pairs", index)
        grad_query, grad_pairs = attend_backward(
            query, pairs, allowed_for(labels), log_total, grad_mixed
        )
        grad_pair = return_keys(grad_pairs).astype(jnp.bfloat16)
        grad_query = grad_query.astype(jnp.bfloat16)
        query_grad = query_grad + useful * over_rows(activation, grad_query)
        key_grad = key_grad + useful * over_rows(activation, grad_pair[0])
        value_grad = value_grad + useful * over_rows(activation, grad_pair[1])
        grad_activation = (
            against(grad_query, query_local)
            + against(grad_pair[0], key_local)
            + against(grad_pair[1], value_local)
        )
        grad_activation = tensor_sum(grad_activation)
        grad_from_first, gain_one_part = norm_back(hidden, gain_one, grad_activation)
        gain_one_grad = gain_one_grad + useful * gain_one_part
        grad_input = grad_middle + grad_from_first
        remember(backward, "grad_input", grad_input, index, valid)
        arriving_back = from_behind(grad_input.astype(jnp.bfloat16), "section", -1).astype(
            grad_input.dtype
        )
    sums = (
        lax.psum(query_grad.astype(jnp.bfloat16), "dp").astype(jnp.float32),
        lax.psum(key_grad.astype(jnp.bfloat16), "dp").astype(jnp.float32),
        lax.psum(value_grad.astype(jnp.bfloat16), "dp").astype(jnp.float32),
        lax.psum(out_grad.astype(jnp.bfloat16), "dp").astype(jnp.float32),
        lax.psum(gain_one_grad.astype(jnp.bfloat16), "dp").astype(jnp.float32),
        lax.psum(gain_two_grad.astype(jnp.bfloat16), "dp").astype(jnp.float32),
        lax.psum(router_grad.astype(jnp.bfloat16), "dp").astype(jnp.float32),
    )
    both_grads = replica_scatter(jnp.stack([gate_grad, up_grad]), 2)
    down_part = replica_scatter(down_grad, 2)
    return (
        saved["result"][None],
        backward["grad_input"][None],
        sums[4][None],
        sums[0][None],
        sums[1][None],
        sums[2][None],
        sums[3][None],
        sums[5][None],
        sums[6][None],
        both_grads[0][None],
        both_grads[1][None],
        down_part[None],
    )


def solution(mesh):
    in_specs = (
        P(None, "dp", None),
        P(None, "dp", None),
        P(),
        P(None, "dp", None),
        P("section", None),
        P("section", None, "tensor"),
        P("section", None, "tensor"),
        P("section", None, "tensor"),
        P("section", "tensor", None),
        P("section", None),
        P("section", None, None),
        P("section", "dp", None, "tensor"),
        P("section", "dp", None, "tensor"),
        P("section", "dp", "tensor", None),
    )
    out_specs = (
        P("section", None, "dp", None),
        P("section", None, "dp", None),
        P("section", None),
        P("section", None, "tensor"),
        P("section", None, "tensor"),
        P("section", None, "tensor"),
        P("section", "tensor", None),
        P("section", None),
        P("section", None, None),
        P("section", "dp", None, "tensor"),
        P("section", "dp", None, "tensor"),
        P("section", "dp", "tensor", None),
    )
    return jax.shard_map(
        per_device, mesh=mesh, in_specs=in_specs, out_specs=out_specs, check_vma=False
    )
```

profile of v0, /device:TPU:1, one launch (start us, length us, event | category | flops | bytes accessed | tf_op | source)
XLA Modules:
  0.0 1922.1 jit_solution(8725711401058233181)
XLA Ops:
  38.0 13.0 all-to-all-done
  95.1 14.2 collective-permute-done.2
  123.7 32.6 %collective-permute-done = bf16[2,256,384]{2,1,0:T(8,128)(2,1)} collective-permute-done((bf16[2,256,384]{2,1,0:T(8,128)(2,1)}, bf16[2,256,384]{2,1,0:T(8,128)(2,1)}, u32[]{:S(2)}, u32[]{:S(2)}) %collective-permute-start) | collective-permute-done | bytes 393248 | tf_op jit(solution)/shard_map/ppermute | solution.py:47
  190.2 18.5 collective-permute-done.8
  214.6 21.5 %collective-permute-done.9 = bf16[2,2,2,40,1536]{4,3,2,1,0:T(8,128)(2,1)} collective-permute-done((bf16[2,2,2,40,1536]{4,3,2,1,0:T(8,128)(2,1)}, bf16[2,2,2,40,1536]{4,3,2,1,0:T(8,128)(2,1)}, u32[]{:S(2)}, u32[]{:S(2)}) %collective-permute-start.9) | collective-permute-done | bytes 983072 | tf_op jit(solution)/shard_map/ppermute | solution.py:47
  281.5 20.7 %all-to-all-done.1 = bf16[32,2,64,256]{3,2,1,0:T(8,128)(2,1)} async-done(((bf16[32,2,64,256]{3,2,1,0:T(8,128)(2,1)}), bf16[32,2,64,256]{3,2,1,0:T(8,128)(2,1)}, u32[]{:S(2)}, u32[]{:S(2)}) %all-to-all-start.1) | async-done | bytes 2097184 | tf_op jit(solution)/shard_map/all_to_all | solution.py:33
  343.0 23.0 %collective-permute-done.12 = bf16[2,2,2,40,1536]{4,3,2,1,0:T(8,128)(2,1)S(1)} collective-permute-done((bf16[2,2,2,40,1536]{4,3,2,1,0:T(8,128)(2,1)S(1)}, bf16[2,2,2,40,1536]{4,3,2,1,0:T(8,128)(2,1)S(1)}, u32[]{:S(2)}, u32[]{:S(2)}) %collective-permute-start.12) | collective-permute-done | bytes 983072 | tf_op jit(solution)/shard_map/ppermute | solution.py:47
  368.2 21.7 %collective-permute-done.13 = bf16[2,2,2,40,1536]{4,3,2,1,0:T(8,128)(2,1)S(1)} collective-permute-done((bf16[2,2,2,40,1536]{4,3,2,1,0:T(8,128)(2,1)S(1)}, bf16[2,2,2,40,1536]{4,3,2,1,0:T(8,128)(2,1)S(1)}, u32[]{:S(2)}, u32[]{:S(2)}) %collective-permute-start.13) | collective-permute-done | bytes 983072 | tf_op jit(solution)/shard_map/ppermute | solution.py:47
  404.4 22.8 %collective-permute-done.15 = bf16[2,2,2,40,1536]{4,3,2,1,0:T(8,128)(2,1)} collective-permute-done((bf16[2,2,2,40,1536]{4,3,2,1,0:T(8,128)(2,1)}, bf16[2,2,2,40,1536]{4,3,2,1,0:T(8,128)(2,1)}, u32[]{:S(2)}, u32[]{:S(2)}) %collective-permute-start.15) | collective-permute-done | bytes 983072 | tf_op jit(solution)/shard_map/ppermute | solution.py:47
  435.0 20.5 %collective-permute-done.16 = bf16[2,2,2,40,1536]{4,3,2,1,0:T(8,128)(2,1)} collective-permute-done((bf16[2,2,2,40,1536]{4,3,2,1,0:T(8,128)(2,1)}, bf16[2,2,2,40,1536]{4,3,2,1,0:T(8,128)(2,1)}, u32[]{:S(2)}, u32[]{:S(2)}) %collective-permute-start.16) | collective-permute-done | bytes 983072 | tf_op jit(solution)/shard_map/ppermute | solution.py:47
  505.5 16.6 all-to-all-done.2
  563.0 23.0 %collective-permute-done.19 = bf16[2,2,2,40,1536]{4,3,2,1,0:T(8,128)(2,1)S(1)} collective-permute-done((bf16[2,2,2,40,1536]{4,3,2,1,0:T(8,128)(2,1)S(1)}, bf16[2,2,2,40,1536]{4,3,2,1,0:T(8,128)(2,1)S(1)}, u32[]{:S(2)}, u32[]{:S(2)}) %collective-permute-start.19) | collective-permute-done | bytes 983072 | tf_op jit(solution)/shard_map/ppermute | solution.py:47
  588.3 21.7 %collective-permute-done.20 = bf16[2,2,2,40,1536]{4,3,2,1,0:T(8,128)(2,1)S(1)} collective-permute-done((bf16[2,2,2,40,1536]{4,3,2,1,0:T(8,128)(2,1)S(1)}, bf16[2,2,2,40,1536]{4,3,2,1,0:T(8,128)(2,1)S(1)}, u32[]{:S(2)}, u32[]{:S(2)}) %collective-permute-start.20) | collective-permute-done | bytes 983072 | tf_op jit(solution)/shard_map/ppermute | solution.py:47
  631.8 19.7 %collective-permute-done.22 = bf16[2,2,2,40,1536]{4,3,2,1,0:T(8,128)(2,1)S(1)} collective-permute-done((bf16[2,2,2,40,1536]{4,3,2,1,0:T(8,128)(2,1)S(1)}, bf16[2,2,2,40,1536]{4,3,2,1,0:T(8,128)(2,1)S(1)}, u32[]{:S(2)}, u32[]{:S(2)}) %collective-permute-start.22) | collective-permute-done | bytes 983072 | tf_op jit(solution)/shard_map/ppermute | solution.py:47
  657.4 20.0 %collective-permute-done.23 = bf16[2,2,2,40,1536]{4,3,2,1,0:T(8,128)(2,1)} collective-permute-done((bf16[2,2,2,40,1536]{4,3,2,1,0:T(8,128)(2,1)}, bf16[2,2,2,40,1536]{4,3,2,1,0:T(8,128)(2,1)}, u32[]{:S(2)}, u32[]{:S(2)}) %collective-permute-start.23) | collective-permute-done | bytes 983072 | tf_op jit(solution)/shard_map/ppermute | solution.py:47
  715.7 22.6 %collective-permute-done.25 = bf16[2,2,2,40,1536]{4,3,2,1,0:T(8,128)(2,1)S(1)} collective-permute-done((bf16[2,2,2,40,1536]{4,3,2,1,0:T(8,128)(2,1)S(1)}, bf16[2,2,2,40,1536]{4,3,2,1,0:T(8,128)(2,1)S(1)}, u32[]{:S(2)}, u32[]{:S(2)}) %collective-permute-start.25) | collective-permute-done | bytes 983072 | tf_op jit(solution)/shard_map/ppermute | solution.py:47
  741.4 23.0 %collective-permute-done.26 = bf16[2,2,2,40,1536]{4,3,2,1,0:T(8,128)(2,1)} collective-permute-done((bf16[2,2,2,40,1536]{4,3,2,1,0:T(8,128)(2,1)}, bf16[2,2,2,40,1536]{4,3,2,1,0:T(8,128)(2,1)}, u32[]{:S(2)}, u32[]{:S(2)}) %collective-permute-start.26) | collective-permute-done | bytes 983072 | tf_op jit(solution)/shard_map/ppermute | solution.py:47
  797.1 17.1 collective-permute-done.28
  856.3 29.7 %all-reduce.19.cloned.1.call-done = bf16[64,1536]{1,0:T(8,128)(2,1)} async-done(((bf16[64,1536]{1,0:T(8,128)(2,1)}), bf16[64,1536]{1,0:T(8,128)(2,1)}) %all-reduce.19.cloned.1.call-update) | async-done | bytes 196624 | tf_op jit(solution)/shard_map/psum | solution.py:429
  933.1 96.5 %all-reduce.25.cloned.1.call-done = bf16[2,2048,256]{2,0,1:T(2,128)(2,1)} async-done(((bf16[2,2048,256]{2,0,1:T(2,128)(2,1)}), bf16[2,2048,256]{2,0,1:T(2,128)(2,1)}) %all-reduce.25.cloned.1.call-update) | async-done | bytes 2097168
  1097.9 11.1 collective-permute-done.32
  1171.1 12.4 collective-permute-done.35
  1188.7 17.3 collective-permute-done.36
  1217.6 33.9 %all-reduce.21.cloned.1.call-done = bf16[64,1536]{1,0:T(8,128)(2,1)} async-done(((bf16[64,1536]{1,0:T(8,128)(2,1)}), bf16[64,1536]{1,0:T(8,128)(2,1)}) %all-reduce.21.cloned.1.call-update) | async-done | bytes 196624 | tf_op jit(solution)/shard_map/psum | solution.py:429
  1297.0 98.1 %all-reduce.27.cloned.1.call-done = bf16[2,2048,256]{2,0,1:T(2,128)(2,1)} async-done(((bf16[2,2048,256]{2,0,1:T(2,128)(2,1)}), bf16[2,2048,256]{2,0,1:T(2,128)(2,1)}) %all-reduce.27.cloned.1.call-update) | async-done | bytes 2097168
  1459.9 11.1 collective-permute-done.39
  1480.4 14.1 collective-permute-done.40
  1516.8 14.4 collective-permute-done.42
  1538.6 21.1 %collective-permute-done.44 = bf16[2,2,768,256]{3,2,1,0:T(8,128)(2,1)S(1)} collective-permute-done((bf16[2,2,768,256]{3,2,1,0:T(8,128)(2,1)S(1)}, bf16[2,2,768,256]{3,2,1,0:T(8,128)(2,1)S(1)}, u32[]{:S(2)}, u32[]{:S(2)}) %collective-permute-start.44) | collective-permute-done | bytes 1572896 | tf_op jit(solution)/shard_map/ppermute | solution.py:47
  1577.6 28.4 %all-reduce.23.cloned.1.call-done = bf16[64,1536]{1,0:T(8,128)(2,1)} async-done(((bf16[64,1536]{1,0:T(8,128)(2,1)}), bf16[64,1536]{1,0:T(8,128)(2,1)}) %all-reduce.23.cloned.1.call-update) | async-done | bytes 196624 | tf_op jit(solution)/shard_map/psum | solution.py:429
  1657.9 93.8 %all-reduce.29.cloned.1.call-done = bf16[2,2048,256]{2,0,1:T(2,128)(2,1)} async-done(((bf16[2,2048,256]{2,0,1:T(2,128)(2,1)}), bf16[2,2048,256]{2,0,1:T(2,128)(2,1)}) %all-reduce.29.cloned.1.call-update) | async-done | bytes 2097168
  1777.0 124.1 %all-reduce.9 = (bf16[1,1536]{1,0:T(2,128)(2,1)S(1)}, bf16[1,1536]{1,0:T(2,128)(2,1)S(1)}, bf16[1,1536,16]{1,2,0:T(8,128)(2,1)S(1)}) all-reduce(bf16[1,1536]{1,0:T(2,128)(2,1)S(1)} %broadcast_in_dim.394, bf16[1,1536]{1,0:T(2,128)(2,1)S(1)} %broadcast_in_dim.406, ...), channel_id=1, replica_groups=mesh['section'=2,'dp'=32,'tensor'=2] {'dp'}, use_global_device_ids=true, to_apply=%region_96.97 | all-reduce | flops 27648 | bytes 110592 | tf_op jit(solution)/shard_map/psum | solution.py:474
  (1214 shorter events, 924.5 us)
Async XLA Ops:
  13.9 37.1 %all-to-all-start = ((bf16[32,2,64,256]{3,2,1,0:T(8,128)(2,1)}), bf16[32,2,64,256]{3,2,1,0:T(8,128)(2,1)}, u32[]{:S(2)}, u32[]{:S(2)}) async-start(bf16[32,2,64,256]{3,2,1,0:T(8,128)(2,1)} %broadcast_in_dim.354), calls=%async_computation | async-start | bytes 4194304 | tf_op jit(solution)/shard_map/all_to_all | solution.py:33
  95.1 23.3 %collective-permute-start.5 = (bf16[2,2,2,40,1536]{4,3,1,2,0:T(8,128)(2,1)}, bf16[2,2,2,40,1536]{4,3,1,2,0:T(8,128)(2,1)}, u32[]{:S(2)}, u32[]{:S(2)}) collective-permute-start(bf16[2,2,2,40,1536]{4,3,1,2,0:T(8,128)(2,1)} %select_bitcast_fusion.43), channel_id=1, source_target_pairs={{0,4},{4,0},{2,6},{6,2},{8,12},{12,8},{10,14},{14,10},{16,20},{20,... | collective-permute-start | bytes 2949128 | tf_op jit(solution)/shard_map/ppermute | solution.py:47
  112.7 48.5 %collective-permute-start.3 = (bf16[2,2,768,256]{3,2,1,0:T(8,128)(2,1)}, bf16[2,2,768,256]{3,2,1,0:T(8,128)(2,1)}, u32[]{:S(2)}, u32[]{:S(2)}) collective-permute-start(bf16[2,2,768,256]{3,2,1,0:T(8,128)(2,1)} %maximum_select_fusion.2), channel_id=1, source_target_pairs={{0,32},{32,0},{2,34},{34,2},{4,36},{36,4},{6,38},{38,6},{8,40},{40... | collective-permute-start | bytes 4718600 | tf_op jit(solution)/shard_map/ppermute | solution.py:47
  122.8 41.9 %collective-permute-start.6 = (bf16[2,2,2,40,1536]{4,3,1,0,2:T(8,128)(2,1)}, bf16[2,2,2,40,1536]{4,3,1,0,2:T(8,128)(2,1)}, u32[]{:S(2)}, u32[]{:S(2)}) collective-permute-start(bf16[2,2,2,40,1536]{4,3,1,0,2:T(8,128)(2,1)} %select_bitcast_fusion.42), channel_id=1, source_target_pairs={{0,8},{8,0},{2,10},{10,2},{4,12},{12,4},{6,14},{14,6},{16,24},{24,... | collective-permute-start | bytes 2949128 | tf_op jit(solution)/shard_map/ppermute | solution.py:47
  123.4 32.9 %collective-permute-start = (bf16[2,256,384]{2,1,0:T(8,128)(2,1)}, bf16[2,256,384]{2,1,0:T(8,128)(2,1)}, u32[]{:S(2)}, u32[]{:S(2)}) collective-permute-start(bf16[2,256,384]{2,1,0:T(8,128)(2,1)} %bitcast.21), channel_id=1, source_target_pairs={{0,16},{16,0},{2,18},{18,2},{4,20},{20,4},{6,22},{22,6},{8,24},{24... | collective-permute-start | bytes 1179656 | tf_op jit(solution)/shard_map/ppermute | solution.py:47
  185.4 23.3 %collective-permute-start.8 = (bf16[2,2,2,40,1536]{4,3,2,1,0:T(8,128)(2,1)}, bf16[2,2,2,40,1536]{4,3,2,1,0:T(8,128)(2,1)}, u32[]{:S(2)}, u32[]{:S(2)}) collective-permute-start(bf16[2,2,2,40,1536]{4,3,2,1,0:T(8,128)(2,1)} %select_bitcast_fusion.40), channel_id=1, source_target_pairs={{0,4},{4,0},{2,6},{6,2},{8,12},{12,8},{10,14},{14,10},{16,20},{20,... | collective-permute-start | bytes 2949128 | tf_op jit(solution)/shard_map/ppermute | solution.py:47
  212.3 23.9 %collective-permute-start.9 = (bf16[2,2,2,40,1536]{4,3,2,1,0:T(8,128)(2,1)}, bf16[2,2,2,40,1536]{4,3,2,1,0:T(8,128)(2,1)}, u32[]{:S(2)}, u32[]{:S(2)}) collective-permute-start(bf16[2,2,2,40,1536]{4,3,2,1,0:T(8,128)(2,1)} %fusion.258), channel_id=1, source_target_pairs={{0,8},{8,0},{2,10},{10,2},{4,12},{12,4},{6,14},{14,6},{16,24},{24,... | collective-permute-start | bytes 2949128 | tf_op jit(solution)/shard_map/ppermute | solution.py:47
  264.8 37.5 %all-to-all-start.1 = ((bf16[32,2,64,256]{3,2,1,0:T(8,128)(2,1)}), bf16[32,2,64,256]{3,2,1,0:T(8,128)(2,1)}, u32[]{:S(2)}, u32[]{:S(2)}) async-start(bf16[32,2,64,256]{3,2,1,0:T(8,128)(2,1)} %broadcast_in_dim.358), calls=%async_computation.1 | async-start | bytes 4194304 | tf_op jit(solution)/shard_map/all_to_all | solution.py:33
  366.3 23.6 %collective-permute-start.13 = (bf16[2,2,2,40,1536]{4,3,2,1,0:T(8,128)(2,1)S(1)}, bf16[2,2,2,40,1536]{4,3,2,1,0:T(8,128)(2,1)S(1)}, u32[]{:S(2)}, u32[]{:S(2)}) collective-permute-start(bf16[2,2,2,40,1536]{4,3,2,1,0:T(8,128)(2,1)S(1)} %fusion.257), channel_id=1, source_target_pairs={{0,8},{8,0},{2,10},{10,2},{4,12},{12,4},{6,14},{14,6},{16,24},{24,... | collective-permute-start | bytes 2949128 | tf_op jit(solution)/shard_map/ppermute | solution.py:47
  404.0 23.3 %collective-permute-start.15 = (bf16[2,2,2,40,1536]{4,3,2,1,0:T(8,128)(2,1)}, bf16[2,2,2,40,1536]{4,3,2,1,0:T(8,128)(2,1)}, u32[]{:S(2)}, u32[]{:S(2)}) collective-permute-start(bf16[2,2,2,40,1536]{4,3,2,1,0:T(8,128)(2,1)} %select_bitcast_fusion.32), channel_id=1, source_target_pairs={{0,4},{4,0},{2,6},{6,2},{8,12},{12,8},{10,14},{14,10},{16,20},{20,... | collective-permute-start | bytes 2949128 | tf_op jit(solution)/shard_map/ppermute | solution.py:47
  431.6 23.9 %collective-permute-start.16 = (bf16[2,2,2,40,1536]{4,3,2,1,0:T(8,128)(2,1)}, bf16[2,2,2,40,1536]{4,3,2,1,0:T(8,128)(2,1)}, u32[]{:S(2)}, u32[]{:S(2)}) collective-permute-start(bf16[2,2,2,40,1536]{4,3,2,1,0:T(8,128)(2,1)} %fusion.256), channel_id=1, source_target_pairs={{0,8},{8,0},{2,10},{10,2},{4,12},{12,4},{6,14},{14,6},{16,24},{24,... | collective-permute-start | bytes 2949128 | tf_op jit(solution)/shard_map/ppermute | solution.py:47
  485.0 37.0 %all-to-all-start.2 = ((bf16[32,2,64,256]{3,2,1,0:T(8,128)(2,1)}), bf16[32,2,64,256]{3,2,1,0:T(8,128)(2,1)}, u32[]{:S(2)}, u32[]{:S(2)}) async-start(bf16[32,2,64,256]{3,2,1,0:T(8,128)(2,1)} %broadcast_in_dim.363), calls=%async_computation.2 | async-start | bytes 4194304 | tf_op jit(solution)/shard_map/all_to_all | solution.py:33
  493.6 392.4 %all-reduce.19.cloned.1.call-start = ((), (), s32[]{:S(2)}) async-start(), calls=%async_computation.3 | async-start | bytes 393216 | tf_op jit(solution)/shard_map/psum | solution.py:429
  586.4 23.6 %collective-permute-start.20 = (bf16[2,2,2,40,1536]{4,3,2,1,0:T(8,128)(2,1)S(1)}, bf16[2,2,2,40,1536]{4,3,2,1,0:T(8,128)(2,1)S(1)}, u32[]{:S(2)}, u32[]{:S(2)}) collective-permute-start(bf16[2,2,2,40,1536]{4,3,2,1,0:T(8,128)(2,1)S(1)} %fusion.255), channel_id=1, source_target_pairs={{0,8},{8,0},{2,10},{10,2},{4,12},{12,4},{6,14},{14,6},{16,24},{24,... | collective-permute-start | bytes 2949128 | tf_op jit(solution)/shard_map/ppermute | solution.py:47
  628.0 23.5 %collective-permute-start.22 = (bf16[2,2,2,40,1536]{4,3,2,1,0:T(8,128)(2,1)S(1)}, bf16[2,2,2,40,1536]{4,3,2,1,0:T(8,128)(2,1)S(1)}, u32[]{:S(2)}, u32[]{:S(2)}) collective-permute-start(bf16[2,2,2,40,1536]{4,3,2,1,0:T(8,128)(2,1)S(1)} %select_bitcast_fusion.24), channel_id=1, source_target_pairs={{0,4},{4,0},{2,6},{6,2},{8,12},{12,8},{10,14},{14,10},{16,20},{20,... | collective-permute-start | bytes 2949128 | tf_op jit(solution)/shard_map/ppermute | solution.py:47
  652.8 24.5 %collective-permute-start.23 = (bf16[2,2,2,40,1536]{4,3,2,1,0:T(8,128)(2,1)}, bf16[2,2,2,40,1536]{4,3,2,1,0:T(8,128)(2,1)}, u32[]{:S(2)}, u32[]{:S(2)}) collective-permute-start(bf16[2,2,2,40,1536]{4,3,2,1,0:T(8,128)(2,1)} %fusion.252), channel_id=1, source_target_pairs={{0,8},{8,0},{2,10},{10,2},{4,12},{12,4},{6,14},{14,6},{16,24},{24,... | collective-permute-start | bytes 2949128 | tf_op jit(solution)/shard_map/ppermute | solution.py:47
  740.6 23.9 %collective-permute-start.26 = (bf16[2,2,2,40,1536]{4,3,2,1,0:T(8,128)(2,1)}, bf16[2,2,2,40,1536]{4,3,2,1,0:T(8,128)(2,1)}, u32[]{:S(2)}, u32[]{:S(2)}) collective-permute-start(bf16[2,2,2,40,1536]{4,3,2,1,0:T(8,128)(2,1)} %fusion.254), channel_id=1, source_target_pairs={{0,8},{8,0},{2,10},{10,2},{4,12},{12,4},{6,14},{14,6},{16,24},{24,... | collective-permute-start | bytes 2949128 | tf_op jit(solution)/shard_map/ppermute | solution.py:47
  790.5 23.7 %collective-permute-start.28 = (bf16[2,2,2,40,1536]{4,3,2,1,0:T(8,128)(2,1)}, bf16[2,2,2,40,1536]{4,3,2,1,0:T(8,128)(2,1)}, u32[]{:S(2)}, u32[]{:S(2)}) collective-permute-start(bf16[2,2,2,40,1536]{4,3,2,1,0:T(8,128)(2,1)} %select_bitcast_fusion.16), channel_id=1, source_target_pairs={{0,4},{4,0},{2,6},{6,2},{8,12},{12,8},{10,14},{14,10},{16,20},{20,... | collective-permute-start | bytes 2949128 | tf_op jit(solution)/shard_map/ppermute | solution.py:47
  818.6 24.3 %collective-permute-start.29 = (bf16[2,2,2,40,1536]{4,3,2,1,0:T(8,128)(2,1)}, bf16[2,2,2,40,1536]{4,3,2,1,0:T(8,128)(2,1)}, u32[]{:S(2)}, u32[]{:S(2)}) collective-permute-start(bf16[2,2,2,40,1536]{4,3,2,1,0:T(8,128)(2,1)} %fusion.253), channel_id=1, source_target_pairs={{0,8},{8,0},{2,10},{10,2},{4,12},{12,4},{6,14},{14,6},{16,24},{24,... | collective-permute-start | bytes 2949128 | tf_op jit(solution)/shard_map/ppermute | solution.py:47
  856.0 173.6 %all-reduce.25.cloned.1.call-start = ((), (), s32[]{:S(2)}) async-start(), calls=%async_computation.6 | async-start | bytes 4194304
  922.7 328.8 %all-reduce.21.cloned.1.call-start = ((), (), s32[]{:S(2)}) async-start(), calls=%async_computation.4 | async-start | bytes 393216 | tf_op jit(solution)/shard_map/psum | solution.py:429
  1085.4 23.7 %collective-permute-start.32 = (bf16[2,2,2,40,1536]{4,3,2,1,0:T(8,128)(2,1)}, bf16[2,2,2,40,1536]{4,3,2,1,0:T(8,128)(2,1)}, u32[]{:S(2)}, u32[]{:S(2)}) collective-permute-start(bf16[2,2,2,40,1536]{4,3,2,1,0:T(8,128)(2,1)} %select_bitcast_fusion.12), channel_id=1, source_target_pairs={{0,4},{4,0},{2,6},{6,2},{8,12},{12,8},{10,14},{14,10},{16,20},{20,... | collective-permute-start | bytes 2949128 | tf_op jit(solution)/shard_map/ppermute | solution.py:47
  1113.5 24.3 %collective-permute-start.33 = (bf16[2,2,2,40,1536]{4,3,2,1,0:T(8,128)(2,1)}, bf16[2,2,2,40,1536]{4,3,2,1,0:T(8,128)(2,1)}, u32[]{:S(2)}, u32[]{:S(2)}) collective-permute-start(bf16[2,2,2,40,1536]{4,3,2,1,0:T(8,128)(2,1)} %select_bitcast_fusion.11), channel_id=1, source_target_pairs={{0,8},{8,0},{2,10},{10,2},{4,12},{12,4},{6,14},{14,6},{16,24},{24,... | collective-permute-start | bytes 2949128 | tf_op jit(solution)/shard_map/ppermute | solution.py:47
  1217.3 177.7 %all-reduce.27.cloned.1.call-start = ((), (), s32[]{:S(2)}) async-start(), calls=%async_computation.7 | async-start | bytes 4194304
  1288.2 317.9 %all-reduce.23.cloned.1.call-start = ((), (), s32[]{:S(2)}) async-start(), calls=%async_computation.5 | async-start | bytes 393216 | tf_op jit(solution)/shard_map/psum | solution.py:429
  1505.7 29.2 %collective-permute-start.46 = (bf16[2,256,768]{2,1,0:T(8,128)(2,1)S(1)}, bf16[2,256,768]{2,1,0:T(8,128)(2,1)S(1)}, u32[]{:S(2)}, u32[]{:S(2)}) collective-permute-start(bf16[2,256,768]{2,1,0:T(8,128)(2,1)S(1)} %select_convert_fusion.1), channel_id=1, source_target_pairs={{0,32},{32,0},{2,34},{34,2},{4,36},{36,4},{6,38},{38,6},{8,40},{40... | collective-permute-start | bytes 2359304 | tf_op jit(solution)/shard_map/ppermute | solution.py:47
  1516.0 43.7 %collective-permute-start.44 = (bf16[2,2,768,256]{3,2,1,0:T(8,128)(2,1)S(1)}, bf16[2,2,768,256]{3,2,1,0:T(8,128)(2,1)S(1)}, u32[]{:S(2)}, u32[]{:S(2)}) collective-permute-start(bf16[2,2,768,256]{3,2,1,0:T(8,128)(2,1)S(1)} %select_convert_fusion), channel_id=1, source_target_pairs={{0,32},{32,0},{2,34},{34,2},{4,36},{36,4},{6,38},{38,6},{8,40},{40... | collective-permute-start | bytes 4718600 | tf_op jit(solution)/shard_map/ppermute | solution.py:47
  1531.7 30.2 %collective-permute-start.43 = (bf16[2,2,2,40,1536]{4,3,2,1,0:T(8,128)(2,1)S(1)}, bf16[2,2,2,40,1536]{4,3,2,1,0:T(8,128)(2,1)S(1)}, u32[]{:S(2)}, u32[]{:S(2)}) collective-permute-start(bf16[2,2,2,40,1536]{4,3,2,1,0:T(8,128)(2,1)S(1)} %fusion.250), channel_id=1, source_target_pairs={{0,8},{8,0},{2,10},{10,2},{4,12},{12,4},{6,14},{14,6},{16,24},{24,... | collective-permute-start | bytes 2949128 | tf_op jit(solution)/shard_map/ppermute | solution.py:47
  1537.2 222.9 %collective-permute-start.47 = (bf16[2,256,384]{2,1,0:T(8,128)(2,1)}, bf16[2,256,384]{2,1,0:T(8,128)(2,1)}, u32[]{:S(2)}, u32[]{:S(2)}) collective-permute-start(bf16[2,256,384]{2,1,0:T(8,128)(2,1)} %select_convert_fusion.3), channel_id=1, source_target_pairs={{0,16},{16,0},{2,18},{18,2},{4,20},{20,4},{6,22},{22,6},{8,24},{24... | collective-permute-start | bytes 1179656 | tf_op jit(solution)/shard_map/ppermute | solution.py:47
  1573.3 178.5 %all-reduce.29.cloned.1.call-start = ((), (), s32[]{:S(2)}) async-start(), calls=%async_computation.8 | async-start | bytes 4194304
  1576.2 186.4 %collective-permute-start.45 = (bf16[2,2,384,256]{3,2,1,0:T(8,128)(2,1)}, bf16[2,2,384,256]{3,2,1,0:T(8,128)(2,1)}, u32[]{:S(2)}, u32[]{:S(2)}) collective-permute-start(bf16[2,2,384,256]{3,2,1,0:T(8,128)(2,1)} %select_convert_fusion.2), channel_id=1, source_target_pairs={{0,16},{16,0},{2,18},{18,2},{4,20},{20,4},{6,22},{22,6},{8,24},{24... | collective-permute-start | bytes 2359304 | tf_op jit(solution)/shard_map/ppermute | solution.py:47
  1644.8 260.4 %all-reduce.31.cloned.1.call-start = ((), (), s32[]{:S(2)}) async-start(), calls=%async_computation.9 | async-start | bytes 12582912 | tf_op jit(solution)/shard_map/psum | solution.py:470
  (295 other events, 2054.9 us)
Sparse Core Ops, SparseCore 0:
  856.1 29.8 all-reduce.18
  922.8 106.7 all-reduce.24
  1217.5 34.0 all-reduce.20
  1288.3 106.7 all-reduce.26
  1573.4 32.6 all-reduce.22
  1644.9 106.7 all-reduce.28
  1760.3 115.8 all-reduce.30
where the time goes:
time: 1940 us; the launch traced here: 1920 us
  waiting for transfers between devices  898 us (46%)
  local copies, waits for them, and re-layouts  300 us (15%)
  other arithmetic  221 us (11%)
  blocking collectives  211 us (11%)
  matrix products  171 us (9%)
  starting transfers between devices  101 us (5%)
  between operations  19.5 us (1%)
    ppermute x44, waiting for transfers between devices, swapped(): return lax.ppermute(block, axis, route)  459 us
    unnamed x10, waiting for transfers between devices  288 us
    psum x1, blocking collectives, per_device(): lax.psum(gain_one_grad.astype(jnp.bfloat16), 'dp').astype(jnp.float32)  124 us
    psum x3, waiting for transfers between devices, per_device(): lax.psum(grad_part.astype(jnp.bfloat16), 'tensor').astype(jnp.float32)  92.1 us
    all_gather x9, blocking collectives, over_pieces(): tiles = lax.all_gather(shard, axis).astype(jnp.float32)  70.7 us
    ppermute x44, starting transfers between devices, swapped(): return lax.ppermute(block, axis, route)  63.5 us
    all_to_all x3, waiting for transfers between devices, sent_to_all(): return lax.all_to_all(copies, axis, split_axis=0, concat_axis=0, tiled=True)  50.3 us
    another operation x51, other arithmetic, group_all(): jnp.stack([jnp.where(upper_bit, arrived, kept_part), jnp.where(upper_bit,...  48.6 us
  transfers between devices with their start and end apart: 58, of which 45 were waited for; matrix products, arithmetic and copies ran while one was open for 15% of the time, Pallas kernels for 0%

commit v1 on v0

v1 whole, which is shorter than its diff:
```python
import jax
import jax.numpy as jnp
from jax import lax
from jax.sharding import PartitionSpec as P

D = 1536
HD = 64
EXPERTS = 16
NX, NY = 4, 4
EPSILON = 1e-06
SCALE = 0.125
NEGATIVE = -1e30
BF = jnp.bfloat16
F32 = jnp.float32


def moved(value, dx, dy, dc):
    route = []
    for x in range(NX):
        for y in range(NY):
            for c in range(2):
                target = (((x + dx) % NX) * NY + (y + dy) % NY) * 2 + (c ^ dc)
                route.append(((x * NY + y) * 2 + c, target))
    return lax.ppermute(value, "dp", route)


def swapped(value, axis):
    return lax.ppermute(value, axis, [(0, 1), (1, 0)])


def along_y(block):
    return jnp.concatenate([block] + [moved(block, 0, j, 0) for j in (1, 2, 3)], axis=0)


def along_x(block):
    return jnp.concatenate([block] + [moved(block, j, 0, 0) for j in (1, 2, 3)], axis=0)


def back_y(sums):
    parts = sums.reshape(4, -1, sums.shape[-1])
    total = parts[0].astype(F32)
    for j in (1, 2, 3):
        total = total + moved(parts[j], 0, -j, 0).astype(F32)
    return total


def back_x(sums):
    parts = sums.reshape(4, -1, sums.shape[-1])
    total = parts[0].astype(F32)
    for j in (1, 2, 3):
        total = total + moved(parts[j], -j, 0, 0).astype(F32)
    return total


def group_gather(block):
    column = along_y(block)
    return column, moved(column, 0, 0, 1)


def group_sum(own, other):
    both = own.astype(F32) + moved(other, 0, 0, 1).astype(F32)
    return back_y(both.astype(BF))


def tensor_sum(value):
    low = value.astype(BF)
    return low.astype(F32) + swapped(low, "tensor").astype(F32)


def norm_apply(value, gain):
    inverse = lax.rsqrt(jnp.mean(value * value, axis=-1, keepdims=True) + EPSILON)
    return value * inverse * gain


def norm_back(value, gain, grad):
    inverse = lax.rsqrt(jnp.mean(value * value, axis=-1, keepdims=True) + EPSILON)
    scaled = grad * gain
    inner = jnp.mean(scaled * value, axis=-1, keepdims=True)
    gain_grad = jnp.sum(grad * value * inverse, axis=0)
    return (inverse * scaled - inverse * inverse * inverse * value * inner, gain_grad)


def dot(left, right):
    return jnp.dot(left, right, preferred_element_type=F32)


def over_rows(left, right):
    return lax.dot_general(left, right, (((0,), (0,)), ((), ())), preferred_element_type=F32)


def against(left, right):
    return lax.dot_general(left, right, (((1,), (1,)), ((), ())), preferred_element_type=F32)


def scores_of(query, keys, allowed):
    grouped = query.reshape(query.shape[0], 4, 3, HD)
    key_heads = keys.reshape(keys.shape[0], 4, HD)
    scores = jnp.einsum("qkgd,tkd->kgqt", grouped, key_heads, preferred_element_type=F32) * SCALE
    return jnp.where(allowed[None, None], scores, NEGATIVE)


def attend_forward(query, pairs, allowed):
    scores = scores_of(query, pairs[:, :256], allowed)
    top = jnp.max(scores, axis=-1, keepdims=True)
    raised = jnp.exp(scores - top)
    total = jnp.sum(raised, axis=-1, keepdims=True)
    weights = (raised / total).astype(BF)
    value_heads = pairs[:, 256:].reshape(-1, 4, HD)
    mixed = jnp.einsum("kgqt,tkd->qkgd", weights, value_heads, preferred_element_type=F32)
    return mixed.reshape(query.shape).astype(BF), top + jnp.log(total)


def attend_backward(query, pairs, allowed, log_total, grad_mixed, mixed):
    count = query.shape[0]
    scores = scores_of(query, pairs[:, :256], allowed)
    weights = jnp.exp(scores - log_total)
    grouped = query.reshape(count, 4, 3, HD)
    grad_heads = grad_mixed.reshape(count, 4, 3, HD)
    key_heads = pairs[:, :256].reshape(-1, 4, HD)
    value_heads = pairs[:, 256:].reshape(-1, 4, HD)
    grad_values = jnp.einsum("kgqt,qkgd->tkd", weights.astype(BF), grad_heads, preferred_element_type=F32)
    grad_weights = jnp.einsum("qkgd,tkd->kgqt", grad_heads, value_heads, preferred_element_type=F32)
    inner = jnp.einsum("qkgd,qkgd->kgq", grad_heads.astype(F32), mixed.reshape(count, 4, 3, HD).astype(F32))
    grad_scores = (weights * (grad_weights - inner[..., None])).astype(BF)
    grad_query = jnp.einsum("kgqt,tkd->qkgd", grad_scores, key_heads, preferred_element_type=F32) * SCALE
    grad_keys = jnp.einsum("kgqt,qkgd->tkd", grad_scores, grouped, preferred_element_type=F32) * SCALE
    grad_pairs = jnp.concatenate([grad_keys.reshape(-1, 256), grad_values.reshape(-1, 256)], axis=1)
    return grad_query.reshape(query.shape).astype(BF), grad_pairs.astype(BF)


def gates_of(tokens, router, routed):
    logits = dot(tokens, router)
    top = jnp.max(jnp.where(routed > 0, logits, NEGATIVE), axis=1, keepdims=True)
    raised = jnp.where(routed > 0, jnp.exp(jnp.minimum(logits - top, 0.0)), 0.0)
    return raised / jnp.sum(raised, axis=1, keepdims=True)


def experts_forward(tokens, gates, weights):
    split = tokens.reshape(-1, 4, 384)
    gate_pre = jnp.einsum("trd,redf->etf", split, weights[:, 0:2], preferred_element_type=F32)
    up_pre = jnp.einsum("trd,redf->etf", split, weights[:, 2:4], preferred_element_type=F32)
    mid = (jax.nn.silu(gate_pre) * up_pre * gates.T[:, :, None]).astype(BF)
    produced = jnp.einsum("etf,redf->trd", mid, weights[:, 4:6], preferred_element_type=F32)
    return produced.reshape(-1, D), (gate_pre, up_pre, mid)


def experts_backward(tokens, gates, saved, grad_out, weights):
    gate_pre, up_pre, mid = saved
    split = tokens.reshape(-1, 4, 384)
    grad_split = grad_out.reshape(-1, 4, 384)
    raw = jnp.einsum("trd,redf->etf", grad_split, weights[:, 4:6], preferred_element_type=F32)
    sigmoid = jax.nn.sigmoid(gate_pre)
    activated = gate_pre * sigmoid
    grad_gates = jnp.sum(activated * up_pre * raw, axis=2).T
    scaled = raw * gates.T[:, :, None]
    grad_gate = (scaled * up_pre * sigmoid * (1.0 + gate_pre * (1.0 - sigmoid))).astype(BF)
    grad_up = (scaled * activated).astype(BF)
    down_grad = jnp.einsum("trd,etf->redf", grad_split, mid, preferred_element_type=F32).astype(BF)
    gate_grad = jnp.einsum("trd,etf->redf", split, grad_gate, preferred_element_type=F32).astype(BF)
    up_grad = jnp.einsum("trd,etf->redf", split, grad_up, preferred_element_type=F32).astype(BF)
    grad_tokens = jnp.einsum("etf,redf->trd", grad_gate, weights[:, 0:2], preferred_element_type=F32)
    grad_tokens = grad_tokens + jnp.einsum("etf,redf->trd", grad_up, weights[:, 2:4], preferred_element_type=F32)
    weight_grads = jnp.concatenate([gate_grad, up_grad, down_grad], axis=1)
    return grad_tokens.reshape(-1, D), grad_gates, weight_grads


X_GROUPS = [[(x * NY + y) * 2 + c for x in range(NX)] for y in range(NY) for c in range(2)]


Y_GROUPS = [[(x * NY + y) * 2 + c for y in range(NY) for c in range(2)] for x in range(NX)]


def replica_gather(shard):
    return lax.all_gather(shard, "dp", axis=0, axis_index_groups=X_GROUPS)


def replica_scatter(grads):
    flat = grads.reshape(-1, grads.shape[-1])
    return lax.psum_scatter(flat, "dp", scatter_dimension=0, axis_index_groups=X_GROUPS, tiled=True)


def after(value, *others):
    return lax.optimization_barrier((value, *others))[0]


def per_device(
    inputs,
    cotangent,
    segments,
    routes,
    norm_first,
    w_query,
    w_key,
    w_value,
    w_out,
    norm_second,
    w_router,
    w_gate,
    w_up,
    w_down,
):
    section = lax.axis_index("section")
    place = lax.axis_index("dp")
    here_x, here_y, here_c = place // (NY * 2), place // 2 % NY, place % 2
    first = section == 0
    rows = inputs.shape[1]

    def in_order(own, other):
        return jnp.where(first, own, other), jnp.where(first, other, own)

    def pick(pair):
        return lax.dynamic_index_in_dim(pair, section, 0, False)

    qkv_own = jnp.concatenate([w_query[0], w_key[0], w_value[0]], axis=1)
    act_both = norm_apply(inputs.astype(F32), norm_first[0]).astype(BF)
    qkv_both = dot(act_both.reshape(2 * rows, D), qkv_own).astype(BF)
    qkv_sent = lax.ppermute(qkv_both[rows:], "section", [(0, 1)])
    qkv_first = jnp.where(first, qkv_both[:rows], qkv_sent)

    pack = jnp.concatenate([norm_first, norm_second, w_router[0].T.astype(F32)], axis=0)
    packs = in_order(pack, swapped(pack, "section"))
    experts = jnp.concatenate([w_gate[0], w_up[0], jnp.swapaxes(w_down[0], 1, 2)], axis=0)
    experts = after(experts, qkv_sent)
    experts_both = in_order(experts, swapped(experts, "section"))
    expert_weights = [replica_gather(e) for e in experts_both]

    def whole(own, rows_half, *earlier):
        half = lax.dynamic_slice_in_dim(own, here_c * rows_half, rows_half, 0)
        half = swapped(after(half, *earlier), "section")
        rest = moved(half, 0, 0, 1)
        low = jnp.where(here_c == 0, half, rest)
        high = jnp.where(here_c == 0, rest, half)
        return jnp.concatenate([low, high], axis=0)

    outs_w = in_order(w_out[0], whole(w_out[0], 384, experts_both[0]))
    qkvs_w = None

    labels = pick(segments)
    query_places = place * rows + jnp.arange(rows, dtype=jnp.int32)
    query_labels = lax.dynamic_slice_in_dim(labels, place * rows, rows, 0)
    starts = jnp.sum((labels[None, :] < query_labels[:, None]).astype(jnp.int32), axis=1)
    shift = jnp.arange(4, dtype=jnp.int32)
    key_x = (here_x - shift + NX) % NX
    key_y = (here_y - shift + NY) % NY
    key_c = jnp.stack([here_c, 1 - here_c])
    blocks = (key_x[None, None, :] * NY + key_y[None, :, None]) * 2 + key_c[:, None, None]
    key_places = (blocks[..., None] * rows + jnp.arange(rows, dtype=jnp.int32)).reshape(-1)
    allowed = (key_places[None, :] <= query_places[:, None]) & (key_places[None, :] >= starts[:, None])

    own_routes = pick(routes)
    expert_ids = jnp.arange(EXPERTS, dtype=jnp.int32)
    routed_own = jnp.sum((own_routes[:, :, None] == expert_ids).astype(F32), axis=1)
    given = pick(cotangent)
    sent = jnp.concatenate([given, jnp.pad(routed_own.astype(BF), ((0, 0), (0, 128 - EXPERTS)))], axis=1)
    got = group_gather(sent)
    got = jnp.concatenate(got, axis=0)
    routed = got[:, D : D + EXPERTS].astype(F32)
    given_all = got[:, :D]
    local = lax.broadcasted_iota(jnp.int32, (EXPERTS, 2), 0) == (
        2 * (place % 8) + lax.broadcasted_iota(jnp.int32, (EXPERTS, 2), 1)
    )
    local = local.astype(F32)

    hidden = pick(inputs).astype(F32)
    saved = []
    for layer in range(2):
        gain_one, gain_two = packs[layer][0], packs[layer][1]
        router = packs[layer][2:].T.astype(BF)
        activation = norm_apply(hidden, gain_one).astype(BF)
        qkv = qkv_first if layer == 0 else dot(activation, qkvs_w[1]).astype(BF)
        query, pair = qkv[:, :768], qkv[:, 768:]
        column = along_y(along_x(pair))
        pairs = jnp.concatenate([column, moved(column, 0, 0, 1)], axis=0)
        mixed, log_total = attend_forward(query, pairs, allowed)
        middle = hidden + tensor_sum(dot(mixed, outs_w[layer]))
        second = norm_apply(middle, gain_two).astype(BF)
        tokens = jnp.concatenate(group_gather(second), axis=0)
        gates = jnp.dot(gates_of(tokens, router, routed), local, precision=lax.Precision.HIGHEST)
        if layer == 0:
            qkvs_w = in_order(qkv_own, whole(qkv_own, 768, middle))
        produced, kept = experts_forward(tokens, gates, expert_weights[layer])
        produced = produced.astype(BF)
        half = produced.shape[0] // 2
        branch = tensor_sum(group_sum(produced[:half], produced[half:]).reshape(rows, D))
        result = middle + branch
        lefts = []
        for factor, width in ((activation, 192), (mixed, 96)):
            cut = jnp.swapaxes(factor.reshape(rows, 8, width), 0, 1)
            lefts.append(lax.all_gather(cut, "dp", axis=0, axis_index_groups=Y_GROUPS))
        saved.append((lefts, hidden, activation, query, pairs, mixed, log_total, middle, second, tokens, gates, kept, branch, result))
        hidden = result

    me = place % 8
    group_order = (key_y[None, :] * 2 + key_c[:, None]).reshape(-1)

    def left_of(gathered):
        mine = lax.dynamic_index_in_dim(gathered, me, 1, False)
        return jnp.take(mine, group_order, axis=0).reshape(8 * rows, -1)

    grad_output = given.astype(F32)
    grads = []
    for layer in (1, 0):
        lefts, hidden, activation, query, pairs, mixed, log_total, middle, second, tokens, gates, kept, branch, _ = saved[layer]
        gain_one, gain_two = packs[layer][0], packs[layer][1]
        router = packs[layer][2:].T.astype(BF)
        if layer == 1:
            grad_all = given_all
        else:
            grad_all = jnp.concatenate(group_gather(grad_output.astype(BF)), axis=0)
        grad_tokens, grad_gates, weight_grads = experts_backward(tokens, gates, kept, grad_all, expert_weights[layer])
        expert_part = replica_scatter(weight_grads)
        gated = gates * grad_gates
        router_local = jnp.dot(router.astype(F32), local, precision=lax.Precision.HIGHEST)
        grad_tokens = (grad_tokens + against(gated, router_local)).astype(BF)
        half = grad_tokens.shape[0] // 2
        grad_second = tensor_sum(group_sum(grad_tokens[:half], grad_tokens[half:]).reshape(rows, D))
        inner = jnp.sum(grad_output * branch, axis=1, keepdims=True)
        own_gates = gates_of(second, router, routed_own)
        grad_second = grad_second - against(inner * own_gates, router.astype(F32))
        grad_from_norm, gain_two_grad = norm_back(middle, gain_two, grad_second)
        grad_middle = grad_output + grad_from_norm
        grad_branch = grad_middle.astype(BF)
        inner_high = inner.astype(BF)
        inner_low = (inner - inner_high.astype(F32)).astype(BF)
        lanes = jnp.concatenate([inner_high, inner_low, jnp.zeros((rows, 126), BF)], axis=1)
        right = jnp.concatenate(group_gather(jnp.concatenate([grad_branch, lanes], axis=1)), axis=0)
        inner_all = right[:, D : D + 1].astype(F32) + right[:, D + 1 : D + 2].astype(F32)
        out_grad = over_rows(left_of(lefts[1]), right[:, :D])
        logit_grads = gated - 0.5 * gates * inner_all
        router_grad = over_rows(logit_grads, tokens.astype(F32))
        out_grad = jnp.concatenate([out_grad, router_grad, gain_two_grad[None], jnp.zeros((13, D), F32)], axis=0)
        out_blocks = jnp.swapaxes(out_grad.astype(BF).reshape(112, 4, 384), 0, 1)
        out_part = back_x(jnp.take(out_blocks, key_x, axis=0)).reshape(112, 384)
        grad_mixed = against(grad_branch, outs_w[layer]).astype(BF)
        grad_query, grad_pairs = attend_backward(query, pairs, allowed, log_total, grad_mixed, mixed)
        both = grad_pairs[:1024].astype(F32) + moved(grad_pairs[1024:], 0, 0, 1).astype(F32)
        grad_pair = back_x(back_y(both.astype(BF)).astype(BF)).reshape(rows, 512).astype(BF)
        grad_qkv = jnp.concatenate([grad_query, grad_pair], axis=1)
        right = jnp.concatenate(group_gather(grad_qkv), axis=0)
        qkv_grad = over_rows(left_of(lefts[0]), right).astype(BF)
        qkv_part = back_x(jnp.take(qkv_grad.reshape(4, 48, 1280), key_x, axis=0)).reshape(48, 1280)
        grad_activation = tensor_sum(against(grad_qkv, qkvs_w[layer]))
        grad_from_first, gain_one_grad = norm_back(hidden, gain_one, grad_activation)
        grad_output = grad_middle + grad_from_first
        grads.append((grad_output, qkv_part, out_part, gain_one_grad, expert_part))
    grads = grads[::-1]

    def own_of(a, b):
        return jnp.where(first, a, b)

    def from_other(for_first, for_second):
        return swapped(own_of(for_second, for_first).astype(BF), "section").astype(F32)

    def over_sections(a, b):
        return own_of(a, b).astype(F32) + from_other(a, b)

    def by_batch(own, other):
        return jnp.stack([jnp.where(first, own, other), jnp.where(first, other, own)])[None]

    results = by_batch(own_of(saved[0][-1], saved[1][-1]), from_other(saved[0][-1], saved[1][-1]))
    input_grads = by_batch(own_of(grads[0][0], grads[1][0]), from_other(grads[0][0], grads[1][0]))
    qkv_sum = over_sections(grads[0][1], grads[1][1]).astype(BF)
    out_sum = over_sections(grads[0][2], grads[1][2]).astype(BF)
    gain_one_sum = over_sections(grads[0][3], grads[1][3]).astype(BF)
    qkv_all = lax.all_gather(qkv_sum, "dp", axis=0).reshape(4, 8, 48, 1280)
    out_all = lax.all_gather(out_sum, "dp", axis=0).reshape(4, 8, 112, 384)
    gain_one_all = lax.all_gather(gain_one_sum, "dp", axis=0)
    qkv_all = jnp.swapaxes(qkv_all, 0, 1).reshape(D, 1280).astype(F32)
    out_rows = out_all[:, :, :96]
    out_full = jnp.transpose(out_rows, (1, 2, 0, 3)).reshape(768, D).astype(F32)
    router_sum = jnp.transpose(out_all[:, :, 96:98], (1, 2, 0, 3)).reshape(EXPERTS, D)
    router_sum = tensor_sum(router_sum)
    gain_two_sum = jnp.sum(out_all[:, :, 98].astype(F32), axis=1).reshape(1, D)
    gain_one_sum = jnp.sum(gain_one_all.astype(F32), axis=0)[None]
    expert_sum = over_sections(grads[0][4], grads[1][4]).reshape(3, 2, 384, 256)
    return (
        results,
        input_grads,
        gain_one_sum,
        qkv_all[None, :, :768],
        qkv_all[None, :, 768:1024],
        qkv_all[None, :, 1024:],
        out_full[None],
        gain_two_sum,
        router_sum.T[None],
        expert_sum[0][None],
        expert_sum[1][None],
        jnp.swapaxes(expert_sum[2], 1, 2)[None],
    )


def solution(mesh):
    in_specs = (
        P(None, "dp", None),
        P(None, "dp", None),
        P(),
        P(None, "dp", None),
        P("section", None),
        P("section", None, "tensor"),
        P("section", None, "tensor"),
        P("section", None, "tensor"),
        P("section", "tensor", None),
        P("section", None),
        P("section", None, None),
        P("section", "dp", None, "tensor"),
        P("section", "dp", None, "tensor"),
        P("section", "dp", "tensor", None),
    )
    out_specs = (
        P("section", None, "dp", None),
        P("section", None, "dp", None),
        P("section", None),
        P("section", None, "tensor"),
        P("section", None, "tensor"),
        P("section", None, "tensor"),
        P("section", "tensor", None),
        P("section", None),
        P("section", None, None),
        P("section", "dp", None, "tensor"),
        P("section", "dp", None, "tensor"),
        P("section", "dp", "tensor", None),
    )
    return jax.shard_map(
        per_device, mesh=mesh, in_specs=in_specs, out_specs=out_specs, check_vma=False
    )
```

time: 1940 us -> 810 us (0.42)
  waiting for transfers between devices: 898 us -> 211 us
  blocking collectives: 211 us -> 58.2 us
  local copies, waits for them, and re-layouts: 300 us -> 156 us
  other arithmetic: 221 us -> 84.4 us
  starting transfers between devices: 101 us -> 172 us
  matrix products: 171 us -> 101 us
    unnamed x10 -> x8, waiting for transfers between devices: 288 us -> 0.13 us
    ppermute x48 -> x110, waiting for transfers between devices: 468 us -> 210 us  [the longest x90 105 us: moved(): return lax.ppermute(value, 'dp', route)]
    psum x4 -> x0, blocking collectives: 140 us -> none  [the longest x1 124 us: per_device(): lax.psum(gain_one_grad.astype(jnp.bfloat16), 'dp').astype(jnp.float32)]
    ppermute x48 -> x110, starting transfers between devices: 73.4 us -> 171 us  [the longest x90 138 us: moved(): return lax.ppermute(value, 'dp', route)]
    psum x4 -> x0, waiting for transfers between devices: 92.1 us -> none  [the longest x3 92.1 us: per_device(): lax.psum(grad_part.astype(jnp.bfloat16), 'tensor').astype(jnp.float32)]
    another operation x69 -> x3, other arithmetic: 76.9 us -> 0.32 us  [the longest x2 0.24 us: by_batch(): jnp.stack([jnp.where(first, own, other), jnp.where(first, other, own)])]
    gather x18 -> x8, local copies, waits for them, and re-layouts: 74.9 us -> 6.56 us  [the longest x4 3.54 us: left_of(): return jnp.take(mine, group_order, axis=0).reshape(8 * rows, -1)]
    another operation x40 -> x1, local copies, waits for them, and re-layouts: 68.3 us -> 0.01 us  [the longest x6 35.7 us: attend_backward(): jnp.stack([grad_keys.reshape(pairs.shape[1], -1), grad_values.reshape(pai...]
  transfers between devices with their start and end apart: 58 -> 118, of which waited for: 45 -> 52; matrix products, arithmetic and copies ran while one was open for 15% -> 39% of each run, Pallas kernels for 0% -> 0%
where the time goes in v1:
time: 810 us; the launch traced here: 801 us
  waiting for transfers between devices  211 us (26%)
  starting transfers between devices  172 us (21%)
  local copies, waits for them, and re-layouts  156 us (19%)
  matrix products  101 us (12%)
  other arithmetic  84.4 us (10%)
  blocking collectives  58.2 us (7%)
  between operations  17.8 us (2%)
    ppermute x90, starting transfers between devices, moved(): return lax.ppermute(value, 'dp', route)  138 us
    ppermute x90, waiting for transfers between devices, moved(): return lax.ppermute(value, 'dp', route)  105 us
    ppermute x19, waiting for transfers between devices, swapped(): return lax.ppermute(value, axis, [(0, 1), (1, 0)])  103 us
    unnamed x460, local copies, waits for them, and re-layouts  43.5 us
    all_gather x1, blocking collectives, per_device(): gain_one_all = lax.all_gather(gain_one_sum, 'dp', axis=0)  29.5 us
    all_gather x2, blocking collectives, per_device(): lefts.append(lax.all_gather(cut, 'dp', axis=0, axis_index_groups=Y_GROUPS))  28.7 us
    ppermute x19, starting transfers between devices, swapped(): return lax.ppermute(value, axis, [(0, 1), (1, 0)])  28.6 us
    dot_general x8, matrix products, against(): lax.dot_general(left, right, (((1,), (1,)), ((), ())), preferred_element_...  19.8 us
  transfers between devices with their start and end apart: 118, of which 52 were waited for; matrix products, arithmetic and copies ran while one was open for 39% of the time, Pallas kernels for 0%

profile of v1, /device:TPU:1, one launch (start us, length us, event | category | flops | bytes accessed | tf_op | source)
XLA Modules:
  0.0 800.6 jit_solution(2137372104919360900)
XLA Ops:
  15.3 4.4 collective-permute-start
  29.8 20.0 %collective-permute-done.8 = bf16[6,384,256]{2,1,0:T(8,128)(2,1)} collective-permute-done((bf16[6,384,256]{2,1,0:T(8,128)(2,1)S(1)}, bf16[6,384,256]{2,1,0:T(8,128)(2,1)}, u32[]{:S(2)}, u32[]{:S(2)}) %collective-permute-start.8) | collective-permute-done | bytes 1179680 | tf_op jit(solution)/shard_map/ppermute | solution.py:28
  86.9 5.3 collective-permute-start.7
  105.7 19.6 %collective-permute-done.9 = bf16[384,1536]{1,0:T(8,128)(2,1)} collective-permute-done((bf16[384,1536]{1,0:T(8,128)(2,1)}, bf16[384,1536]{1,0:T(8,128)(2,1)}, u32[]{:S(2)}, u32[]{:S(2)}) %collective-permute-start.9) | collective-permute-done | bytes 1179680 | tf_op jit(solution)/shard_map/ppermute | solution.py:28
  135.4 5.2 collective-permute-done.11
  144.5 8.6 %collective-permute-done.13 = bf16[64,1536]{1,0:T(8,128)(2,1)S(1)} collective-permute-done((bf16[64,1536]{1,0:T(8,128)(2,1)S(1)}, bf16[64,1536]{1,0:T(8,128)(2,1)S(1)}, u32[]{:S(2)}, u32[]{:S(2)}) %collective-permute-start.13) | collective-permute-done | bytes 196640 | tf_op jit(solution)/shard_map/ppermute | solution.py:24
  168.5 32.9 %collective-permute-done.26 = bf16[768,1280]{1,0:T(8,128)(2,1)} collective-permute-done((bf16[768,1280]{1,0:T(8,128)(2,1)}, bf16[768,1280]{1,0:T(8,128)(2,1)}, u32[]{:S(2)}, u32[]{:S(2)}) %collective-permute-start.26) | collective-permute-done | bytes 1966112 | tf_op jit(solution)/shard_map/ppermute | solution.py:28
  212.2 4.8 collective-permute-done.23
  242.7 6.0 collective-permute-done.32
  256.9 14.2 %all-gather.6 = bf16[64,64,96]{2,1,0:T(8,128)(2,1)S(1)} all-gather(bf16[8,64,96]{2,1,0:T(8,128)(2,1)S(1)} %bitcast.717), channel_id=8, replica_groups={{0,2,4,6,8,10,12,14},{16,18,20,22,24,26,28,30},{32,34,36,38,40,42,44,46..., dimensions={0}, use_global_device_ids=true | all-gather | bytes 884736 | tf_op jit(solution)/shard_map/all_gather | solution.py:289
  294.5 14.5 %all-gather.7 = bf16[64,64,96]{2,1,0:T(8,128)(2,1)S(1)} all-gather(bf16[8,64,96]{2,1,0:T(8,128)(2,1)S(1)} %bitcast.718), channel_id=9, replica_groups={{0,2,4,6,8,10,12,14},{16,18,20,22,24,26,28,30},{32,34,36,38,40,42,44,46..., dimensions={0}, use_global_device_ids=true | all-gather | bytes 884736 | tf_op jit(solution)/shard_map/all_gather | solution.py:289
  317.4 4.6 collective-permute-done.36
  349.4 4.1 bitcast_add_fusion.1
  383.3 4.0 collective-permute-done.42
  390.5 5.2 collective-permute-done.48
  399.5 6.6 copy.465
  420.7 4.2 fusion.34
  448.7 8.6 %collective-permute-done.54 = bf16[256,512]{0,1:T(8,128)(2,1)S(1)} collective-permute-done((bf16[256,512]{0,1:T(8,128)(2,1)S(1)}, bf16[256,512]{0,1:T(8,128)(2,1)S(1)}, u32[]{:S(2)}, u32[]{:S(2)}) %collective-permute-start.54) | collective-permute-done | bytes 262176 | tf_op jit(solution)/shard_map/ppermute | solution.py:24
  490.2 4.1 collective-permute-start.62
  521.3 6.7 copy.461
  534.0 4.6 collective-permute-done.66
  538.6 4.5 collective-permute-done.65
  558.6 4.0 fusion.96
  571.2 4.7 fusion.1
  636.5 6.3 collective-permute-start.87
  651.8 12.9 %collective-permute-start.88 = (bf16[256,1280]{0,1:T(8,128)(2,1)}, bf16[256,1280]{0,1:T(8,128)(2,1)S(1)}, u32[]{:S(2)}, u32[]{:S(2)}) collective-permute-start(bf16[256,1280]{0,1:T(8,128)(2,1)} %pad_maximum_fusion.21), channel_id=1, source_target_pairs={{0,2},{2,0},{4,6},{6,4},{8,10},{10,8},{12,14},{14,12},{16,18},{18,... | collective-permute-start | bytes 1966088 | tf_op jit(solution)/shard_map/ppermute | solution.py:24
  694.6 5.0 collective-permute-done.91
  704.4 4.2 fusion.55
  717.8 29.5 %all-gather.9 = bf16[32,1,1536]{2,1,0:T(2,128)(2,1)S(1)} all-gather(bf16[1,1,1536]{2,1,0:T(2,128)(2,1)S(1)} %reshape.796), channel_id=4, replica_groups=mesh['section'=2,'dp'=32,'tensor'=2] {'dp'}, dimensions={0}, use_global_device_ids=true | all-gather | bytes 101376 | tf_op jit(solution)/shard_map/all_gather | solution.py:367
  758.9 5.2 copy.456
  764.1 6.5 reshape.708
  771.2 10.3 %collective-permute-done.108 = bf16[16,1536]{1,0:T(8,128)(2,1)} collective-permute-done((bf16[16,1536]{1,0:T(8,128)(2,1)}, bf16[16,1536]{1,0:T(8,128)(2,1)}, u32[]{:S(2)}, u32[]{:S(2)}) %collective-permute-start.108) | collective-permute-done | bytes 49184 | tf_op jit(solution)/shard_map/ppermute | solution.py:28
  (969 shorter events, 501.5 us)
Async XLA Ops:
  7.2 152.3 %all-gather.17.cloned.1.call-start = ((), (), s32[]{:S(2)}) async-start(), calls=%async_computation.4 | async-start | bytes 5898240 | tf_op jit(solution)/shard_map/all_gather | solution.py:174
  22.8 26.9 %collective-permute-start.8 = (bf16[6,384,256]{2,1,0:T(8,128)(2,1)S(1)}, bf16[6,384,256]{2,1,0:T(8,128)(2,1)}, u32[]{:S(2)}, u32[]{:S(2)}) collective-permute-start(bf16[6,384,256]{2,1,0:T(8,128)(2,1)S(1)} %pad_maximum_fusion.11), channel_id=1, source_target_pairs={{0,64},{64,0},{1,65},{65,1},{2,66},{66,2},{3,67},{67,3},{4,68},{68... | collective-permute-start | bytes 3538952 | tf_op jit(solution)/shard_map/ppermute | solution.py:28
  25.8 68.0 %collective-permute-start.17 = (bf16[64,1664]{1,0:T(8,128)(2,1)S(1)}, bf16[64,1664]{1,0:T(8,128)(2,1)S(1)}, u32[]{:S(2)}, u32[]{:S(2)}) collective-permute-start(bf16[64,1664]{1,0:T(8,128)(2,1)S(1)} %get-tuple-element.202), channel_id=1, source_target_pairs={{0,4},{2,6},{4,8},{6,10},{8,12},{10,14},{12,0},{14,2},{16,20},{18,... | collective-permute-start | bytes 638984 | tf_op jit(solution)/shard_map/ppermute | solution.py:24
  27.1 66.7 %collective-permute-start.18 = (bf16[64,1664]{1,0:T(8,128)(2,1)S(1)}, bf16[64,1664]{1,0:T(8,128)(2,1)S(1)}, u32[]{:S(2)}, u32[]{:S(2)}) collective-permute-start(bf16[64,1664]{1,0:T(8,128)(2,1)S(1)} %get-tuple-element.202), channel_id=1, source_target_pairs={{0,8},{2,10},{4,12},{6,14},{8,0},{10,2},{12,4},{14,6},{16,24},{18,... | collective-permute-start | bytes 638984 | tf_op jit(solution)/shard_map/ppermute | solution.py:24
  52.6 278.4 %all-gather.19.cloned.1.call-start = ((), (), s32[]{:S(2)}) async-start(), calls=%async_computation.5 | async-start | bytes 5898240 | tf_op jit(solution)/shard_map/all_gather | solution.py:174
  94.9 60.4 %collective-permute-start.20 = (bf16[256,1664]{1,0:T(8,128)(2,1)}, bf16[256,1664]{1,0:T(8,128)(2,1)}, u32[]{:S(2)}, u32[]{:S(2)}) collective-permute-start(bf16[256,1664]{1,0:T(8,128)(2,1)} %pad_maximum_fusion.14), channel_id=1, source_target_pairs={{0,2},{2,0},{4,6},{6,4},{8,10},{10,8},{12,14},{14,12},{16,18},{18,... | collective-permute-start | bytes 2555912 | tf_op jit(solution)/shard_map/ppermute | solution.py:24
  97.3 27.9 %collective-permute-start.9 = (bf16[384,1536]{1,0:T(8,128)(2,1)}, bf16[384,1536]{1,0:T(8,128)(2,1)}, u32[]{:S(2)}, u32[]{:S(2)}) collective-permute-start(bf16[384,1536]{1,0:T(8,128)(2,1)} %dynamic-slice_bitcast_fusion), channel_id=1, source_target_pairs={{0,64},{64,0},{1,65},{65,1},{2,66},{66,2},{3,67},{67,3},{4,68},{68... | collective-permute-start | bytes 3538952 | tf_op jit(solution)/shard_map/ppermute | solution.py:28
  98.8 573.6 %all-gather.21.cloned.1.call-start = ((), (), s32[]{:S(2)}) async-start(), calls=%async_computation.6 | async-start | bytes 2359296 | tf_op jit(solution)/shard_map/all_gather | solution.py:289
  156.6 44.8 %collective-permute-start.26 = (bf16[768,1280]{1,0:T(8,128)(2,1)}, bf16[768,1280]{1,0:T(8,128)(2,1)}, u32[]{:S(2)}, u32[]{:S(2)}) collective-permute-start(bf16[768,1280]{1,0:T(8,128)(2,1)} %constant_dynamic-slice_fusion), channel_id=1, source_target_pairs={{0,64},{64,0},{1,65},{65,1},{2,66},{66,2},{3,67},{67,3},{4,68},{68... | collective-permute-start | bytes 5898248 | tf_op jit(solution)/shard_map/ppermute | solution.py:28
  165.8 37.2 %collective-permute-start.21 = (bf16[256,1536]{1,0:T(8,128)(2,1)}, bf16[256,1536]{1,0:T(8,128)(2,1)}, u32[]{:S(2)}, u32[]{:S(2)}) collective-permute-start(bf16[256,1536]{1,0:T(8,128)(2,1)} %copy.523), channel_id=1, source_target_pairs={{0,2},{2,0},{4,6},{6,4},{8,10},{10,8},{12,14},{14,12},{16,18},{18,... | collective-permute-start | bytes 2359304 | tf_op jit(solution)/shard_map/ppermute | solution.py:24
  208.8 465.3 %all-gather.23.cloned.1.call-start = ((), (), s32[]{:S(2)}) async-start(), calls=%async_computation.7 | async-start | bytes 2359296 | tf_op jit(solution)/shard_map/all_gather | solution.py:289
  250.3 27.1 %collective-permute-start.34 = (bf16[1024,512]{1,0:T(8,128)(2,1)}, bf16[1024,512]{1,0:T(8,128)(2,1)S(1)}, u32[]{:S(2)}, u32[]{:S(2)}) collective-permute-start(bf16[1024,512]{1,0:T(8,128)(2,1)} %get-tuple-element.188), channel_id=1, source_target_pairs={{0,2},{2,0},{4,6},{6,4},{8,10},{10,8},{12,14},{14,12},{16,18},{18,... | collective-permute-start | bytes 3145736 | tf_op jit(solution)/shard_map/ppermute | solution.py:24
  277.4 472.0 %reduce-scatter.5.cloned.1.call-start = ((), (), s32[]{:S(2)}) async-start(), calls=%async_computation.3 | async-start | bytes 5898240 | tf_op jit(solution)/shard_map/reduce_scatter | solution.py:179
  346.9 25.7 %collective-permute-start.40 = (bf16[256,1536]{1,0:T(8,128)(2,1)}, bf16[256,1536]{1,0:T(8,128)(2,1)}, u32[]{:S(2)}, u32[]{:S(2)}) collective-permute-start(bf16[256,1536]{1,0:T(8,128)(2,1)} %copy.526), channel_id=1, source_target_pairs={{0,2},{2,0},{4,6},{6,4},{8,10},{10,8},{12,14},{14,12},{16,18},{18,... | collective-permute-start | bytes 2359304 | tf_op jit(solution)/shard_map/ppermute | solution.py:24
  406.2 343.1 %reduce-scatter.3.cloned.1.call-start = ((), (), s32[]{:S(2)}) async-start(), calls=%async_computation.2 | async-start | bytes 5898240 | tf_op jit(solution)/shard_map/reduce_scatter | solution.py:179
  415.5 21.7 %collective-permute-start.100 = (bf16[64,1664]{1,0:T(8,128)(2,1)}, bf16[64,1664]{1,0:T(8,128)(2,1)}, u32[]{:S(2)}, u32[]{:S(2)}) collective-permute-start(bf16[64,1664]{1,0:T(8,128)(2,1)} %concatenate.188), channel_id=1, source_target_pairs={{0,4},{2,6},{4,8},{6,10},{8,12},{10,14},{12,0},{14,2},{16,20},{18,... | collective-permute-start | bytes 638984 | tf_op jit(solution)/shard_map/ppermute | solution.py:24
  431.8 42.6 %collective-permute-start.45 = (bf16[64,1536]{1,0:T(8,128)(2,1)}, bf16[64,1536]{1,0:T(8,128)(2,1)}, u32[]{:S(2)}, u32[]{:S(2)}) collective-permute-start(bf16[64,1536]{1,0:T(8,128)(2,1)} %select_convert_fusion.1), channel_id=1, source_target_pairs={{0,64},{64,0},{1,65},{65,1},{2,66},{66,2},{3,67},{67,3},{4,68},{68... | collective-permute-start | bytes 589832 | tf_op jit(solution)/shard_map/ppermute | solution.py:28
  438.6 22.5 %collective-permute-start.103 = (bf16[256,1664]{1,0:T(8,128)(2,1)S(1)}, bf16[256,1664]{1,0:T(8,128)(2,1)S(1)}, u32[]{:S(2)}, u32[]{:S(2)}) collective-permute-start(bf16[256,1664]{1,0:T(8,128)(2,1)S(1)} %pad_maximum_fusion.16), channel_id=1, source_target_pairs={{0,2},{2,0},{4,6},{6,4},{8,10},{10,8},{12,14},{14,12},{16,18},{18,... | collective-permute-start | bytes 2555912 | tf_op jit(solution)/shard_map/ppermute | solution.py:24
  528.1 223.7 %all-gather.27.cloned.1.call-start = ((), (), s32[]{:S(2)}) async-start(), calls=%async_computation.9 | async-start | bytes 2838528 | tf_op jit(solution)/shard_map/all_gather | solution.py:366
  553.6 29.7 %collective-permute-start.93 = (bf16[64,1664]{1,0:T(8,128)(2,1)}, bf16[64,1664]{1,0:T(8,128)(2,1)}, u32[]{:S(2)}, u32[]{:S(2)}) collective-permute-start(bf16[64,1664]{1,0:T(8,128)(2,1)} %concatenate.181), channel_id=1, source_target_pairs={{0,4},{2,6},{4,8},{6,10},{8,12},{10,14},{12,0},{14,2},{16,20},{18,... | collective-permute-start | bytes 638984 | tf_op jit(solution)/shard_map/ppermute | solution.py:24
  555.1 28.1 %collective-permute-start.94 = (bf16[64,1664]{1,0:T(8,128)(2,1)}, bf16[64,1664]{1,0:T(8,128)(2,1)}, u32[]{:S(2)}, u32[]{:S(2)}) collective-permute-start(bf16[64,1664]{1,0:T(8,128)(2,1)} %concatenate.181), channel_id=1, source_target_pairs={{0,8},{2,10},{4,12},{6,14},{8,0},{10,2},{12,4},{14,6},{16,24},{18,... | collective-permute-start | bytes 638984 | tf_op jit(solution)/shard_map/ppermute | solution.py:24
  558.4 24.8 %collective-permute-start.95 = (bf16[64,1664]{1,0:T(8,128)(2,1)}, bf16[64,1664]{1,0:T(8,128)(2,1)}, u32[]{:S(2)}, u32[]{:S(2)}) collective-permute-start(bf16[64,1664]{1,0:T(8,128)(2,1)} %concatenate.181), channel_id=1, source_target_pairs={{0,12},{2,14},{4,0},{6,2},{8,4},{10,6},{12,8},{14,10},{16,28},{18,... | collective-permute-start | bytes 638984 | tf_op jit(solution)/shard_map/ppermute | solution.py:24
  618.2 26.2 %collective-permute-start.85 = (bf16[64,1280]{0,1:T(8,128)(2,1)}, bf16[64,1280]{0,1:T(8,128)(2,1)}, u32[]{:S(2)}, u32[]{:S(2)}) collective-permute-start(bf16[64,1280]{0,1:T(8,128)(2,1)} %pad_maximum_fusion.22), channel_id=1, source_target_pairs={{0,4},{2,6},{4,8},{6,10},{8,12},{10,14},{12,0},{14,2},{16,20},{18,... | collective-permute-start | bytes 491528 | tf_op jit(solution)/shard_map/ppermute | solution.py:24
  620.1 26.2 %collective-permute-start.86 = (bf16[64,1280]{0,1:T(8,128)(2,1)}, bf16[64,1280]{0,1:T(8,128)(2,1)}, u32[]{:S(2)}, u32[]{:S(2)}) collective-permute-start(bf16[64,1280]{0,1:T(8,128)(2,1)} %pad_maximum_fusion.22), channel_id=1, source_target_pairs={{0,8},{2,10},{4,12},{6,14},{8,0},{10,2},{12,4},{14,6},{16,24},{18,... | collective-permute-start | bytes 491528 | tf_op jit(solution)/shard_map/ppermute | solution.py:24
  621.7 164.1 %all-gather.25.cloned.1.call-start = ((), (), s32[]{:S(2)}) async-start(), calls=%async_computation.8 | async-start | bytes 4055040 | tf_op jit(solution)/shard_map/all_gather | solution.py:365
  643.0 21.7 %collective-permute-start.78 = (bf16[64,1280]{0,1:T(8,128)(2,1)S(1)}, bf16[64,1280]{0,1:T(8,128)(2,1)S(1)}, u32[]{:S(2)}, u32[]{:S(2)}) collective-permute-start(bf16[64,1280]{0,1:T(8,128)(2,1)S(1)} %pad_maximum_fusion.23), channel_id=1, source_target_pairs={{0,4},{2,6},{4,8},{6,10},{8,12},{10,14},{12,0},{14,2},{16,20},{18,... | collective-permute-start | bytes 491528 | tf_op jit(solution)/shard_map/ppermute | solution.py:24
  643.1 21.6 %collective-permute-start.79 = (bf16[64,1280]{0,1:T(8,128)(2,1)S(1)}, bf16[64,1280]{0,1:T(8,128)(2,1)S(1)}, u32[]{:S(2)}, u32[]{:S(2)}) collective-permute-start(bf16[64,1280]{0,1:T(8,128)(2,1)S(1)} %pad_maximum_fusion.23), channel_id=1, source_target_pairs={{0,8},{2,10},{4,12},{6,14},{8,0},{10,2},{12,4},{14,6},{16,24},{18,... | collective-permute-start | bytes 491528 | tf_op jit(solution)/shard_map/ppermute | solution.py:24
  644.3 24.1 %collective-permute-start.80 = (bf16[64,1280]{0,1:T(8,128)(2,1)S(1)}, bf16[64,1280]{0,1:T(8,128)(2,1)S(1)}, u32[]{:S(2)}, u32[]{:S(2)}) collective-permute-start(bf16[64,1280]{0,1:T(8,128)(2,1)S(1)} %pad_maximum_fusion.23), channel_id=1, source_target_pairs={{0,12},{2,14},{4,0},{6,2},{8,4},{10,6},{12,8},{14,10},{16,28},{18,... | collective-permute-start | bytes 491528 | tf_op jit(solution)/shard_map/ppermute | solution.py:24
  651.8 24.9 %collective-permute-start.88 = (bf16[256,1280]{0,1:T(8,128)(2,1)}, bf16[256,1280]{0,1:T(8,128)(2,1)S(1)}, u32[]{:S(2)}, u32[]{:S(2)}) collective-permute-start(bf16[256,1280]{0,1:T(8,128)(2,1)} %pad_maximum_fusion.21), channel_id=1, source_target_pairs={{0,2},{2,0},{4,6},{6,4},{8,10},{10,8},{12,14},{14,12},{16,18},{18,... | collective-permute-start | bytes 1966088 | tf_op jit(solution)/shard_map/ppermute | solution.py:24
  715.3 32.9 %collective-permute-start.76 = (bf16[64,1536]{1,0:T(8,128)(2,1)S(1)}, bf16[64,1536]{1,0:T(8,128)(2,1)S(1)}, u32[]{:S(2)}, u32[]{:S(2)}) collective-permute-start(bf16[64,1536]{1,0:T(8,128)(2,1)S(1)} %select_convert_fusion), channel_id=1, source_target_pairs={{0,64},{64,0},{1,65},{65,1},{2,66},{66,2},{3,67},{67,3},{4,68},{68... | collective-permute-start | bytes 589832 | tf_op jit(solution)/shard_map/ppermute | solution.py:28
  751.8 31.2 %collective-permute-start.109 = (bf16[2304,256]{1,0:T(8,128)(2,1)}, bf16[2304,256]{1,0:T(8,128)(2,1)S(1)}, u32[]{:S(2)}, u32[]{:S(2)}) collective-permute-start(bf16[2304,256]{1,0:T(8,128)(2,1)} %broadcast_select_fusion.3), channel_id=1, source_target_pairs={{0,64},{64,0},{1,65},{65,1},{2,66},{66,2},{3,67},{67,3},{4,68},{68... | collective-permute-start | bytes 3538952 | tf_op jit(solution)/shard_map/ppermute | solution.py:28
  753.4 28.1 %collective-permute-start.108 = (bf16[16,1536]{1,0:T(8,128)(2,1)}, bf16[16,1536]{1,0:T(8,128)(2,1)}, u32[]{:S(2)}, u32[]{:S(2)}) collective-permute-start(bf16[16,1536]{1,0:T(8,128)(2,1)} %bitcast.295), channel_id=1, source_target_pairs={{0,1},{1,0},{2,3},{3,2},{4,5},{5,4},{6,7},{7,6},{8,9},{9,8},{10,11... | collective-permute-start | bytes 147464 | tf_op jit(solution)/shard_map/ppermute | solution.py:28
  (296 other events, 2751.4 us)
Sparse Core Ops, SparseCore 0:
  52.7 57.6 all-gather.16
  112.1 53.1 all-gather.18
  209.0 25.5 all-gather.20
  277.5 22.9 all-gather.22
  406.3 50.1 reduce-scatter.4
  528.1 51.9 reduce-scatter.2
  621.8 49.9 all-gather.26
  704.5 48.6 all-gather.24

commit v2 on v1

v2 whole, which is shorter than its diff:
```python
import functools

import jax
import jax.numpy as jnp
from jax import lax
from jax.experimental import pallas as pl
from jax.experimental.pallas import tpu as pltpu
from jax.sharding import PartitionSpec as P

D = 1536
HD = 64
EXPERTS = 16
NX, NY = 4, 4
EPSILON = 1e-06
SCALE = 0.125
NEGATIVE = -1e30
BF = jnp.bfloat16
F32 = jnp.float32


def moved(value, dx, dy, dc):
    route = []
    for x in range(NX):
        for y in range(NY):
            for c in range(2):
                target = (((x + dx) % NX) * NY + (y + dy) % NY) * 2 + (c ^ dc)
                route.append(((x * NY + y) * 2 + c, target))
    return lax.ppermute(value, "dp", route)


def swapped(value, axis):
    return lax.ppermute(value, axis, [(0, 1), (1, 0)])


def along_y(block):
    return jnp.concatenate([block] + [moved(block, 0, j, 0) for j in (1, 2, 3)], axis=0)


def along_x(block):
    return jnp.concatenate([block] + [moved(block, j, 0, 0) for j in (1, 2, 3)], axis=0)


def back_y(sums):
    parts = sums.reshape(4, -1, sums.shape[-1])
    total = parts[0].astype(F32)
    for j in (1, 2, 3):
        total = total + moved(parts[j], 0, -j, 0).astype(F32)
    return total


def back_x(sums):
    parts = sums.reshape(4, -1, sums.shape[-1])
    total = parts[0].astype(F32)
    for j in (1, 2, 3):
        total = total + moved(parts[j], -j, 0, 0).astype(F32)
    return total


def group_gather(block):
    column = along_y(block)
    return column, moved(column, 0, 0, 1)


def group_sum(own, other):
    both = own.astype(F32) + moved(other, 0, 0, 1).astype(F32)
    return back_y(both.astype(BF))


def tensor_sum(value):
    low = value.astype(BF)
    return low.astype(F32) + swapped(low, "tensor").astype(F32)


def norm_apply(value, gain):
    inverse = lax.rsqrt(jnp.mean(value * value, axis=-1, keepdims=True) + EPSILON)
    return value * inverse * gain


def norm_back(value, gain, grad):
    inverse = lax.rsqrt(jnp.mean(value * value, axis=-1, keepdims=True) + EPSILON)
    scaled = grad * gain
    inner = jnp.mean(scaled * value, axis=-1, keepdims=True)
    gain_grad = jnp.sum(grad * value * inverse, axis=0)
    return (inverse * scaled - inverse * inverse * inverse * value * inner, gain_grad)


def dot(left, right):
    return jnp.dot(left, right, preferred_element_type=F32)


def over_rows(left, right):
    return lax.dot_general(left, right, (((0,), (0,)), ((), ())), preferred_element_type=F32)


def against(left, right):
    return lax.dot_general(left, right, (((1,), (1,)), ((), ())), preferred_element_type=F32)


def nn(a, b):
    return lax.dot_general(a, b, (((1,), (0,)), ((), ())), preferred_element_type=F32)


def nt(a, b):
    return lax.dot_general(a, b, (((1,), (1,)), ((), ())), preferred_element_type=F32)


def tn(a, b):
    return lax.dot_general(a, b, (((0,), (0,)), ((), ())), preferred_element_type=F32)


SMEM = pl.BlockSpec(memory_space=pltpu.SMEM)
VMEM = pl.BlockSpec(memory_space=pltpu.VMEM)
ANY = pl.BlockSpec(memory_space=pl.ANY)


def shaped(*shape, dtype=BF):
    return jax.ShapeDtypeStruct(shape, dtype)


def params(mib):
    del mib
    return pltpu.CompilerParams(vmem_limit_bytes=58 << 20)


def cost(flops, bytes_accessed, exps=0):
    return pl.CostEstimate(flops=flops, bytes_accessed=bytes_accessed, transcendentals=exps)


def stacked(refs):
    return jnp.concatenate([ref[...] for ref in refs], axis=0)


def spread(block):
    lane = lax.broadcasted_iota(jnp.int32, (64, 128), 1)
    parts = []
    for k in range(6):
        wide = block[:, (k // 2) * 128 : (k // 2 + 1) * 128].astype(F32)
        half = k // 3
        if k % 2 != half:
            wide = pltpu.roll(wide, 64, 1)
        parts.append(jnp.where((lane >= 64) == (half == 1), wide, 0.0))
    return jnp.concatenate(parts, axis=0)


def gathered(turned):
    rows = turned.T
    lane = lax.broadcasted_iota(jnp.int32, (64, 128), 1)
    outs = []
    for b in range(3):
        two = []
        for k in (2 * b, 2 * b + 1):
            part = rows[k * 64 : (k + 1) * 64]
            if k % 2 != k // 3:
                part = pltpu.roll(part, 64, 1)
            two.append(part)
        outs.append(jnp.where(lane < 64, two[0], two[1]))
    return jnp.concatenate(outs, axis=1)


def bias_of(place_ref, h, start_ref):
    row = lax.broadcasted_iota(jnp.int32, (1024, 128), 0)
    token = lax.broadcasted_iota(jnp.int32, (1024, 128), 1) & 63
    x = (place_ref[0] - (row >> 6)) & 3
    y = (place_ref[1] - (row >> 8)) & 3
    c = place_ref[2] if h == 0 else 1 - place_ref[2]
    key = ((x * 4 + y) * 2 + c) * 64 + (row & 63)
    query = ((place_ref[0] * 4 + place_ref[1]) * 2 + place_ref[2]) * 64 + token
    bias = jnp.where((key <= query) & (key >= start_ref[...]), 0.0, NEGATIVE)
    return jnp.concatenate([bias, bias, bias], axis=1)


def attend_kernel(place_ref, st_ref, q_ref, *refs):
    keys = [stacked(refs[0:4]), stacked(refs[4:8])]
    values = [stacked(refs[8:12]), stacked(refs[12:16])]
    out_ref, lse_ref = refs[16:]
    query = (spread(q_ref[...]) * 0.125).astype(BF)
    scores = [nt(k, query) + bias_of(place_ref, h, st_ref) for h, k in enumerate(keys)]
    top = jnp.maximum(*[jnp.max(s, axis=0, keepdims=True) for s in scores])
    total = jnp.zeros_like(top)
    mixed = jnp.zeros((128, 384), F32)
    for s, v in zip(scores, values):
        raised = jnp.exp(s - top)
        total = total + jnp.sum(raised, axis=0, keepdims=True)
        mixed = mixed + tn(v, raised.astype(BF))
    out_ref[...] = gathered(mixed / total).astype(BF)
    lse_ref[0] = top + jnp.log(total)


def column(rows, width, base):
    return pl.BlockSpec((rows, width), lambda j: (0, j + base))


PAIRS = [SMEM, pl.BlockSpec((1, 128), lambda j: (0, 0))], [column(256, 128, 0)] * 8 + [column(256, 128, 2)] * 8
LSE = pl.BlockSpec((1, 1, 384), lambda j: (j, 0, 0))


def ignoring(count, kernel):
    return lambda *refs: kernel(*refs[count:])


def attend_forward(masks, query, pieces, *earlier):
    return pl.pallas_call(
        ignoring(len(earlier), attend_kernel),
        grid=(2,),
        in_specs=[ANY] * len(earlier) + PAIRS[0] + [column(64, 384, 0)] + PAIRS[1],
        out_specs=[column(64, 384, 0), LSE],
        out_shape=[shaped(64, 768), shaped(2, 1, 384, dtype=F32)],
        compiler_params=params(40),
        cost_estimate=cost(12 * 64 * 2048 * 64 * 4, 2 << 20, 12 * 64 * 2048),
        name="attend_forward",
    )(*earlier, *masks, query, *pieces, *pieces)


def attend_back_kernel(place_ref, st_ref, q_ref, do_ref, lse_ref, *refs):
    j = pl.program_id(0)
    key_columns = pl.ds(pl.multiple_of(j * 128, 128), 128)
    value_columns = pl.ds(pl.multiple_of(256 + j * 128, 128), 128)
    keys = [stacked(refs[0:4]), stacked(refs[4:8])]
    values = [stacked(refs[8:12]), stacked(refs[12:16])]
    dq_ref, near_ref, far_ref = refs[16:]
    query = (spread(q_ref[...]) * 0.125).astype(BF)
    grad = spread(do_ref[...]).astype(BF)
    weights, raws = [], []
    inner = jnp.zeros((1, 384), F32)
    for h, (k, v) in enumerate(zip(keys, values)):
        s = nt(k, query) + bias_of(place_ref, h, st_ref)
        w = jnp.exp(s - lse_ref[0])
        raw = nt(v, grad)
        inner = inner + jnp.sum(w * raw, axis=0, keepdims=True)
        weights.append(w)
        raws.append(raw)
    turned = jnp.zeros((128, 384), F32)
    for w, raw, k, out_ref in zip(weights, raws, keys, (near_ref, far_ref)):
        ds = (w * (raw - inner)).astype(BF)
        out_ref[:, key_columns] = nn(ds, query).astype(BF)
        out_ref[:, value_columns] = nn(w.astype(BF), grad).astype(BF)
        turned = turned + tn(k, ds)
    dq_ref[...] = gathered(turned * 0.125).astype(BF)


def attend_backward(masks, query, grad, lse, pieces, *earlier):
    return pl.pallas_call(
        ignoring(len(earlier), attend_back_kernel),
        grid=(2,),
        in_specs=[ANY] * len(earlier) + PAIRS[0] + [column(64, 384, 0)] * 2 + [LSE] + PAIRS[1],
        out_specs=[column(64, 384, 0)] + [pl.BlockSpec((1024, 512), lambda j: (0, 0))] * 2,
        out_shape=[shaped(64, 768), shaped(1024, 512), shaped(1024, 512)],
        compiler_params=params(48),
        cost_estimate=cost(12 * 64 * 2048 * 64 * 10, 4 << 20, 12 * 64 * 2048),
        name="attend_backward",
    )(*earlier, *masks, query, grad, lse, *pieces, *pieces)


def whole(*shape):
    return pl.BlockSpec(shape, lambda j: (0,) * len(shape))


def expert_kernel(where_ref, weight_ref, router_ref, routed_ref, *refs):
    token_refs, (pa_ref, pb_ref, pre_ref, mid_ref, gates_ref, all_ref) = refs[:8], refs[8:]
    for h, out_ref in enumerate((pa_ref, pb_ref)):
        rows = pl.ds(h * 256, 256)
        tokens = stacked(token_refs[4 * h : 4 * h + 4])
        all_ref[rows] = tokens
        parts = [tokens[:, r * 384 : (r + 1) * 384] for r in range(4)]
        routed = routed_ref[rows, 0:16].astype(F32) > 0
        logits = jnp.where(routed, nt(tokens, router_ref[...]), NEGATIVE)
        raised = jnp.exp(logits - jnp.max(logits, axis=1, keepdims=True))
        raised = jnp.where(routed, raised, 0.0)
        gates = raised / jnp.sum(raised, axis=1, keepdims=True)
        expert = lax.broadcasted_iota(jnp.int32, (256, 16), 1) - 2 * where_ref[3]
        gates = jnp.where((expert == 0) | (expert == 1), gates, 0.0)
        gates_ref[rows] = gates
        mids = []
        for e in range(2):
            gate_pre = sum(nn(parts[r], weight_ref[r, e]) for r in range(4))
            up_pre = sum(nn(parts[r], weight_ref[r, 2 + e]) for r in range(4))
            pre_ref[rows, e * 256 : (e + 1) * 256] = gate_pre.astype(BF)
            pre_ref[rows, (2 + e) * 256 : (3 + e) * 256] = up_pre.astype(BF)
            gate = jnp.sum(jnp.where(expert == e, gates, 0.0), axis=1, keepdims=True)
            mid = (gate_pre * jax.nn.sigmoid(gate_pre) * up_pre * gate).astype(BF)
            mid_ref[rows, e * 256 : (e + 1) * 256] = mid
            mids.append(mid)
        for r in range(4):
            made = nt(mids[0], weight_ref[r, 4]) + nt(mids[1], weight_ref[r, 5])
            out_ref[:, r * 384 : (r + 1) * 384] = made.astype(BF)


def experts_forward(where, tokens, routed, router, weights):
    return pl.pallas_call(
        expert_kernel,
        grid=(1,),
        in_specs=[SMEM, whole(4, 6, 384, 256), whole(16, D), whole(512, 128)] + [whole(64, D)] * 8,
        out_specs=[whole(256, D)] * 2 + [whole(512, 1024), whole(512, 512), whole(512, 16), whole(512, D)],
        out_shape=[shaped(256, D), shaped(256, D), shaped(512, 1024), shaped(512, 512)]
        + [shaped(512, 16, dtype=F32), shaped(512, D)],
        compiler_params=params(48),
        cost_estimate=cost(512 * 1536 * 1536 * 2, 10 << 20, 512 * 512),
        name="experts_forward",
    )(where, weights, router, routed, *tokens)


def expert_back_kernel(order_ref, weight_ref, router_ref, pre_ref, gates_ref, *refs):
    grad_refs, (pa_ref, pb_ref, gpre_ref, gated_ref) = refs[:-4], refs[-4:]
    if len(grad_refs) > 1:
        grad_refs, all_ref = grad_refs[:8], refs[8]
    for h, out_ref in enumerate((pa_ref, pb_ref)):
        rows = pl.ds(h * 256, 256)
        if len(grad_refs) > 1:
            grad_out = stacked(grad_refs[4 * h : 4 * h + 4])
            all_ref[rows] = grad_out
        else:
            grad_out = grad_refs[0][rows]
        parts = [grad_out[:, r * 384 : (r + 1) * 384] for r in range(4)]
        gates = gates_ref[rows]
        expert = lax.broadcasted_iota(jnp.int32, (256, 16), 1) - 2 * order_ref[3]
        gated = jnp.zeros((256, 16), F32)
        grads = []
        for e in range(2):
            raw = sum(nn(parts[r], weight_ref[r, 4 + e]) for r in range(4))
            gate_pre = pre_ref[rows, e * 256 : (e + 1) * 256].astype(F32)
            up_pre = pre_ref[rows, (2 + e) * 256 : (3 + e) * 256].astype(F32)
            sigmoid = jax.nn.sigmoid(gate_pre)
            activated = gate_pre * sigmoid
            grad_gates = jnp.sum(activated * up_pre * raw, axis=1, keepdims=True)
            gated = jnp.where(expert == e, gates * grad_gates, gated)
            raw = raw * jnp.sum(jnp.where(expert == e, gates, 0.0), axis=1, keepdims=True)
            grad_gate = (raw * up_pre * sigmoid * (1.0 + gate_pre * (1.0 - sigmoid))).astype(BF)
            grad_up = (raw * activated).astype(BF)
            gpre_ref[rows, e * 256 : (e + 1) * 256] = grad_gate
            gpre_ref[rows, (2 + e) * 256 : (3 + e) * 256] = grad_up
            grads.append((grad_gate, grad_up))
        gated_ref[rows] = gated
        high = gated.astype(BF)
        low = (gated - high.astype(F32)).astype(BF)
        for r in range(4):
            router = router_ref[:, r * 384 : (r + 1) * 384]
            made = nn(high, router) + nn(low, router)
            for e in range(2):
                made = made + nt(grads[e][0], weight_ref[r, e]) + nt(grads[e][1], weight_ref[r, 2 + e])
            out_ref[:, r * 384 : (r + 1) * 384] = made.astype(BF)


def experts_backward(where, grads, pre, gates, router, weights, *earlier):
    pieces = len(grads) > 1
    outs = pl.pallas_call(
        ignoring(len(earlier), expert_back_kernel),
        grid=(1,),
        in_specs=[ANY] * len(earlier)
        + [SMEM, whole(4, 6, 384, 256), whole(16, D), whole(512, 1024), whole(512, 16)]
        + ([whole(64, D)] * 8 if pieces else [whole(512, D)]),
        out_specs=[whole(512, D)] * pieces + [whole(256, D), whole(256, D), whole(512, 1024), whole(512, 16)],
        out_shape=[shaped(512, D)] * pieces
        + [shaped(256, D), shaped(256, D), shaped(512, 1024), shaped(512, 16, dtype=F32)],
        compiler_params=params(48),
        cost_estimate=cost(512 * 1536 * 1536 * 2, 10 << 20, 512 * 512),
        name="experts_backward",
    )(*earlier, where, weights, router, pre, gates, *grads)
    return outs if pieces else [grads[0]] + list(outs)


def expert_weight_kernel(gpre_ref, mid_ref, tokens_ref, grads_ref, out_ref):
    for n in range(6):
        left_ref, right_ref = (tokens_ref, gpre_ref) if n < 4 else (grads_ref, mid_ref)
        out_ref[0, n] = tn(left_ref[...], right_ref[:, (n % 4) * 256 : (n % 4 + 1) * 256]).astype(BF)


def expert_weight_grads(tokens, grads, gpre, mid, *earlier):
    return pl.pallas_call(
        ignoring(len(earlier), expert_weight_kernel),
        grid=(4,),
        in_specs=[ANY] * len(earlier) + [whole(512, 1024), whole(512, 512)] + [column(512, 384, 0)] * 2,
        out_specs=pl.BlockSpec((1, 6, 384, 256), lambda r: (r, 0, 0, 0)),
        out_shape=shaped(4, 6, 384, 256),
        compiler_params=params(40),
        cost_estimate=cost(512 * 1536 * 1536 * 2, 10 << 20),
        name="expert_weight_grads",
    )(*earlier, gpre, mid, tokens, grads)


def chosen(size, width, me):
    row = lax.broadcasted_iota(jnp.int32, (size, width), 0)
    lane = lax.broadcasted_iota(jnp.int32, (size, width), 1)
    return (row == lane + me * width).astype(BF)


def source(where_ref, b):
    return ((where_ref[1] - (b & 3)) & 3) * 2 + (where_ref[2] if b < 4 else 1 - where_ref[2])


def out_slice_kernel(where_ref, left_ref, right_ref, gated_ref, gates_ref, gains_ref, tokens_ref, out_ref):
    me = where_ref[3]
    pick = chosen(768, 96, me)
    left = jnp.concatenate([nn(left_ref[b, :, 1536:2304], pick).astype(BF) for b in range(8)], axis=0)
    right = jnp.concatenate([right_ref[b, :, 0:1536] for b in range(8)], axis=0)
    rows = tn(left, right)
    lane = lax.broadcasted_iota(jnp.int32, (64, 16), 1)
    logits = []
    for b in range(8):
        block = slice(b * 64, (b + 1) * 64)
        lanes = right_ref[source(where_ref, b), :, 1536:1664].astype(F32)
        inner = lanes[:, 0:1] + lanes[:, 1:2]
        grad = gated_ref[block] - 0.5 * gates_ref[block] * inner
        one = [jnp.sum(jnp.where(lane == 2 * me + e, grad, 0.0), axis=1, keepdims=True) for e in range(2)]
        logits.append(jnp.where(lane == 0, one[0], jnp.where(lane == 1, one[1], 0.0)).astype(BF))
    extra = tn(jnp.concatenate(logits, axis=0), tokens_ref[...])
    row = lax.broadcasted_iota(jnp.int32, (16, D), 0)
    gains = gains_ref[...]
    extra = jnp.where(row == 2, gains[0:1], jnp.where(row == 3, gains[1:2], extra))
    for r in range(4):
        to = (where_ref[0] - r) & 3
        out_ref[to, 0:96] = rows[:, r * 384 : (r + 1) * 384].astype(BF)
        out_ref[to, 96:112] = extra[:, r * 384 : (r + 1) * 384].astype(BF)


def out_slice(where, left, right, gated, gates, gains, tokens, *earlier):
    return pl.pallas_call(
        ignoring(len(earlier), out_slice_kernel),
        grid=(1,),
        in_specs=[ANY] * len(earlier)
        + [SMEM, whole(8, 64, 2304), whole(8, 64, 1664), whole(512, 16), whole(512, 16), whole(2, D), whole(512, D)],
        out_specs=whole(4, 112, 384),
        out_shape=shaped(4, 112, 384),
        compiler_params=params(40),
        cost_estimate=cost(512 * 1536 * 256, 6 << 20),
        name="out_slice",
    )(*earlier, where, left, right, gated, gates, gains, tokens)


def qkv_slice_kernel(relative, where_ref, left_ref, gain_ref, *refs):
    out_ref = refs[-1]
    me = where_ref[3]
    pick = chosen(1536, 192, me)
    if relative:
        right = stacked(refs[:8])
        order = [source(where_ref, b) for b in range(8)]
    else:
        right = jnp.concatenate([refs[0][b, :, 1664:2944] for b in range(8)], axis=0)
        order = list(range(8))
    left = jnp.concatenate([nn(left_ref[b, :, 0:1536], pick).astype(BF) for b in order], axis=0)
    rows = tn(left, right).astype(BF)
    row = lax.broadcasted_iota(jnp.int32, (8, 384), 0)
    for r in range(4):
        to = (where_ref[0] - r) & 3
        out_ref[to, 0:48] = rows[r * 48 : (r + 1) * 48]
        out_ref[to, 48:56, 0:384] = jnp.where(row == 0, gain_ref[:, r * 384 : (r + 1) * 384], 0.0).astype(BF)
        out_ref[to, 48:56, 384:1280] = jnp.zeros((8, 896), BF)


def qkv_slice(where, left, gain, rights, *earlier):
    relative = len(rights) == 8
    specs = [whole(64, 1280)] * 8 if relative else [whole(8, 64, 2944)]
    return pl.pallas_call(
        ignoring(len(earlier), functools.partial(qkv_slice_kernel, relative)),
        grid=(1,),
        in_specs=[ANY] * len(earlier) + [SMEM, whole(8, 64, 2304), whole(1, D)] + specs,
        out_specs=whole(4, 56, 1280),
        out_shape=shaped(4, 56, 1280),
        compiler_params=params(40),
        cost_estimate=cost(512 * 1536 * 512, 6 << 20),
        name="qkv_slice",
    )(*earlier, where, left, gain, *rights)


def qkv_rows_kernel(in_ref, q_ref, k_ref, v_ref):
    for x in range(4):
        rows = slice(x * 48, (x + 1) * 48)
        q_ref[rows] = in_ref[x, 0, 0:48, 0:768].astype(F32)
        k_ref[rows] = in_ref[x, 0, 0:48, 768:1024].astype(F32)
        v_ref[rows] = in_ref[x, 0, 0:48, 1024:1280].astype(F32)


def qkv_rows(everything):
    rows = lambda width: pl.BlockSpec((192, width), lambda j: (j, 0))
    return pl.pallas_call(
        qkv_rows_kernel,
        grid=(8,),
        in_specs=[pl.BlockSpec((4, 1, 56, 1280), lambda j: (0, j, 0, 0))],
        out_specs=[rows(768), rows(256), rows(256)],
        out_shape=[shaped(D, 768, dtype=F32), shaped(D, 256, dtype=F32), shaped(D, 256, dtype=F32)],
        compiler_params=params(32),
        cost_estimate=cost(0, 12 << 20),
        name="qkv_rows",
    )(everything)


def out_rows_kernel(in_ref, out_ref):
    for x in range(4):
        out_ref[:, x * 384 : (x + 1) * 384] = in_ref[x, 0, 0:96].astype(F32)


def out_rows(everything):
    return pl.pallas_call(
        out_rows_kernel,
        grid=(8,),
        in_specs=[pl.BlockSpec((4, 1, 112, 384), lambda j: (0, j, 0, 0))],
        out_specs=pl.BlockSpec((96, D), lambda j: (j, 0)),
        out_shape=shaped(768, D, dtype=F32),
        compiler_params=params(32),
        cost_estimate=cost(0, 7 << 20),
        name="out_rows",
    )(everything)


def gates_of(tokens, router, routed):
    logits = dot(tokens, router)
    top = jnp.max(jnp.where(routed > 0, logits, NEGATIVE), axis=1, keepdims=True)
    raised = jnp.where(routed > 0, jnp.exp(jnp.minimum(logits - top, 0.0)), 0.0)
    return raised / jnp.sum(raised, axis=1, keepdims=True)


X_GROUPS = [[(x * NY + y) * 2 + c for x in range(NX)] for y in range(NY) for c in range(2)]


Y_GROUPS = [[(x * NY + y) * 2 + c for y in range(NY) for c in range(2)] for x in range(NX)]


def replica_gather(shard):
    return lax.all_gather(shard, "dp", axis=0, axis_index_groups=X_GROUPS)


def replica_scatter(grads):
    flat = grads.reshape(-1, grads.shape[-1])
    return lax.psum_scatter(flat, "dp", scatter_dimension=0, axis_index_groups=X_GROUPS, tiled=True)


def after(value, *others):
    return lax.optimization_barrier((value, *others))[0]


def group_pieces(block):
    near = [block] + [moved(block, 0, j, 0) for j in (1, 2, 3)]
    return near + [moved(piece, 0, 0, 1) for piece in near]


def ordered(value):
    probe = value[(0,) * value.ndim]
    return probe == probe


def behind(value, earlier):
    return jnp.where(ordered(earlier), value, jnp.zeros_like(value))


def per_device(
    inputs,
    cotangent,
    segments,
    routes,
    norm_first,
    w_query,
    w_key,
    w_value,
    w_out,
    norm_second,
    w_router,
    w_gate,
    w_up,
    w_down,
):
    section = lax.axis_index("section")
    place = lax.axis_index("dp")
    here_x, here_y, here_c = place // (NY * 2), place // 2 % NY, place % 2
    me = place % 8
    first = section == 0
    rows = inputs.shape[1]

    def in_order(own, other):
        return jnp.where(first, own, other), jnp.where(first, other, own)

    def pick(pair):
        return lax.dynamic_index_in_dim(pair, section, 0, False)

    qkv_own = jnp.concatenate([w_query[0], w_key[0], w_value[0]], axis=1)
    act_both = norm_apply(inputs.astype(F32), norm_first[0]).astype(BF)
    qkv_both = dot(act_both.reshape(2 * rows, D), qkv_own).astype(BF)
    qkv_sent = lax.ppermute(qkv_both[rows:], "section", [(0, 1)])
    qkv_first = jnp.where(first, qkv_both[:rows], qkv_sent)

    pack = jnp.concatenate([norm_first, norm_second, w_router[0].T.astype(F32)], axis=0)
    packs = in_order(pack, swapped(pack, "section"))
    routers = [p[2:].astype(BF) for p in packs]
    experts = jnp.concatenate([w_gate[0], w_up[0], jnp.swapaxes(w_down[0], 1, 2)], axis=0)
    experts_other = swapped(experts, "section")
    expert_weights = [None, None]
    dense = jnp.concatenate(
        [lax.dynamic_slice_in_dim(qkv_own, place * 48, 48, 0)[:, i * 256 : (i + 1) * 256] for i in range(5)]
        + [lax.dynamic_slice_in_dim(w_out[0], place * 24, 24, 0)[:, i * 256 : (i + 1) * 256] for i in range(6)],
        axis=0,
    )
    dense = swapped(dense, "section")
    where = jnp.stack([here_x, here_y, here_c, me]).astype(jnp.int32)

    labels = pick(segments)
    query_labels = lax.dynamic_slice_in_dim(labels, place * rows, rows, 0)
    starts = jnp.sum((labels[None, :] < query_labels[:, None]).astype(jnp.int32), axis=1)
    masks = (where, jnp.concatenate([starts, starts])[None])

    own_routes = pick(routes)
    expert_ids = jnp.arange(EXPERTS, dtype=jnp.int32)
    routed_own = jnp.sum((own_routes[:, :, None] == expert_ids).astype(F32), axis=1)
    given = pick(cotangent)
    sent = jnp.concatenate([given, jnp.pad(routed_own.astype(BF), ((0, 0), (0, 128 - EXPERTS)))], axis=1)
    got = group_pieces(sent)
    given_all = jnp.concatenate(got, axis=0)
    routed = jnp.concatenate([piece[:, D:] for piece in got], axis=0)

    hidden = pick(inputs).astype(F32)
    saved = []
    outs_w = qkvs_w = None
    for layer in range(2):
        gain_one, gain_two = packs[layer][0], packs[layer][1]
        activation = norm_apply(hidden, gain_one).astype(BF)
        qkv = qkv_first if layer == 0 else dot(activation, qkvs_w[1]).astype(BF)
        query, pair = qkv[:, :768], qkv[:, 768:]
        slab = along_x(pair)
        if layer == 0:
            experts_first = jnp.where(first & ordered(slab), experts, experts_other)
            expert_weights[0] = replica_gather(experts_first)
            slab = behind(slab, experts_first)
        near = [slab] + [moved(slab, 0, j, 0) for j in (1, 2, 3)]
        pieces = near + [moved(piece, 0, 0, 1) for piece in near]
        mixed, log_total = attend_forward(masks, query, pieces, *([] if layer == 0 else [saved[0][-2]]))
        if layer == 0:
            mixed_sent = lax.ppermute(mixed, "section", [(1, 0)])
            partial = dot(jnp.concatenate([mixed, mixed_sent], axis=0), w_out[0]).astype(BF)
            both_axes = ("section", "tensor")
            straight = lax.ppermute(partial[rows:], both_axes, [(0, 2), (1, 3)])
            across = lax.ppermute(partial[rows:], both_axes, [(0, 3), (1, 2)])
            turned = lax.ppermute(partial[:rows], both_axes, [(0, 1), (1, 0)])
            middle = hidden + (
                jnp.where(first, partial[:rows], straight).astype(F32) + jnp.where(first, turned, across).astype(F32)
            )
            dense_all = lax.all_gather(behind(dense, pieces[3]), "dp", axis=0)
            other_qkv = jnp.swapaxes(dense_all[:, :240].reshape(32, 5, 48, 256), 1, 2).reshape(D, 1280)
            other_out = jnp.swapaxes(dense_all[:, 240:].reshape(32, 6, 24, 256), 1, 2).reshape(768, D)
            qkvs_w = in_order(qkv_own, other_qkv)
            outs_w = in_order(w_out[0], other_out)
            experts_second = jnp.where(first & ordered(mixed), experts_other, experts)
            expert_weights[1] = replica_gather(experts_second)
        else:
            middle = hidden + tensor_sum(dot(mixed, outs_w[layer]))
        second = norm_apply(middle, gain_two).astype(BF)
        tokens = group_pieces(second)
        made_near, made_far, pre, mid, gates, tokens = experts_forward(
            where, tokens, routed, routers[layer], expert_weights[layer]
        )
        made = group_sum(made_near, made_far).reshape(rows, D).astype(BF)
        if layer == 0:
            made = behind(made, qkvs_w[1])
        branch = tensor_sum(made)
        result = middle + branch
        cut = behind(jnp.concatenate([activation, mixed], axis=1), result)
        lefts = lax.all_gather(cut, "dp", axis=0, axis_index_groups=Y_GROUPS)
        saved.append(
            (hidden, query, pieces, log_total, middle, second, tokens, pre, mid, gates, branch, lefts, cut, result)
        )
        hidden = result

    def own_of(a, b):
        return jnp.where(first, a, b)

    def from_other(for_first, for_second):
        return swapped(own_of(for_second, for_first).astype(BF), "section").astype(F32)

    def over_sections(a, b):
        return own_of(a, b).astype(F32) + from_other(a, b)

    grad_output = given.astype(F32)
    grads = []
    earlier = [saved[1][-2]]
    for layer in (1, 0):
        hidden, query, pieces, log_total, middle, second, tokens, pre, mid, gates, branch, lefts, _, _ = saved[layer]
        gain_one, gain_two = packs[layer][0], packs[layer][1]
        router = routers[layer]
        grad_pieces = [given_all] if layer == 1 else group_pieces(grad_output.astype(BF))
        grad_all, back_near, back_far, grad_pre, gated = experts_backward(
            where, grad_pieces, pre, gates, router, expert_weights[layer], *earlier
        )
        both = (back_near.astype(F32) + moved(back_far, 0, 0, 1).astype(F32)).astype(BF)
        weight_grads = expert_weight_grads(tokens, grad_all, grad_pre, mid, both)
        expert_part = replica_scatter(weight_grads)
        grad_second = tensor_sum(back_y(both).reshape(rows, D))
        inner = jnp.sum(grad_output * branch, axis=1, keepdims=True)
        own_gates = gates_of(second, router.T, routed_own)
        grad_second = grad_second - dot(inner * own_gates, router.astype(F32))
        grad_from_norm, gain_two_grad = norm_back(middle, gain_two, grad_second)
        grad_middle = grad_output + grad_from_norm
        grad_branch = grad_middle.astype(BF)
        inner_high = inner.astype(BF)
        inner_low = (inner - inner_high.astype(F32)).astype(BF)
        lanes = jnp.concatenate([inner_high, inner_low, jnp.zeros((rows, 126), BF)], axis=1)
        right = jnp.concatenate([grad_branch, lanes], axis=1)
        grad_mixed = against(grad_branch, outs_w[layer]).astype(BF)
        if layer == 1:
            earlier = [weight_grads, lefts, saved[0][-3]]
        else:
            earlier = [weight_grads, right, grads[0][3]]
        grad_query, back_near, back_far = attend_backward(masks, query, grad_mixed, log_total, pieces, *earlier)
        both = (back_near.astype(F32) + moved(back_far, 0, 0, 1).astype(F32)).astype(BF)
        if layer == 0:
            late = grads[0]
            out_blocks = [out_slice(where, *late[2], both)]
            late_qkv = qkv_slice(where, late[2][0], jnp.zeros((1, D), F32), [late[2][1]], both)
            late_qkv = back_x(late_qkv.reshape(224, 1280)).reshape(56, 1280)
        half = back_y(both)
        grad_pair = back_x(half.astype(BF)).reshape(rows, 512).astype(BF)
        grad_qkv = jnp.concatenate([grad_query, grad_pair], axis=1)
        grad_activation = tensor_sum(against(grad_qkv, qkvs_w[layer]))
        grad_from_first, gain_one_grad = norm_back(hidden, gain_one, grad_activation)
        grad_input = grad_middle + grad_from_first
        if layer == 1:
            gains = jnp.stack([gain_two_grad, gain_one_grad])
            right = jnp.concatenate([right, grad_qkv], axis=1)
            earlier = [right]
            right = lax.all_gather(right, "dp", axis=0, axis_index_groups=Y_GROUPS)
            grads.append((grad_input, None, (lefts, right, gated, gates, gains, tokens), expert_part))
        else:
            gains = jnp.stack([gain_two_grad, jnp.zeros_like(gain_two_grad)])
            right = lax.all_gather(right, "dp", axis=0, axis_index_groups=Y_GROUPS)
            out_blocks = [out_slice(where, lefts, right, gated, gates, gains, tokens, half)] + out_blocks
            out_blocks = over_sections(*out_blocks).astype(BF)
            out_sum = back_x(out_blocks.reshape(448, 384)).reshape(112, 384).astype(BF)
            qkv_blocks = qkv_slice(where, lefts, gain_one_grad[None], group_pieces(grad_qkv), out_sum, expert_part)
            qkv_part = back_x(qkv_blocks.reshape(224, 1280)).reshape(56, 1280)
            grads.append((grad_input, qkv_part, None, expert_part))
        grad_output = grad_input
    grads = grads[::-1]

    def by_batch(own, other):
        return jnp.stack([jnp.where(first, own, other), jnp.where(first, other, own)])[None]

    results = by_batch(own_of(saved[0][-1], saved[1][-1]), from_other(saved[0][-1], saved[1][-1]))
    input_grads = by_batch(own_of(grads[0][0], grads[1][0]), from_other(grads[0][0], grads[1][0]))
    qkv_sum = over_sections(grads[0][1], late_qkv).astype(BF)
    out_all = lax.all_gather(out_sum, "dp", axis=0).reshape(4, 8, 112, 384)
    qkv_all = lax.all_gather(qkv_sum, "dp", axis=0).reshape(4, 8, 56, 1280)
    query_sum, key_sum, value_sum = qkv_rows(qkv_all)
    out_full = out_rows(out_all)
    router_sum = jnp.transpose(out_all[:, :, 96:98], (1, 2, 0, 3)).reshape(EXPERTS, D)
    router_sum = tensor_sum(router_sum)
    gain_two_sum = jnp.sum(out_all[:, :, 98].astype(F32), axis=1).reshape(1, D)
    gain_one_sum = jnp.sum(out_all[:, :, 99].astype(F32) + qkv_all[:, :, 48, :384].astype(F32), axis=1).reshape(1, D)
    expert_sum = over_sections(grads[0][3], grads[1][3]).reshape(3, 2, 384, 256)
    return (
        results,
        input_grads,
        gain_one_sum,
        query_sum[None],
        key_sum[None],
        value_sum[None],
        out_full[None],
        gain_two_sum,
        router_sum.T[None],
        expert_sum[0][None],
        expert_sum[1][None],
        jnp.swapaxes(expert_sum[2], 1, 2)[None],
    )


def solution(mesh):
    in_specs = (
        P(None, "dp", None),
        P(None, "dp", None),
        P(),
        P(None, "dp", None),
        P("section", None),
        P("section", None, "tensor"),
        P("section", None, "tensor"),
        P("section", None, "tensor"),
        P("section", "tensor", None),
        P("section", None),
        P("section", None, None),
        P("section", "dp", None, "tensor"),
        P("section", "dp", None, "tensor"),
        P("section", "dp", "tensor", None),
    )
    out_specs = (
        P("section", None, "dp", None),
        P("section", None, "dp", None),
        P("section", None),
        P("section", None, "tensor"),
        P("section", None, "tensor"),
        P("section", None, "tensor"),
        P("section", "tensor", None),
        P("section", None),
        P("section", None, None),
        P("section", "dp", None, "tensor"),
        P("section", "dp", None, "tensor"),
        P("section", "dp", "tensor", None),
    )
    return jax.shard_map(
        per_device, mesh=mesh, in_specs=in_specs, out_specs=out_specs, check_vma=False
    )
```

time: 810 us -> 678 us (0.84)
  Pallas kernels: 0 us -> 109 us
  local copies, waits for them, and re-layouts: 156 us -> 65.3 us
  matrix products: 101 us -> 18.6 us
  blocking collectives: 58.2 us -> 0 us
  other arithmetic: 84.4 us -> 53.8 us
  starting transfers between devices: 172 us -> 182 us
    pallas_call x0 -> x16, Pallas kernels: none -> 109 us  [the longest x2 18.2 us: experts_backward(): pl.pallas_call(ignoring(len(earlier), expert_back_kernel), grid=(1,), in_...]
    dot_general x40 -> x0, matrix products: 74.8 us -> none  [the longest x6 9.06 us: over_rows(): lax.dot_general(left, right, (((0,), (0,)), ((), ())), preferred_element_...]
    all_gather x3 -> x0, blocking collectives: 58.2 us -> none  [the longest x1 29.5 us: per_device(): gain_one_all = lax.all_gather(gain_one_sum, 'dp', axis=0)]
    ppermute x19 -> x16, waiting for transfers between devices: 103 us -> 59.5 us  [swapped(): return lax.ppermute(value, axis, [(0, 1), (1, 0)])]
    concatenate x20 -> x5, local copies, waits for them, and re-layouts: 29.3 us -> 4.86 us  [the longest x1 1.76 us: per_device(): right = jnp.concatenate([right, grad_qkv], axis=1)]
    convert_element_type x8 -> x1, local copies, waits for them, and re-layouts: 19.5 us -> 0.1 us  [per_device(): routed_own.astype(BF)]
    ppermute x1, waiting for transfers between devices: 2.8 us -> 21.9 us  [per_device(): qkv_sent = lax.ppermute(qkv_both[rows:], 'section', [(0, 1)])]
    all_gather x3 -> x6, waiting for transfers between devices: 0.02 us -> 19 us  [the longest x1 19 us: per_device(): qkv_all = lax.all_gather(qkv_sum, 'dp', axis=0).reshape(4, 8, 56, 1280)]
  transfers between devices with their start and end apart: 118 -> 126, of which waited for: 52 -> 57; matrix products, arithmetic and copies ran while one was open for 39% -> 18% of each run, Pallas kernels for 0% -> 15%
where the time goes in v2:
time: 678 us; the launch traced here: 667 us
  waiting for transfers between devices  212 us (31%)
  starting transfers between devices  182 us (27%)
  Pallas kernels  109 us (16%)
  local copies, waits for them, and re-layouts  65.3 us (10%)
  other arithmetic  53.8 us (8%)
  between operations  25.5 us (4%)
  matrix products  18.6 us (3%)
    ppermute x94, starting transfers between devices, moved(): return lax.ppermute(value, 'dp', route)  134 us
    ppermute x94, waiting for transfers between devices, moved(): return lax.ppermute(value, 'dp', route)  99.5 us
    ppermute x16, waiting for transfers between devices, swapped(): return lax.ppermute(value, axis, [(0, 1), (1, 0)])  59.5 us
    ppermute x16, starting transfers between devices, swapped(): return lax.ppermute(value, axis, [(0, 1), (1, 0)])  36.3 us
    unnamed x324, local copies, waits for them, and re-layouts  31.8 us
    ppermute x1, waiting for transfers between devices, per_device(): qkv_sent = lax.ppermute(qkv_both[rows:], 'section', [(0, 1)])  21.9 us
    all_gather x1, waiting for transfers between devices, per_device(): qkv_all = lax.all_gather(qkv_sum, 'dp', axis=0).reshape(4, 8, 56, 1280)  19 us
    pallas_call x2, Pallas kernels, experts_backward(): pl.pallas_call(ignoring(len(earlier), expert_back_kernel), grid=(1,), in_...  18.2 us
  transfers between devices with their start and end apart: 126, of which 57 were waited for; matrix products, arithmetic and copies ran while one was open for 18% of the time, Pallas kernels for 15%

profile of v2, /device:TPU:1, one launch (start us, length us, event | category | flops | bytes accessed | tf_op | source)
XLA Modules:
  0.0 666.9 jit_solution(12751555383572577186)
XLA Ops:
  19.8 21.9 %collective-permute-done = bf16[64,1280]{1,0:T(8,128)(2,1)S(1)} collective-permute-done((bf16[64,1280]{1,0:T(8,128)(2,1)S(1)}, bf16[64,1280]{1,0:T(8,128)(2,1)S(1)}, u32[]{:S(2)}, u32[]{:S(2)}) %collective-permute-start) | collective-permute-done | bytes 163872 | tf_op jit(solution)/shard_map/ppermute | solution.py:576
  83.2 5.3 collective-permute-start.8
  89.5 5.8 collective-permute-start.9
  99.7 5.6 attend_forward.2
  107.8 5.6 collective-permute-done.12
  124.1 6.2 collective-permute-done.14
  137.3 6.4 collective-permute-done.25.refs_1_
  148.8 5.1 collective-permute-start.31
  155.4 8.7 %experts_forward.2 = (bf16[256,1536]{1,0:T(8,128)(2,1)}, bf16[256,1536]{1,0:T(8,128)(2,1)}, bf16[512,1024]{1,0:T(8,128)(2,1)}, bf16[512,512]{1,0:T(8,128)(2,1)},...) custom-call(s32[4]{0:T(128)} %pad_add_fusion.refs_0_.where_ref.refs_1_.refs_3_.refs_2_, bf16[4,6,384,256]{3,2,1,0:T(8,128)(2,1)} %bitcast.263, ...), custom_call_target="tpu_custom_call" | custom-call | flops 2415919104 | bytes 10485760 | tf_op jit(solution)/shard_map/experts_forward/pallas_call | solution.py:289
  186.5 5.4 collective-permute-done.36
  221.0 5.6 attend_forward.3
  230.1 6.5 collective-permute-done.47
  254.0 8.5 %experts_forward.3 = (bf16[256,1536]{1,0:T(8,128)(2,1)}, bf16[256,1536]{1,0:T(8,128)(2,1)}, bf16[512,1024]{1,0:T(8,128)(2,1)}, bf16[512,512]{1,0:T(8,128)(2,1)},...) custom-call(s32[4]{0:T(128)} %pad_add_fusion.refs_0_.where_ref.refs_1_.refs_3_.refs_2_, bf16[4,6,384,256]{3,2,1,0:T(8,128)(2,1)} %bitcast.265, ...), custom_call_target="tpu_custom_call" | custom-call | flops 2415919104 | bytes 10485760 | tf_op jit(solution)/shard_map/experts_forward/pallas_call | solution.py:289
  270.4 5.7 collective-permute-done.58
  276.2 4.9 collective-permute-done.57
  284.1 4.7 collective-permute-done.59
  303.0 9.4 %experts_backward.2 = (bf16[256,1536]{1,0:T(8,128)(2,1)}, bf16[256,1536]{1,0:T(8,128)(2,1)}, bf16[512,1024]{1,0:T(8,128)(2,1)}, f32[512,16]{1,0:T(8,128)}) custom-call(bf16[64,2304]{1,0:T(8,128)(2,1)} %maximum_select_fusion.1.refs_0_, s32[4]{0:T(128)} %pad_add_fusion.refs_0_.where_ref.refs_1_.refs_3_.refs_2_, bf16[4,6,384,256]{3,2,1,0:T(8,128)(2,1)} %bitcast.266, ...), custom_call_target="tpu_custom_call" | custom-call | flops 2415919104 | bytes 10485760 | tf_op jit(solution)/shard_map/experts_backward/pallas_call | solution.py:345
  318.0 6.8 %expert_weight_grads.2.refs_0_ = bf16[4,6,384,256]{3,2,1,0:T(8,128)(2,1)} custom-call(bf16[256,1536]{1,0:T(8,128)(2,1)} %add_convert_fusion.3.refs_0_, bf16[512,1024]{1,0:T(8,128)(2,1)} %get-tuple-element.56.refs_1_, bf16[512,512]{1,0:T(8,128)(2,1)} %get-tuple-element.57.refs_2_, bf16[512,1536]{1,0:T(8,128)(2,1)} %get-tuple-element.58.refs_3_.refs_7_, ...), custom_call_target="tpu_custom_call" | custom-call | flops 2415919104 | bytes 10485760 | tf_op jit(solution)/shard_map/expert_weight_grads/pallas_call | solution.py:368
  347.4 8.3 %attend_backward.2 = (bf16[64,768]{1,0:T(8,128)(2,1)}, bf16[1024,512]{1,0:T(8,128)(2,1)}, bf16[1024,512]{1,0:T(8,128)(2,1)}) custom-call(bf16[4,6,384,256]{3,2,1,0:T(8,128)(2,1)} %expert_weight_grads.2.refs_0_, bf16[8,64,2304]{2,1,0:T(8,128)(2,1)} %all-gather.17.cloned.1.call-done.refs_1_.refs_2_, ...), custom_call_target="tpu_custom_call" | custom-call | flops 1006632960 | bytes 4194304 | tf_op jit(solution)/shard_map/attend_backward/pallas_call | solution.py:242
  368.1 5.1 collective-permute-done.69
  373.3 6.5 collective-permute-done.68
  429.0 8.9 %experts_backward.3 = (bf16[512,1536]{1,0:T(8,128)(2,1)}, bf16[256,1536]{1,0:T(8,128)(2,1)}, bf16[256,1536]{1,0:T(8,128)(2,1)}, bf16[512,1024]{1,0:T(8,128)(2,1)}, f32[512,16]{1,0:T(8,128)}) custom-call(bf16[64,2944]{1,0:T(8,128)(2,1)} %concatenate.95.refs_0_, s32[4]{0:T(128)} %pad_add_fusion.refs_0_.where_ref.refs_1_.refs_3_.refs_2_, ...), custom_call_target="tpu_custom_call" | custom-call | flops 2415919104 | bytes 10485760 | tf_op jit(solution)/shard_map/experts_backward/pallas_call | solution.py:345
  446.5 7.1 %collective-permute-done.84 = bf16[64,1536]{1,0:T(8,128)(2,1)S(1)} collective-permute-done((bf16[64,1536]{1,0:T(8,128)(2,1)S(1)}, bf16[64,1536]{1,0:T(8,128)(2,1)S(1)}, u32[]{:S(2)}, u32[]{:S(2)}) %collective-permute-start.84) | collective-permute-done | bytes 196640 | tf_op jit(solution)/shard_map/ppermute | solution.py:28
  464.2 6.8 %expert_weight_grads.3.refs_0_ = bf16[4,6,384,256]{3,2,1,0:T(8,128)(2,1)} custom-call(bf16[256,1536]{1,0:T(8,128)(2,1)} %copy-done.12, bf16[512,1024]{1,0:T(8,128)(2,1)} %get-tuple-element.67.refs_1_, bf16[512,512]{1,0:T(8,128)(2,1)} %get-tuple-element.68.refs_2_, bf16[512,1536]{1,0:T(8,128)(2,1)} %get-tuple-element.69.refs_3_.refs_7_, ...), custom_call_target="tpu_custom_call" | custom-call | flops 2415919104 | bytes 10485760 | tf_op jit(solution)/shard_map/expert_weight_grads/pallas_call | solution.py:368
  475.1 8.3 %attend_backward.3 = (bf16[64,768]{1,0:T(8,128)(2,1)}, bf16[1024,512]{1,0:T(8,128)(2,1)}, bf16[1024,512]{1,0:T(8,128)(2,1)}) custom-call(bf16[4,6,384,256]{3,2,1,0:T(8,128)(2,1)} %expert_weight_grads.3.refs_0_, bf16[64,1664]{1,0:T(8,128)(2,1)} %concatenate.96.refs_1_, bf16[2304,256]{1,0:T(8,128)(2,1)} %reduce-scatter.3.cloned.1.call-done.refs_2_, ...), custom_call_target="tpu_custom_call" | custom-call | flops 1006632960 | bytes 4194304 | tf_op jit(solution)/shard_map/attend_backward/pallas_call | solution.py:242
  500.7 6.1 collective-permute-done.88
  516.9 7.3 %collective-permute-done.95 = bf16[4,112,384]{2,1,0:T(8,128)(2,1)S(1)} collective-permute-done((bf16[4,112,384]{2,1,0:T(8,128)(2,1)S(1)}, bf16[4,112,384]{2,1,0:T(8,128)(2,1)S(1)}, u32[]{:S(2)}, u32[]{:S(2)}) %collective-permute-start.95) | collective-permute-done | bytes 344096 | tf_op jit(solution)/shard_map/ppermute | solution.py:32
  542.7 5.3 qkv_slice.3
  606.3 6.3 out_rows.1
  612.6 13.8 %collective-permute-done.113 = bf16[16,1536]{1,0:T(8,128)(2,1)S(1)} collective-permute-done((bf16[16,1536]{1,0:T(8,128)(2,1)S(1)}, bf16[16,1536]{1,0:T(8,128)(2,1)S(1)}, u32[]{:S(2)}, u32[]{:S(2)}) %collective-permute-start.113) | collective-permute-done | bytes 49184 | tf_op jit(solution)/shard_map/ppermute | solution.py:32
  631.1 19.0 %all-gather.33.cloned.1.call-done = bf16[1792,1280]{1,0:T(8,128)(2,1)} async-done(((bf16[56,1280]{1,0:T(8,128)(2,1)}), bf16[1792,1280]{1,0:T(8,128)(2,1)}) %all-gather.33.cloned.1.call-update) | async-done | bytes 4587536 | tf_op jit(solution)/shard_map/all_gather | solution.py:736
  651.4 7.3 %qkv_rows.1 = (f32[1536,768]{1,0:T(8,128)}, f32[1536,256]{1,0:T(8,128)}, f32[1536,256]{1,0:T(8,128)}) custom-call(bf16[4,8,56,1280]{3,2,1,0:T(8,128)(2,1)} %bitcast.228), custom_call_target="tpu_custom_call" | custom-call | bytes 12582912 | tf_op jit(solution)/shard_map/qkv_rows/pallas_call | solution.py:474
  (730 shorter events, 397.4 us)
Async XLA Ops:
  7.2 148.1 %all-gather.23.cloned.1.call-start = ((), (), s32[]{:S(2)}) async-start(), calls=%async_computation.7 | async-start | bytes 5898240 | tf_op jit(solution)/shard_map/all_gather | solution.py:518
  10.9 32.7 %collective-permute-start.1 = (bf16[6,384,256]{2,1,0:T(8,128)(2,1)}, bf16[6,384,256]{2,1,0:T(8,128)(2,1)}, u32[]{:S(2)}, u32[]{:S(2)}) collective-permute-start(bf16[6,384,256]{2,1,0:T(8,128)(2,1)} %pad_maximum_fusion.1), channel_id=1, source_target_pairs={{0,64},{64,0},{1,65},{65,1},{2,66},{66,2},{3,67},{67,3},{4,68},{68... | collective-permute-start | bytes 3538952 | tf_op jit(solution)/shard_map/ppermute | solution.py:32
  17.9 23.8 %collective-permute-start = (bf16[64,1280]{1,0:T(8,128)(2,1)S(1)}, bf16[64,1280]{1,0:T(8,128)(2,1)S(1)}, u32[]{:S(2)}, u32[]{:S(2)}) collective-permute-start(bf16[64,1280]{1,0:T(8,128)(2,1)S(1)} %slice.419), channel_id=1, source_target_pairs={{0,64},{1,65},{2,66},{3,67},{4,68},{5,69},{6,70},{7,71},{8,72},{9,... | collective-permute-start | bytes 491528 | tf_op jit(solution)/shard_map/ppermute | solution.py:576
  44.8 129.2 %all-gather.21.cloned.1.call-start = ((), (), s32[]{:S(2)}) async-start(), calls=%async_computation.6 | async-start | bytes 6488064 | tf_op jit(solution)/shard_map/all_gather | solution.py:633
  67.9 185.2 %all-gather.25.cloned.1.call-start = ((), (), s32[]{:S(2)}) async-start(), calls=%async_computation.8 | async-start | bytes 5898240 | tf_op jit(solution)/shard_map/all_gather | solution.py:518
  69.6 18.9 %collective-permute-start.19 = (bf16[64,1664]{1,0:T(8,128)(2,1)}, bf16[64,1664]{1,0:T(8,128)(2,1)S(1)}, u32[]{:S(2)}, u32[]{:S(2)}) collective-permute-start(bf16[64,1664]{1,0:T(8,128)(2,1)} %get-tuple-element.163), channel_id=1, source_target_pairs={{0,8},{2,10},{4,12},{6,14},{8,0},{10,2},{12,4},{14,6},{16,24},{18,... | collective-permute-start | bytes 638984 | tf_op jit(solution)/shard_map/ppermute | solution.py:28
  72.1 23.9 %collective-permute-start.20 = (bf16[64,1664]{1,0:T(8,128)(2,1)}, bf16[64,1664]{1,0:T(8,128)(2,1)}, u32[]{:S(2)}, u32[]{:S(2)}) collective-permute-start(bf16[64,1664]{1,0:T(8,128)(2,1)} %get-tuple-element.163), channel_id=1, source_target_pairs={{0,12},{2,14},{4,0},{6,2},{8,4},{10,6},{12,8},{14,10},{16,28},{18,... | collective-permute-start | bytes 638984 | tf_op jit(solution)/shard_map/ppermute | solution.py:28
  83.2 14.6 %collective-permute-start.8 = (bf16[256,512]{1,0:T(8,128)(2,1)S(1)}, bf16[256,512]{1,0:T(8,128)(2,1)S(1)}, u32[]{:S(2)}, u32[]{:S(2)}) collective-permute-start(bf16[256,512]{1,0:T(8,128)(2,1)S(1)} %maximum_select_fusion.4.refs_3_.refs_11_.refs_8_.refs_16_), channel_id=1, source_target_pairs={{0,2},{2,0},{4,6},{6,4},{8,10},{10,8},{12,14},{14,12},{16,18},{18,... | collective-permute-start | bytes 786440 | tf_op jit(solution)/shard_map/ppermute | solution.py:28
  97.7 22.6 %collective-permute-start.22 = (bf16[64,1664]{1,0:T(8,128)(2,1)S(1)}, bf16[64,1664]{1,0:T(8,128)(2,1)S(1)}, u32[]{:S(2)}, u32[]{:S(2)}) collective-permute-start(bf16[64,1664]{1,0:T(8,128)(2,1)S(1)} %collective-permute-done.18), channel_id=1, source_target_pairs={{0,2},{2,0},{4,6},{6,4},{8,10},{10,8},{12,14},{14,12},{16,18},{18,... | collective-permute-start | bytes 638984 | tf_op jit(solution)/shard_map/ppermute | solution.py:28
  97.9 36.9 %collective-permute-start.23 = (bf16[64,1664]{1,0:T(8,128)(2,1)S(1)}, bf16[64,1664]{1,0:T(8,128)(2,1)S(1)}, u32[]{:S(2)}, u32[]{:S(2)}) collective-permute-start(bf16[64,1664]{1,0:T(8,128)(2,1)S(1)} %collective-permute-done.19), channel_id=1, source_target_pairs={{0,2},{2,0},{4,6},{6,4},{8,10},{10,8},{12,14},{14,12},{16,18},{18,... | collective-permute-start | bytes 638984 | tf_op jit(solution)/shard_map/ppermute | solution.py:28
  98.3 55.6 %collective-permute-start.24 = (bf16[64,1664]{1,0:T(8,128)(2,1)}, bf16[64,1664]{1,0:T(8,128)(2,1)S(1)}, u32[]{:S(2)}, u32[]{:S(2)}) collective-permute-start(bf16[64,1664]{1,0:T(8,128)(2,1)} %collective-permute-done.20), channel_id=1, source_target_pairs={{0,2},{2,0},{4,6},{6,4},{8,10},{10,8},{12,14},{14,12},{16,18},{18,... | collective-permute-start | bytes 638984 | tf_op jit(solution)/shard_map/ppermute | solution.py:28
  115.7 14.6 %collective-permute-start.15 = (bf16[64,1536]{1,0:T(8,128)(2,1)S(1)}, bf16[64,1536]{1,0:T(8,128)(2,1)S(1)}, u32[]{:S(2)}, u32[]{:S(2)}) collective-permute-start(bf16[64,1536]{1,0:T(8,128)(2,1)S(1)} %get-tuple-element.149), channel_id=1, source_target_pairs={{0,65},{1,64},{2,67},{3,66},{4,69},{5,68},{6,71},{7,70},{8,73},{9,... | collective-permute-start | bytes 589832 | tf_op jit(solution)/shard_map/ppermute | solution.py:628
  132.1 16.1 %collective-permute-start.26 = (bf16[64,1536]{1,0:T(8,128)(2,1)S(1)}, bf16[64,1536]{1,0:T(8,128)(2,1)S(1)}, u32[]{:S(2)}, u32[]{:S(2)}) collective-permute-start(bf16[64,1536]{1,0:T(8,128)(2,1)S(1)} %multiply_convert_fusion.2.refs_0_), channel_id=1, source_target_pairs={{0,8},{2,10},{4,12},{6,14},{8,0},{10,2},{12,4},{14,6},{16,24},{18,... | collective-permute-start | bytes 589832 | tf_op jit(solution)/shard_map/ppermute | solution.py:28
  132.5 16.4 %collective-permute-start.27 = (bf16[64,1536]{1,0:T(8,128)(2,1)S(1)}, bf16[64,1536]{1,0:T(8,128)(2,1)S(1)}, u32[]{:S(2)}, u32[]{:S(2)}) collective-permute-start(bf16[64,1536]{1,0:T(8,128)(2,1)S(1)} %multiply_convert_fusion.2.refs_0_), channel_id=1, source_target_pairs={{0,12},{2,14},{4,0},{6,2},{8,4},{10,6},{12,8},{14,10},{16,28},{18,... | collective-permute-start | bytes 589832 | tf_op jit(solution)/shard_map/ppermute | solution.py:28
  135.4 19.1 %collective-permute-start.28 = (bf16[64,1536]{1,0:T(8,128)(2,1)S(1)}, bf16[64,1536]{1,0:T(8,128)(2,1)S(1)}, u32[]{:S(2)}, u32[]{:S(2)}) collective-permute-start(bf16[64,1536]{1,0:T(8,128)(2,1)S(1)} %multiply_convert_fusion.2.refs_0_), channel_id=1, source_target_pairs={{0,2},{2,0},{4,6},{6,4},{8,10},{10,8},{12,14},{14,12},{16,18},{18,... | collective-permute-start | bytes 589832 | tf_op jit(solution)/shard_map/ppermute | solution.py:28
  169.6 177.9 %all-gather.19.cloned.1.call-start = ((), (), s32[]{:S(2)}) async-start(), calls=%async_computation.3 | async-start | bytes 2654208 | tf_op jit(solution)/shard_map/all_gather | solution.py:653
  202.1 15.0 %collective-permute-start.40 = (bf16[256,512]{1,0:T(8,128)(2,1)S(1)}, bf16[256,512]{1,0:T(8,128)(2,1)S(1)}, u32[]{:S(2)}, u32[]{:S(2)}) collective-permute-start(bf16[256,512]{1,0:T(8,128)(2,1)S(1)} %pad_maximum_fusion.2.refs_4_.refs_12_.refs_8_.refs_16_), channel_id=1, source_target_pairs={{0,4},{2,6},{4,8},{6,10},{8,12},{10,14},{12,0},{14,2},{16,20},{18,... | collective-permute-start | bytes 786440 | tf_op jit(solution)/shard_map/ppermute | solution.py:28
  203.0 14.2 %collective-permute-start.41 = (bf16[256,512]{1,0:T(8,128)(2,1)S(1)}, bf16[256,512]{1,0:T(8,128)(2,1)S(1)}, u32[]{:S(2)}, u32[]{:S(2)}) collective-permute-start(bf16[256,512]{1,0:T(8,128)(2,1)S(1)} %pad_maximum_fusion.2.refs_4_.refs_12_.refs_8_.refs_16_), channel_id=1, source_target_pairs={{0,8},{2,10},{4,12},{6,14},{8,0},{10,2},{12,4},{14,6},{16,24},{18,... | collective-permute-start | bytes 786440 | tf_op jit(solution)/shard_map/ppermute | solution.py:28
  252.4 95.0 %all-gather.17.cloned.1.call-start = ((), (), s32[]{:S(2)}) async-start(), calls=%async_computation.2 | async-start | bytes 2654208 | tf_op jit(solution)/shard_map/all_gather | solution.py:653
  292.2 182.9 %reduce-scatter.3.cloned.1.call-start = ((), (), s32[]{:S(2)}) async-start(), calls=%async_computation.4 | async-start | bytes 5898240 | tf_op jit(solution)/shard_map/reduce_scatter | solution.py:523
  324.8 171.4 %all-gather.29.cloned.1.call-start = ((), (), s32[]{:S(2)}) async-start(), calls=%async_computation.10 | async-start | bytes 3391488 | tf_op jit(solution)/shard_map/all_gather | solution.py:715
  365.5 14.2 %collective-permute-start.68 = (bf16[256,512]{1,0:T(8,128)(2,1)}, bf16[256,512]{1,0:T(8,128)(2,1)}, u32[]{:S(2)}, u32[]{:S(2)}) collective-permute-start(bf16[256,512]{1,0:T(8,128)(2,1)} %get-tuple-element.125), channel_id=1, source_target_pairs={{0,8},{2,10},{4,12},{6,14},{8,0},{10,2},{12,4},{14,6},{16,24},{18,... | collective-permute-start | bytes 786440 | tf_op jit(solution)/shard_map/ppermute | solution.py:28
  390.5 118.2 %all-gather.27.cloned.1.call-start = ((), (), s32[]{:S(2)}) async-start(), calls=%async_computation.9 | async-start | bytes 1916928 | tf_op jit(solution)/shard_map/all_gather | solution.py:719
  406.5 18.6 %collective-permute-start.75 = (bf16[64,1536]{1,0:T(8,128)(2,1)S(1)}, bf16[64,1536]{1,0:T(8,128)(2,1)S(1)}, u32[]{:S(2)}, u32[]{:S(2)}) collective-permute-start(bf16[64,1536]{1,0:T(8,128)(2,1)S(1)} %convert_element_type.566.refs_6_), channel_id=1, source_target_pairs={{0,8},{2,10},{4,12},{6,14},{8,0},{10,2},{12,4},{14,6},{16,24},{18,... | collective-permute-start | bytes 589832 | tf_op jit(solution)/shard_map/ppermute | solution.py:28
  408.1 18.8 %collective-permute-start.76 = (bf16[64,1536]{1,0:T(8,128)(2,1)S(1)}, bf16[64,1536]{1,0:T(8,128)(2,1)S(1)}, u32[]{:S(2)}, u32[]{:S(2)}) collective-permute-start(bf16[64,1536]{1,0:T(8,128)(2,1)S(1)} %convert_element_type.566.refs_6_), channel_id=1, source_target_pairs={{0,12},{2,14},{4,0},{6,2},{8,4},{10,6},{12,8},{14,10},{16,28},{18,... | collective-permute-start | bytes 589832 | tf_op jit(solution)/shard_map/ppermute | solution.py:28
  409.0 18.0 %collective-permute-start.77 = (bf16[64,1536]{1,0:T(8,128)(2,1)S(1)}, bf16[64,1536]{1,0:T(8,128)(2,1)S(1)}, u32[]{:S(2)}, u32[]{:S(2)}) collective-permute-start(bf16[64,1536]{1,0:T(8,128)(2,1)S(1)} %convert_element_type.566.refs_6_), channel_id=1, source_target_pairs={{0,2},{2,0},{4,6},{6,4},{8,10},{10,8},{12,14},{14,12},{16,18},{18,... | collective-permute-start | bytes 589832 | tf_op jit(solution)/shard_map/ppermute | solution.py:28
  464.2 105.4 %reduce-scatter.5.cloned.1.call-start = ((), (), s32[]{:S(2)}) async-start(), calls=%async_computation.5 | async-start | bytes 5898240 | tf_op jit(solution)/shard_map/reduce_scatter | solution.py:523
  471.1 131.7 %all-gather.31.cloned.1.call-start = ((), (), s32[]{:S(2)}) async-start(), calls=%async_computation.11 | async-start | bytes 2838528 | tf_op jit(solution)/shard_map/all_gather | solution.py:735
  491.9 15.0 %collective-permute-start.88 = (bf16[256,512]{1,0:T(8,128)(2,1)}, bf16[256,512]{1,0:T(8,128)(2,1)S(1)}, u32[]{:S(2)}, u32[]{:S(2)}) collective-permute-start(bf16[256,512]{1,0:T(8,128)(2,1)} %get-tuple-element.122), channel_id=1, source_target_pairs={{0,8},{2,10},{4,12},{6,14},{8,0},{10,2},{12,4},{14,6},{16,24},{18,... | collective-permute-start | bytes 786440 | tf_op jit(solution)/shard_map/ppermute | solution.py:28
  537.4 112.7 %all-gather.33.cloned.1.call-start = ((), (), s32[]{:S(2)}) async-start(), calls=%async_computation.12 | async-start | bytes 4730880 | tf_op jit(solution)/shard_map/all_gather | solution.py:736
  601.3 25.7 %collective-permute-start.114 = (bf16[2304,256]{1,0:T(8,128)(2,1)}, bf16[2304,256]{1,0:T(8,128)(2,1)}, u32[]{:S(2)}, u32[]{:S(2)}) collective-permute-start(bf16[2304,256]{1,0:T(8,128)(2,1)} %broadcast_select_fusion.1), channel_id=1, source_target_pairs={{0,64},{64,0},{1,65},{65,1},{2,66},{66,2},{3,67},{67,3},{4,68},{68... | collective-permute-start | bytes 3538952 | tf_op jit(solution)/shard_map/ppermute | solution.py:32
  603.8 22.5 %collective-permute-start.113 = (bf16[16,1536]{1,0:T(8,128)(2,1)S(1)}, bf16[16,1536]{1,0:T(8,128)(2,1)S(1)}, u32[]{:S(2)}, u32[]{:S(2)}) collective-permute-start(bf16[16,1536]{1,0:T(8,128)(2,1)S(1)} %bitcast.254), channel_id=1, source_target_pairs={{0,1},{1,0},{2,3},{3,2},{4,5},{5,4},{6,7},{7,6},{8,9},{9,8},{10,11... | collective-permute-start | bytes 147464 | tf_op jit(solution)/shard_map/ppermute | solution.py:32
  (242 other events, 2699.1 us)
Sparse Core Ops, SparseCore 0:
  44.9 57.6 all-gather.22
  104.8 54.7 all-gather.20
  169.7 49.4 all-gather.24
  252.6 24.5 all-gather.18
  292.4 26.3 all-gather.16
  324.9 52.8 reduce-scatter.2
  390.6 36.2 all-gather.28
  464.3 27.6 all-gather.26
  495.0 57.4 reduce-scatter.4
  555.2 45.9 all-gather.30
  604.1 45.9 all-gather.32

commit v3 on v2

--- a/solution.py
+++ b/solution.py
@@ -251,18 +251,222 @@
     )(*earlier, *masks, query, grad, lse, *pieces, *pieces)
 
 
+def choose_kernel(layer, section_ref, gate_ref, up_ref, down_ref, sent_gate_ref, sent_ref, out_ref, sems):
+    def copied(pairs):
+        copies = [pltpu.make_async_copy(a, b, sems.at[i]) for i, (a, b) in enumerate(pairs)]
+        for copy in copies:
+            copy.start()
+        for copy in copies:
+            copy.wait()
+
+    gates, ups, downs = out_ref.at[0:2], out_ref.at[2:4], out_ref.at[4:6]
+
+    @pl.when(section_ref[0] == layer)
+    def _():
+        copied([(gate_ref, gates), (up_ref, ups), (down_ref, downs)])
+
+    @pl.when(section_ref[0] != layer)
+    def _():
+        copied([(sent_gate_ref, gates), (sent_ref, out_ref.at[2:6])])
+
+
+def choose(layer, section, parts, *earlier):
+    return pl.pallas_call(
+        ignoring(len(earlier), lambda *refs: choose_kernel(layer, *refs)),
+        in_specs=[ANY] * len(earlier) + [SMEM] + [ANY] * len(parts),
+        out_specs=VMEM,
+        out_shape=shaped(6, 384, 256),
+        scratch_shapes=[pltpu.SemaphoreType.DMA((3,))],
+        compiler_params=params(16),
+        cost_estimate=cost(0, 3 << 20),
+        name="choose",
+    )(*earlier, section, *parts)
+
+
+def side_by_side(parts, axis, *earlier):
+    def kernel(*refs):
+        refs[-1][...] = jnp.concatenate([ref[...] for ref in refs[:-1]], axis=axis)
+
+    shape = list(parts[0].shape)
+    shape[axis] = sum(part.shape[axis] for part in parts)
+    return pl.pallas_call(
+        ignoring(len(earlier), kernel),
+        in_specs=[ANY] * len(earlier) + [VMEM] * len(parts),
+        out_specs=VMEM,
+        out_shape=jax.ShapeDtypeStruct(tuple(shape), parts[0].dtype),
+        compiler_params=params(16),
+        cost_estimate=cost(0, 2 << 20),
+        name="side_by_side",
+    )(*earlier, *parts)
+
+
+def fetched(own, refs, held, sems, where_ref, others):
+    def copies(pairs):
+        return [pltpu.make_async_copy(a, b, sems.at[i]) for i, (a, b) in enumerate(pairs)]
+
+    mine, sent = copies(refs), copies(others)
+    is_own = where_ref[4] == own
+
+    @pl.when(is_own)
+    def _():
+        for copy in mine:
+            copy.start()
+
+    @pl.when(jnp.logical_not(is_own))
+    def _():
+        for copy in sent:
+            copy.start()
+
+    def wait():
+        @pl.when(is_own)
+        def _():
+            for copy in mine:
+                copy.wait()
+
+        @pl.when(jnp.logical_not(is_own))
+        def _():
+            for copy in sent:
+                copy.wait()
+
+    return wait
+
+
+def fetch_qkv(layer, where_ref, q_ref, k_ref, v_ref, sent_ref, held, sems):
+    own = [(q_ref, held.at[:, 0:768]), (k_ref, held.at[:, 768:1024]), (v_ref, held.at[:, 1024:1280])]
+    return fetched(layer, own, held, sems, where_ref, [(sent_ref.at[:, 0:1280], held)])
+
+
+def fetch_out(layer, where_ref, out_ref, sent_ref, held, sems):
+    halves = [
+        (sent_ref.at[h * 768 : (h + 1) * 768, 1280:2048], held.at[:, h * 768 : (h + 1) * 768]) for h in range(2)
+    ]
+    return fetched(layer, [(out_ref, held)], held, sems, where_ref, halves)
+
+
+QKV_HELD = [pltpu.VMEM((1536, 1280), BF), pltpu.SemaphoreType.DMA((3,))]
+OUT_HELD = [pltpu.VMEM((768, 1536), BF), pltpu.SemaphoreType.DMA((2,))]
+
+
+def normed(value, gain):
+    inverse = lax.rsqrt(jnp.mean(value * value, axis=-1, keepdims=True) + EPSILON)
+    return inverse, value * inverse * gain
+
+
+def qkv_kernel(layer, where_ref, hidden_ref, gain_ref, q_ref, k_ref, v_ref, sent_ref, act_ref, out_ref, held, sems):
+    wait = fetch_qkv(layer, where_ref, q_ref, k_ref, v_ref, sent_ref, held, sems)
+    act = normed(hidden_ref[...], gain_ref[...])[1].astype(BF)
+    act_ref[...] = act
+    wait()
+    out_ref[...] = nn(act, held[...]).astype(BF)
+
+
+def qkv_of(layer, where, hidden, gain, weights, sent):
+    return pl.pallas_call(
+        functools.partial(qkv_kernel, layer),
+        in_specs=[SMEM, VMEM, VMEM] + [ANY] * 4,
+        out_specs=[VMEM, VMEM],
+        out_shape=[shaped(64, D), shaped(64, 1280)],
+        scratch_shapes=QKV_HELD,
+        compiler_params=params(40),
+        cost_estimate=cost(64 * 1536 * 1280 * 2, 4 << 20),
+        name="qkv_of",
+    )(where, hidden, gain, *weights, sent)
+
+
+def out_kernel(layer, where_ref, mixed_ref, out_w_ref, sent_ref, out_ref, held, sems):
+    fetch_out(layer, where_ref, out_w_ref, sent_ref, held, sems)()
+    out_ref[...] = nn(mixed_ref[...], held[...]).astype(BF)
+
+
+def out_of(layer, where, mixed, weight, sent):
+    return pl.pallas_call(
+        functools.partial(out_kernel, layer),
+        in_specs=[SMEM, VMEM] + [ANY] * 2,
+        out_specs=VMEM,
+        out_shape=shaped(64, D),
+        scratch_shapes=OUT_HELD,
+        compiler_params=params(40),
+        cost_estimate=cost(64 * 1536 * 768 * 2, 3 << 20),
+        name="out_of",
+    )(where, mixed, weight, sent)
+
+
+def act_back_kernel(layer, where_ref, grad_ref, q_ref, k_ref, v_ref, sent_ref, out_ref, held, sems):
+    fetch_qkv(layer, where_ref, q_ref, k_ref, v_ref, sent_ref, held, sems)()
+    out_ref[...] = nt(grad_ref[...], held[...]).astype(BF)
+
+
+def act_back(layer, where, grad, weights, sent, *earlier):
+    return pl.pallas_call(
+        ignoring(len(earlier), functools.partial(act_back_kernel, layer)),
+        in_specs=[ANY] * len(earlier) + [SMEM, VMEM] + [ANY] * 4,
+        out_specs=VMEM,
+        out_shape=shaped(64, D),
+        scratch_shapes=QKV_HELD,
+        compiler_params=params(40),
+        cost_estimate=cost(64 * 1536 * 1280 * 2, 4 << 20),
+        name="act_back",
+    )(*earlier, where, grad, *weights, sent)
+
+
+def middle_back_kernel(
+    layer, where_ref, low_ref, got_ref, grad_ref, branch_ref, middle_ref, gain_ref, router_ref, routed_ref, out_w_ref, sent_ref,
+    grad_middle_ref, right_ref, mixed_ref, gain_grad_ref, held, sems,
+):
+    wait = fetch_out(layer, where_ref, out_w_ref, sent_ref, held, sems)
+    grad, middle, gain = grad_ref[...], middle_ref[...], gain_ref[...]
+    inverse, second = normed(middle, gain)
+    routed = routed_ref[...] > 0
+    logits = jnp.where(routed, nt(second.astype(BF), router_ref[...]), NEGATIVE)
+    raised = jnp.exp(logits - jnp.max(logits, axis=1, keepdims=True))
+    raised = jnp.where(routed, raised, 0.0)
+    gates = raised / jnp.sum(raised, axis=1, keepdims=True)
+    inner = jnp.sum(grad * branch_ref[...], axis=1, keepdims=True)
+    own = inner * gates
+    high = own.astype(BF)
+    low = (own - high.astype(F32)).astype(BF)
+    total = low_ref[...].astype(F32) + got_ref[...].astype(F32)
+    total = total - nn(high, router_ref[...]) - nn(low, router_ref[...])
+    scaled = total * gain
+    mean = jnp.mean(scaled * middle, axis=-1, keepdims=True)
+    gain_grad_ref[...] = jnp.sum(total * middle * inverse, axis=0, keepdims=True)
+    grad_middle = grad + inverse * scaled - inverse * inverse * inverse * middle * mean
+    grad_middle_ref[...] = grad_middle
+    grad_branch = grad_middle.astype(BF)
+    right_ref[:, 0:1536] = grad_branch
+    inner_high = inner.astype(BF).astype(F32)
+    lane = lax.broadcasted_iota(jnp.int32, (64, 128), 1)
+    lanes = jnp.where(lane == 0, inner_high, jnp.where(lane == 1, inner - inner_high, 0.0))
+    right_ref[:, 1536:1664] = lanes.astype(BF)
+    wait()
+    mixed_ref[...] = nt(grad_branch, held[...]).astype(BF)
+
+
+def middle_back(layer, where, low, got, grad, branch, middle, gain, router, routed, weight, sent):
+    return pl.pallas_call(
+        functools.partial(middle_back_kernel, layer),
+        in_specs=[SMEM] + [VMEM] * 8 + [ANY] * 2,
+        out_specs=[VMEM] * 4,
+        out_shape=[shaped(64, D, dtype=F32), shaped(64, 1664), shaped(64, 768), shaped(1, D, dtype=F32)],
+        scratch_shapes=OUT_HELD,
+        compiler_params=params(40),
+        cost_estimate=cost(64 * 1536 * 768 * 2, 5 << 20),
+        name="middle_back",
+    )(where, low, got, grad, branch, middle, gain, router, routed, weight, sent)
+
+
 def whole(*shape):
     return pl.BlockSpec(shape, lambda j: (0,) * len(shape))
 
 
-def expert_kernel(where_ref, weight_ref, router_ref, routed_ref, *refs):
-    token_refs, (pa_ref, pb_ref, pre_ref, mid_ref, gates_ref, all_ref) = refs[:8], refs[8:]
+def expert_kernel(where_ref, weight_ref, router_ref, *refs):
+    token_refs, routed_refs, (pa_ref, pb_ref, pre_ref, mid_ref, gates_ref, all_ref) = refs[:8], refs[8:16], refs[16:]
     for h, out_ref in enumerate((pa_ref, pb_ref)):
         rows = pl.ds(h * 256, 256)
         tokens = stacked(token_refs[4 * h : 4 * h + 4])
         all_ref[rows] = tokens
         parts = [tokens[:, r * 384 : (r + 1) * 384] for r in range(4)]
-        routed = routed_ref[rows, 0:16].astype(F32) > 0
+        routed = stacked(routed_refs[4 * h : 4 * h + 4])[:, 0:16].astype(F32) > 0
         logits = jnp.where(routed, nt(tokens, router_ref[...]), NEGATIVE)
         raised = jnp.exp(logits - jnp.max(logits, axis=1, keepdims=True))
         raised = jnp.where(routed, raised, 0.0)
@@ -285,31 +489,28 @@
             out_ref[:, r * 384 : (r + 1) * 384] = made.astype(BF)
 
 
-def experts_forward(where, tokens, routed, router, weights):
-    return pl.pallas_call(
-        expert_kernel,
+def experts_forward(where, tokens, given, router, weights, *earlier):
+    routed = pl.BlockSpec((64, 128), lambda j: (0, 12))
+    return pl.pallas_call(
+        ignoring(len(earlier), expert_kernel),
         grid=(1,),
-        in_specs=[SMEM, whole(4, 6, 384, 256), whole(16, D), whole(512, 128)] + [whole(64, D)] * 8,
+        in_specs=[ANY] * len(earlier)
+        + [SMEM, whole(4, 6, 384, 256), whole(16, D)] + [whole(64, D)] * 8 + [routed] * 8,
         out_specs=[whole(256, D)] * 2 + [whole(512, 1024), whole(512, 512), whole(512, 16), whole(512, D)],
         out_shape=[shaped(256, D), shaped(256, D), shaped(512, 1024), shaped(512, 512)]
         + [shaped(512, 16, dtype=F32), shaped(512, D)],
         compiler_params=params(48),
         cost_estimate=cost(512 * 1536 * 1536 * 2, 10 << 20, 512 * 512),
         name="experts_forward",
-    )(where, weights, router, routed, *tokens)
+    )(*earlier, where, weights, router, *tokens, *given)
 
 
 def expert_back_kernel(order_ref, weight_ref, router_ref, pre_ref, gates_ref, *refs):
-    grad_refs, (pa_ref, pb_ref, gpre_ref, gated_ref) = refs[:-4], refs[-4:]
-    if len(grad_refs) > 1:
-        grad_refs, all_ref = grad_refs[:8], refs[8]
+    grad_refs, (all_ref, pa_ref, pb_ref, gpre_ref, gated_ref) = refs[:8], refs[8:]
     for h, out_ref in enumerate((pa_ref, pb_ref)):
         rows = pl.ds(h * 256, 256)
-        if len(grad_refs) > 1:
-            grad_out = stacked(grad_refs[4 * h : 4 * h + 4])
-            all_ref[rows] = grad_out
-        else:
-            grad_out = grad_refs[0][rows]
+        grad_out = stacked(grad_refs[4 * h : 4 * h + 4])
+        all_ref[rows] = grad_out
         parts = [grad_out[:, r * 384 : (r + 1) * 384] for r in range(4)]
         gates = gates_ref[rows]
         expert = lax.broadcasted_iota(jnp.int32, (256, 16), 1) - 2 * order_ref[3]
@@ -341,21 +542,89 @@
 
 
 def experts_backward(where, grads, pre, gates, router, weights, *earlier):
-    pieces = len(grads) > 1
-    outs = pl.pallas_call(
+    return pl.pallas_call(
         ignoring(len(earlier), expert_back_kernel),
         grid=(1,),
         in_specs=[ANY] * len(earlier)
         + [SMEM, whole(4, 6, 384, 256), whole(16, D), whole(512, 1024), whole(512, 16)]
-        + ([whole(64, D)] * 8 if pieces else [whole(512, D)]),
-        out_specs=[whole(512, D)] * pieces + [whole(256, D), whole(256, D), whole(512, 1024), whole(512, 16)],
-        out_shape=[shaped(512, D)] * pieces
-        + [shaped(256, D), shaped(256, D), shaped(512, 1024), shaped(512, 16, dtype=F32)],
+        + [whole(64, D)] * 8,
+        out_specs=[whole(512, D), whole(256, D), whole(256, D), whole(512, 1024), whole(512, 16)],
+        out_shape=[shaped(512, D), shaped(256, D), shaped(256, D), shaped(512, 1024), shaped(512, 16, dtype=F32)],
         compiler_params=params(48),
         cost_estimate=cost(512 * 1536 * 1536 * 2, 10 << 20, 512 * 512),
         name="experts_backward",
     )(*earlier, where, weights, router, pre, gates, *grads)
-    return outs if pieces else [grads[0]] + list(outs)
+
+
+def last_expert_kernel(where_ref, weight_ref, router_ref, *refs):
+    token_refs, given_refs = refs[:8], refs[8:16]
+    pa_ref, pb_ref, mid_ref, gpre_ref, gates_ref, gated_ref, tokens_ref, all_ref = refs[16:]
+    for h, out_ref in enumerate((pa_ref, pb_ref)):
+        rows = pl.ds(h * 256, 256)
+        tokens = stacked(token_refs[4 * h : 4 * h + 4])
+        tokens_ref[rows] = tokens
+        given = stacked(given_refs[4 * h : 4 * h + 4])
+        grad_out = given[:, 0:1536]
+        all_ref[rows] = grad_out
+        parts = [tokens[:, r * 384 : (r + 1) * 384] for r in range(4)]
+        grad_parts = [grad_out[:, r * 384 : (r + 1) * 384] for r in range(4)]
+        routed = given[:, 1536:1552].astype(F32) > 0
+        logits = jnp.where(routed, nt(tokens, router_ref[...]), NEGATIVE)
+        raised = jnp.exp(logits - jnp.max(logits, axis=1, keepdims=True))
+        raised = jnp.where(routed, raised, 0.0)
+        gates = raised / jnp.sum(raised, axis=1, keepdims=True)
+        expert = lax.broadcasted_iota(jnp.int32, (256, 16), 1) - 2 * where_ref[3]
+        gates = jnp.where((expert == 0) | (expert == 1), gates, 0.0)
+        gates_ref[rows] = gates
+        gated = jnp.zeros((256, 16), F32)
+        mids, grads = [], []
+        for e in range(2):
+            gate_pre = sum(nn(parts[r], weight_ref[r, e]) for r in range(4))
+            up_pre = sum(nn(parts[r], weight_ref[r, 2 + e]) for r in range(4))
+            raw = sum(nn(grad_parts[r], weight_ref[r, 4 + e]) for r in range(4))
+            gate = jnp.sum(jnp.where(expert == e, gates, 0.0), axis=1, keepdims=True)
+            sigmoid = jax.nn.sigmoid(gate_pre)
+            activated = gate_pre * sigmoid
+            product = activated * up_pre
+            mid = (product * gate).astype(BF)
+            mid_ref[rows, e * 256 : (e + 1) * 256] = mid
+            mids.append(mid)
+            gated = jnp.where(expert == e, gates * jnp.sum(product * raw, axis=1, keepdims=True), gated)
+            raw = raw * gate
+            grad_gate = (raw * up_pre * sigmoid * (1.0 + gate_pre * (1.0 - sigmoid))).astype(BF)
+            grad_up = (raw * activated).astype(BF)
+            gpre_ref[rows, e * 256 : (e + 1) * 256] = grad_gate
+            gpre_ref[rows, (2 + e) * 256 : (3 + e) * 256] = grad_up
+            grads.append((grad_gate, grad_up))
+        gated_ref[rows] = gated
+        high = gated.astype(BF)
+        low = (gated - high.astype(F32)).astype(BF)
+        for r in range(4):
+            lanes = slice(r * 384, (r + 1) * 384)
+            made = (nt(mids[0], weight_ref[r, 4]) + nt(mids[1], weight_ref[r, 5])).astype(BF)
+            back = nn(high, router_ref[:, lanes]) + nn(low, router_ref[:, lanes])
+            for e in range(2):
+                back = back + nt(grads[e][0], weight_ref[r, e]) + nt(grads[e][1], weight_ref[r, 2 + e])
+            back = back.astype(BF)
+            for j in range(4):
+                out_ref[j * 128 : j * 128 + 64, lanes] = made[j * 64 : (j + 1) * 64]
+                out_ref[j * 128 + 64 : (j + 1) * 128, lanes] = back[j * 64 : (j + 1) * 64]
+
+
+def last_experts(where, tokens, given, router, weights, *earlier):
+    return pl.pallas_call(
+        ignoring(len(earlier), last_expert_kernel),
+        grid=(1,),
+        in_specs=[ANY] * len(earlier)
+        + [SMEM, whole(4, 6, 384, 256), whole(16, D)] + [whole(64, D)] * 8 + [whole(64, 1664)] * 8,
+        out_specs=[whole(512, D)] * 2
+        + [whole(512, 512), whole(512, 1024), whole(512, 16), whole(512, 16), whole(512, D), whole(512, D)],
+        out_shape=[shaped(512, D), shaped(512, D), shaped(512, 512), shaped(512, 1024)]
+        + [shaped(512, 16, dtype=F32), shaped(512, 16, dtype=F32), shaped(512, D), shaped(512, D)],
+        compiler_params=params(48),
+        cost_estimate=cost(512 * 1536 * 1536 * 4, 16 << 20, 512 * 512),
+        name="last_experts",
+    )(*earlier, where, weights, router, *tokens, *given)
 
 
 def expert_weight_kernel(gpre_ref, mid_ref, tokens_ref, grads_ref, out_ref):
@@ -387,117 +656,92 @@
     return ((where_ref[1] - (b & 3)) & 3) * 2 + (where_ref[2] if b < 4 else 1 - where_ref[2])
 
 
-def out_slice_kernel(where_ref, left_ref, right_ref, gated_ref, gates_ref, gains_ref, tokens_ref, out_ref):
+def dense_slice_kernel(pieces, where_ref, left_ref, gated_ref, gates_ref, gains_ref, tokens_ref, right_ref, *refs):
     me = where_ref[3]
-    pick = chosen(768, 96, me)
-    left = jnp.concatenate([nn(left_ref[b, :, 1536:2304], pick).astype(BF) for b in range(8)], axis=0)
-    right = jnp.concatenate([right_ref[b, :, 0:1536] for b in range(8)], axis=0)
-    rows = tn(left, right)
+    out_ref = refs[8 if pieces else 0]
+    if pieces:
+        right = refs[9]
+        for b in range(8):
+            right[pl.ds(pl.multiple_of(source(where_ref, b) * 64, 64), 64), :] = refs[b][...]
+        right = right[...]
+    else:
+        right = right_ref[:, 1664:2944]
+    left = nn(left_ref[:, 0:1536], chosen(1536, 192, me)).astype(BF)
+    rows = tn(left, right).astype(BF)
+    left = nn(left_ref[:, 1536:2304], chosen(768, 96, me)).astype(BF)
     lane = lax.broadcasted_iota(jnp.int32, (64, 16), 1)
     logits = []
     for b in range(8):
         block = slice(b * 64, (b + 1) * 64)
-        lanes = right_ref[source(where_ref, b), :, 1536:1664].astype(F32)
+        start = pl.multiple_of(source(where_ref, b) * 64, 64)
+        lanes = right_ref[pl.ds(start, 64), 1536:1664].astype(F32)
         inner = lanes[:, 0:1] + lanes[:, 1:2]
         grad = gated_ref[block] - 0.5 * gates_ref[block] * inner
         one = [jnp.sum(jnp.where(lane == 2 * me + e, grad, 0.0), axis=1, keepdims=True) for e in range(2)]
         logits.append(jnp.where(lane == 0, one[0], jnp.where(lane == 1, one[1], 0.0)).astype(BF))
     extra = tn(jnp.concatenate(logits, axis=0), tokens_ref[...])
     row = lax.broadcasted_iota(jnp.int32, (16, D), 0)
-    gains = gains_ref[...]
-    extra = jnp.where(row == 2, gains[0:1], jnp.where(row == 3, gains[1:2], extra))
+    extra = jnp.where(row == 2, gains_ref[0:1], jnp.where(row == 3, gains_ref[1:2], extra))
+    wide = jnp.concatenate([tn(left, right_ref[:, 0:1536]), extra], axis=0).astype(BF)
     for r in range(4):
-        to = (where_ref[0] - r) & 3
-        out_ref[to, 0:96] = rows[:, r * 384 : (r + 1) * 384].astype(BF)
-        out_ref[to, 96:112] = extra[:, r * 384 : (r + 1) * 384].astype(BF)
-
-
-def out_slice(where, left, right, gated, gates, gains, tokens, *earlier):
-    return pl.pallas_call(
-        ignoring(len(earlier), out_slice_kernel),
+        to = (where_ref[0] - r) & 3 if pieces else r
+        for c in range(10):
+            out_ref[to, c * 48 : (c + 1) * 48] = rows[r * 48 : (r + 1) * 48, c * 128 : (c + 1) * 128]
+        for c in range(3):
+            lanes = slice(r * 384 + c * 128, r * 384 + (c + 1) * 128)
+            out_ref[to, 480 + c * 112 : 480 + (c + 1) * 112] = wide[:, lanes]
+
+
+def dense_slice(layer, where, left, gated, gates, gains, tokens, right, pieces, *earlier):
+    return pl.pallas_call(
+        ignoring(len(earlier), functools.partial(dense_slice_kernel, len(pieces) > 0)),
         grid=(1,),
         in_specs=[ANY] * len(earlier)
-        + [SMEM, whole(8, 64, 2304), whole(8, 64, 1664), whole(512, 16), whole(512, 16), whole(2, D), whole(512, D)],
-        out_specs=whole(4, 112, 384),
-        out_shape=shaped(4, 112, 384),
+        + [SMEM, pl.BlockSpec((512, 2304), lambda j: (0, layer)), whole(512, 16), whole(512, 16), whole(2, D)]
+        + [whole(512, D), whole(*right.shape)]
+        + [whole(64, 1280)] * len(pieces),
+        out_specs=whole(4, 816, 128),
+        out_shape=shaped(4, 816, 128),
+        scratch_shapes=[pltpu.VMEM((512, 1280), BF)] if pieces else [],
         compiler_params=params(40),
-        cost_estimate=cost(512 * 1536 * 256, 6 << 20),
-        name="out_slice",
-    )(*earlier, where, left, right, gated, gates, gains, tokens)
-
-
-def qkv_slice_kernel(relative, where_ref, left_ref, gain_ref, *refs):
-    out_ref = refs[-1]
-    me = where_ref[3]
-    pick = chosen(1536, 192, me)
-    if relative:
-        right = stacked(refs[:8])
-        order = [source(where_ref, b) for b in range(8)]
-    else:
-        right = jnp.concatenate([refs[0][b, :, 1664:2944] for b in range(8)], axis=0)
-        order = list(range(8))
-    left = jnp.concatenate([nn(left_ref[b, :, 0:1536], pick).astype(BF) for b in order], axis=0)
-    rows = tn(left, right).astype(BF)
-    row = lax.broadcasted_iota(jnp.int32, (8, 384), 0)
-    for r in range(4):
-        to = (where_ref[0] - r) & 3
-        out_ref[to, 0:48] = rows[r * 48 : (r + 1) * 48]
-        out_ref[to, 48:56, 0:384] = jnp.where(row == 0, gain_ref[:, r * 384 : (r + 1) * 384], 0.0).astype(BF)
-        out_ref[to, 48:56, 384:1280] = jnp.zeros((8, 896), BF)
-
-
-def qkv_slice(where, left, gain, rights, *earlier):
-    relative = len(rights) == 8
-    specs = [whole(64, 1280)] * 8 if relative else [whole(8, 64, 2944)]
-    return pl.pallas_call(
-        ignoring(len(earlier), functools.partial(qkv_slice_kernel, relative)),
-        grid=(1,),
-        in_specs=[ANY] * len(earlier) + [SMEM, whole(8, 64, 2304), whole(1, D)] + specs,
-        out_specs=whole(4, 56, 1280),
-        out_shape=shaped(4, 56, 1280),
-        compiler_params=params(40),
-        cost_estimate=cost(512 * 1536 * 512, 6 << 20),
-        name="qkv_slice",
-    )(*earlier, where, left, gain, *rights)
-
-
-def qkv_rows_kernel(in_ref, q_ref, k_ref, v_ref):
+        cost_estimate=cost(512 * 1536 * 1024 * 2, 8 << 20),
+        name="dense_slice",
+    )(*earlier, where, left, gated, gates, gains, tokens, right, *pieces)
+
+
+def dense_rows_kernel(in_ref, q_ref, k_ref, v_ref, out_ref, router_ref, gains_ref, held_ref):
+    j = pl.program_id(0)
     for x in range(4):
         rows = slice(x * 48, (x + 1) * 48)
-        q_ref[rows] = in_ref[x, 0, 0:48, 0:768].astype(F32)
-        k_ref[rows] = in_ref[x, 0, 0:48, 768:1024].astype(F32)
-        v_ref[rows] = in_ref[x, 0, 0:48, 1024:1280].astype(F32)
-
-
-def qkv_rows(everything):
-    rows = lambda width: pl.BlockSpec((192, width), lambda j: (j, 0))
-    return pl.pallas_call(
-        qkv_rows_kernel,
+        for c in range(10):
+            to_ref, lane = (q_ref, c) if c < 6 else (k_ref, c - 6) if c < 8 else (v_ref, c - 8)
+            to_ref[rows, lane * 128 : (lane + 1) * 128] = in_ref[x, 0, c * 48 : (c + 1) * 48].astype(F32)
+        for c in range(3):
+            lanes = slice(x * 384 + c * 128, x * 384 + (c + 1) * 128)
+            out_ref[:, lanes] = in_ref[x, 0, 480 + c * 112 : 576 + c * 112].astype(F32)
+            held_ref[j, :, lanes] = in_ref[x, 0, 576 + c * 112 : 592 + c * 112].astype(F32)
+
+    @pl.when(j == 7)
+    def _():
+        held = held_ref[...]
+        router = jnp.concatenate([held[i, 0:2] for i in range(8)], axis=0)
+        router_ref[...] = router.T
+        gains_ref[...] = jnp.sum(held, axis=0)
+
+
+def dense_rows(everything):
+    rows = lambda count, width: pl.BlockSpec((count, width), lambda j: (j, 0))
+    return pl.pallas_call(
+        dense_rows_kernel,
         grid=(8,),
-        in_specs=[pl.BlockSpec((4, 1, 56, 1280), lambda j: (0, j, 0, 0))],
-        out_specs=[rows(768), rows(256), rows(256)],
-        out_shape=[shaped(D, 768, dtype=F32), shaped(D, 256, dtype=F32), shaped(D, 256, dtype=F32)],
-        compiler_params=params(32),
-        cost_estimate=cost(0, 12 << 20),
-        name="qkv_rows",
-    )(everything)
-
-
-def out_rows_kernel(in_ref, out_ref):
-    for x in range(4):
-        out_ref[:, x * 384 : (x + 1) * 384] = in_ref[x, 0, 0:96].astype(F32)
-
-
-def out_rows(everything):
-    return pl.pallas_call(
-        out_rows_kernel,
-        grid=(8,),
-        in_specs=[pl.BlockSpec((4, 1, 112, 384), lambda j: (0, j, 0, 0))],
-        out_specs=pl.BlockSpec((96, D), lambda j: (j, 0)),
-        out_shape=shaped(768, D, dtype=F32),
-        compiler_params=params(32),
-        cost_estimate=cost(0, 7 << 20),
-        name="out_rows",
+        in_specs=[pl.BlockSpec((4, 1, 816, 128), lambda j: (0, j, 0, 0))],
+        out_specs=[rows(192, 768), rows(192, 256), rows(192, 256), rows(96, D), whole(D, 16), whole(16, D)],
+        out_shape=[shaped(D, 768, dtype=F32), shaped(D, 256, dtype=F32), shaped(D, 256, dtype=F32)]
+        + [shaped(768, D, dtype=F32), shaped(D, 16, dtype=F32), shaped(16, D, dtype=F32)],
+        scratch_shapes=[pltpu.VMEM((8, 16, D), F32)],
+        compiler_params=params(40),
+        cost_estimate=cost(0, 20 << 20),
+        name="dense_rows",
     )(everything)
 
 
@@ -533,12 +777,15 @@
 
 
 def ordered(value):
-    probe = value[(0,) * value.ndim]
+    probe = value[(-1,) * value.ndim]
     return probe == probe
 
 
-def behind(value, earlier):
-    return jnp.where(ordered(earlier), value, jnp.zeros_like(value))
+def behind(value, *earlier):
+    known = ordered(earlier[0])
+    for other in earlier[1:]:
+        known = known & ordered(other)
+    return jnp.where(known, value, jnp.zeros_like(value))
 
 
 def per_device(
@@ -570,25 +817,29 @@
     def pick(pair):
         return lax.dynamic_index_in_dim(pair, section, 0, False)
 
-    qkv_own = jnp.concatenate([w_query[0], w_key[0], w_value[0]], axis=1)
-    act_both = norm_apply(inputs.astype(F32), norm_first[0]).astype(BF)
-    qkv_both = dot(act_both.reshape(2 * rows, D), qkv_own).astype(BF)
+    weights_in = (w_query[0], w_key[0], w_value[0])
+    dense = jnp.concatenate(
+        [lax.dynamic_slice_in_dim(w, place * 48, 48, 0) for w in weights_in]
+        + [lax.dynamic_slice(w_out[0], (place % 16 * 48, place // 16 * 768), (48, 768))],
+        axis=1,
+    )
+    dense = swapped(dense, "section")
+
+    act_both = norm_apply(inputs.astype(F32), norm_first[0]).astype(BF).reshape(2 * rows, D)
+    qkv_both = jnp.concatenate([dot(act_both, w).astype(BF) for w in weights_in], axis=1)
     qkv_sent = lax.ppermute(qkv_both[rows:], "section", [(0, 1)])
     qkv_first = jnp.where(first, qkv_both[:rows], qkv_sent)
+    dense_all = lax.all_gather(behind(dense, qkv_both), "dp", axis=0).reshape(D, 2048)
 
     pack = jnp.concatenate([norm_first, norm_second, w_router[0].T.astype(F32)], axis=0)
     packs = in_order(pack, swapped(pack, "section"))
     routers = [p[2:].astype(BF) for p in packs]
-    experts = jnp.concatenate([w_gate[0], w_up[0], jnp.swapaxes(w_down[0], 1, 2)], axis=0)
-    experts_other = swapped(experts, "section")
+    turned_down = jnp.swapaxes(w_down[0], 1, 2)
+    sent_gate = swapped(w_gate[0], "section")
+    sent_rest = swapped(side_by_side([w_up[0], turned_down], 0, qkv_sent), "section")
+    halves = (w_gate[0], w_up[0], turned_down, sent_gate, sent_rest)
     expert_weights = [None, None]
-    dense = jnp.concatenate(
-        [lax.dynamic_slice_in_dim(qkv_own, place * 48, 48, 0)[:, i * 256 : (i + 1) * 256] for i in range(5)]
-        + [lax.dynamic_slice_in_dim(w_out[0], place * 24, 24, 0)[:, i * 256 : (i + 1) * 256] for i in range(6)],
-        axis=0,
-    )
-    dense = swapped(dense, "section")
-    where = jnp.stack([here_x, here_y, here_c, me]).astype(jnp.int32)
+    where = jnp.stack([here_x, here_y, here_c, me, section]).astype(jnp.int32)
 
     labels = pick(segments)
     query_labels = lax.dynamic_slice_in_dim(labels, place * rows, rows, 0)
@@ -600,26 +851,22 @@
     routed_own = jnp.sum((own_routes[:, :, None] == expert_ids).astype(F32), axis=1)
     given = pick(cotangent)
     sent = jnp.concatenate([given, jnp.pad(routed_own.astype(BF), ((0, 0), (0, 128 - EXPERTS)))], axis=1)
-    got = group_pieces(sent)
-    given_all = jnp.concatenate(got, axis=0)
-    routed = jnp.concatenate([piece[:, D:] for piece in got], axis=0)
+    given_all = group_pieces(sent)
 
     hidden = pick(inputs).astype(F32)
     saved = []
-    outs_w = qkvs_w = None
     for layer in range(2):
-        gain_one, gain_two = packs[layer][0], packs[layer][1]
-        activation = norm_apply(hidden, gain_one).astype(BF)
-        qkv = qkv_first if layer == 0 else dot(activation, qkvs_w[1]).astype(BF)
+        gain_one, gain_two = packs[layer][0:1], packs[layer][1:2]
+        if layer == 0:
+            activation, qkv = norm_apply(hidden, gain_one).astype(BF), qkv_first
+        else:
+            activation, qkv = qkv_of(1, where, hidden, gain_one, weights_in, dense_all)
         query, pair = qkv[:, :768], qkv[:, 768:]
-        slab = along_x(pair)
-        if layer == 0:
-            experts_first = jnp.where(first & ordered(slab), experts, experts_other)
-            expert_weights[0] = replica_gather(experts_first)
-            slab = behind(slab, experts_first)
+        around = [moved(pair, j, 0, 0) for j in (1, 2, 3)]
+        slab = jnp.concatenate([pair] + around, axis=0)
         near = [slab] + [moved(slab, 0, j, 0) for j in (1, 2, 3)]
         pieces = near + [moved(piece, 0, 0, 1) for piece in near]
-        mixed, log_total = attend_forward(masks, query, pieces, *([] if layer == 0 else [saved[0][-2]]))
+        mixed, log_total = attend_forward(masks, query, pieces)
         if layer == 0:
             mixed_sent = lax.ppermute(mixed, "section", [(1, 0)])
             partial = dot(jnp.concatenate([mixed, mixed_sent], axis=0), w_out[0]).astype(BF)
@@ -627,33 +874,42 @@
             straight = lax.ppermute(partial[rows:], both_axes, [(0, 2), (1, 3)])
             across = lax.ppermute(partial[rows:], both_axes, [(0, 3), (1, 2)])
             turned = lax.ppermute(partial[:rows], both_axes, [(0, 1), (1, 0)])
+            experts_first = choose(0, section[None].astype(jnp.int32), halves, dense_all, mixed)
+            expert_weights[0] = replica_gather(experts_first)
             middle = hidden + (
                 jnp.where(first, partial[:rows], straight).astype(F32) + jnp.where(first, turned, across).astype(F32)
             )
-            dense_all = lax.all_gather(behind(dense, pieces[3]), "dp", axis=0)
-            other_qkv = jnp.swapaxes(dense_all[:, :240].reshape(32, 5, 48, 256), 1, 2).reshape(D, 1280)
-            other_out = jnp.swapaxes(dense_all[:, 240:].reshape(32, 6, 24, 256), 1, 2).reshape(768, D)
-            qkvs_w = in_order(qkv_own, other_qkv)
-            outs_w = in_order(w_out[0], other_out)
-            experts_second = jnp.where(first & ordered(mixed), experts_other, experts)
-            expert_weights[1] = replica_gather(experts_second)
         else:
-            middle = hidden + tensor_sum(dot(mixed, outs_w[layer]))
+            partial = out_of(1, where, mixed, w_out[0], dense_all)
+            middle = hidden + (partial.astype(F32) + swapped(partial, "tensor").astype(F32))
         second = norm_apply(middle, gain_two).astype(BF)
         tokens = group_pieces(second)
-        made_near, made_far, pre, mid, gates, tokens = experts_forward(
-            where, tokens, routed, routers[layer], expert_weights[layer]
-        )
-        made = group_sum(made_near, made_far).reshape(rows, D).astype(BF)
         if layer == 0:
-            made = behind(made, qkvs_w[1])
-        branch = tensor_sum(made)
+            experts_second = choose(1, section[None].astype(jnp.int32), halves, second)
+            expert_weights[1] = replica_gather(experts_second)
+        cut = (activation, mixed)
+        if layer == 0:
+            made_near, made_far, pre, mid, gates, tokens = experts_forward(
+                where, tokens, given_all, routers[0], expert_weights[0], experts_second
+            )
+            made = group_sum(made_near, made_far).reshape(rows, D).astype(BF)
+            branch = tensor_sum(made)
+            rest = (mid, gates, pre)
+        else:
+            near, far, mid, grad_pre, gates, gated, tokens, grad_all = last_experts(
+                where, tokens, given_all, routers[1], expert_weights[1]
+            )
+            both = (near.astype(F32) + moved(far, 0, 0, 1).astype(F32)).astype(BF)
+            low = back_y(both).reshape(2 * rows, D).astype(BF)
+            lefts = side_by_side([*saved[0][8], *cut], 1, low)
+            weight_grads = expert_weight_grads(tokens, grad_all, grad_pre, mid, lefts)
+            lefts = lax.all_gather(lefts, "dp", axis=0, axis_index_groups=Y_GROUPS).reshape(8 * rows, 4608)
+            got = behind(swapped(low, "tensor"), weight_grads)
+            branch = low[:rows].astype(F32) + got[:rows].astype(F32)
+            low, got = low[rows:], got[rows:]
+            rest = (mid, gates, gated)
         result = middle + branch
-        cut = behind(jnp.concatenate([activation, mixed], axis=1), result)
-        lefts = lax.all_gather(cut, "dp", axis=0, axis_index_groups=Y_GROUPS)
-        saved.append(
-            (hidden, query, pieces, log_total, middle, second, tokens, pre, mid, gates, branch, lefts, cut, result)
-        )
+        saved.append((hidden, query, pieces, log_total, middle, second, tokens, branch, cut, result, rest))
         hidden = result
 
     def own_of(a, b):
@@ -667,90 +923,83 @@
 
     grad_output = given.astype(F32)
     grads = []
-    earlier = [saved[1][-2]]
     for layer in (1, 0):
-        hidden, query, pieces, log_total, middle, second, tokens, pre, mid, gates, branch, lefts, _, _ = saved[layer]
-        gain_one, gain_two = packs[layer][0], packs[layer][1]
+        hidden, query, pieces, log_total, middle, second, tokens, branch, _, _, rest = saved[layer]
+        gain_one, gain_two = packs[layer][0:1], packs[layer][1:2]
         router = routers[layer]
-        grad_pieces = [given_all] if layer == 1 else group_pieces(grad_output.astype(BF))
-        grad_all, back_near, back_far, grad_pre, gated = experts_backward(
-            where, grad_pieces, pre, gates, router, expert_weights[layer], *earlier
+        mid, gates, rest = rest
+        if layer == 1:
+            gated = rest
+        else:
+            grad_all, back_near, back_far, grad_pre, gated = experts_backward(
+                where, group_pieces(grad_output.astype(BF)), rest, gates, router, expert_weights[0], *earlier
+            )
+            both = (back_near.astype(F32) + moved(back_far, 0, 0, 1).astype(F32)).astype(BF)
+            weight_grads = expert_weight_grads(tokens, grad_all, grad_pre, mid, both)
+            low = behind(back_y(both), weight_grads).reshape(rows, D).astype(BF)
+            got = swapped(low, "tensor")
+        expert_part = replica_scatter(weight_grads)
+        grad_middle, right, grad_mixed, gain_two_grad = middle_back(
+            layer, where, low, got, grad_output, branch, middle, gain_two, router, routed_own, w_out[0], dense_all
         )
+        grad_query, back_near, back_far = attend_backward(masks, query, grad_mixed, log_total, pieces)
         both = (back_near.astype(F32) + moved(back_far, 0, 0, 1).astype(F32)).astype(BF)
-        weight_grads = expert_weight_grads(tokens, grad_all, grad_pre, mid, both)
-        expert_part = replica_scatter(weight_grads)
-        grad_second = tensor_sum(back_y(both).reshape(rows, D))
-        inner = jnp.sum(grad_output * branch, axis=1, keepdims=True)
-        own_gates = gates_of(second, router.T, routed_own)
-        grad_second = grad_second - dot(inner * own_gates, router.astype(F32))
-        grad_from_norm, gain_two_grad = norm_back(middle, gain_two, grad_second)
-        grad_middle = grad_output + grad_from_norm
-        grad_branch = grad_middle.astype(BF)
-        inner_high = inner.astype(BF)
-        inner_low = (inner - inner_high.astype(F32)).astype(BF)
-        lanes = jnp.concatenate([inner_high, inner_low, jnp.zeros((rows, 126), BF)], axis=1)
-        right = jnp.concatenate([grad_branch, lanes], axis=1)
-        grad_mixed = against(grad_branch, outs_w[layer]).astype(BF)
-        if layer == 1:
-            earlier = [weight_grads, lefts, saved[0][-3]]
-        else:
-            earlier = [weight_grads, right, grads[0][3]]
-        grad_query, back_near, back_far = attend_backward(masks, query, grad_mixed, log_total, pieces, *earlier)
-        both = (back_near.astype(F32) + moved(back_far, 0, 0, 1).astype(F32)).astype(BF)
+        half = back_y(both)
         if layer == 0:
-            late = grads[0]
-            out_blocks = [out_slice(where, *late[2], both)]
-            late_qkv = qkv_slice(where, late[2][0], jnp.zeros((1, D), F32), [late[2][1]], both)
-            late_qkv = back_x(late_qkv.reshape(224, 1280)).reshape(56, 1280)
-        half = back_y(both)
+            late = dense_slice(1, *grads[0][1], [], both)
+            half = behind(half, late)
         grad_pair = back_x(half.astype(BF)).reshape(rows, 512).astype(BF)
         grad_qkv = jnp.concatenate([grad_query, grad_pair], axis=1)
-        grad_activation = tensor_sum(against(grad_qkv, qkvs_w[layer]))
+        partial = act_back(layer, where, grad_qkv, weights_in, dense_all, lefts if layer == 1 else expert_part)
+        grad_activation = partial.astype(F32) + swapped(partial, "tensor").astype(F32)
         grad_from_first, gain_one_grad = norm_back(hidden, gain_one, grad_activation)
         grad_input = grad_middle + grad_from_first
+        gains = jnp.concatenate([gain_two_grad, gain_one_grad[None]], axis=0)
         if layer == 1:
-            gains = jnp.stack([gain_two_grad, gain_one_grad])
             right = jnp.concatenate([right, grad_qkv], axis=1)
-            earlier = [right]
-            right = lax.all_gather(right, "dp", axis=0, axis_index_groups=Y_GROUPS)
-            grads.append((grad_input, None, (lefts, right, gated, gates, gains, tokens), expert_part))
+            earlier = [right, expert_part]
+            right = lax.all_gather(right, "dp", axis=0, axis_index_groups=Y_GROUPS).reshape(8 * rows, 2944)
+            grads.append((grad_input, (where, lefts, gated, gates, gains, tokens, right), expert_part))
         else:
-            gains = jnp.stack([gain_two_grad, jnp.zeros_like(gain_two_grad)])
-            right = lax.all_gather(right, "dp", axis=0, axis_index_groups=Y_GROUPS)
-            out_blocks = [out_slice(where, lefts, right, gated, gates, gains, tokens, half)] + out_blocks
-            out_blocks = over_sections(*out_blocks).astype(BF)
-            out_sum = back_x(out_blocks.reshape(448, 384)).reshape(112, 384).astype(BF)
-            qkv_blocks = qkv_slice(where, lefts, gain_one_grad[None], group_pieces(grad_qkv), out_sum, expert_part)
-            qkv_part = back_x(qkv_blocks.reshape(224, 1280)).reshape(56, 1280)
-            grads.append((grad_input, qkv_part, None, expert_part))
+            late = replica_scatter(late)
+            right = lax.all_gather(right, "dp", axis=0, axis_index_groups=Y_GROUPS).reshape(8 * rows, 1664)
+            blocks = dense_slice(0, where, lefts, gated, gates, gains, tokens, right, group_pieces(grad_qkv))
+            grads.append((grad_input, back_x(blocks.reshape(4 * 816, 128)).reshape(816, 128), expert_part))
         grad_output = grad_input
     grads = grads[::-1]
 
     def by_batch(own, other):
         return jnp.stack([jnp.where(first, own, other), jnp.where(first, other, own)])[None]
 
-    results = by_batch(own_of(saved[0][-1], saved[1][-1]), from_other(saved[0][-1], saved[1][-1]))
+    results = by_batch(own_of(saved[0][9], saved[1][9]), from_other(saved[0][9], saved[1][9]))
     input_grads = by_batch(own_of(grads[0][0], grads[1][0]), from_other(grads[0][0], grads[1][0]))
-    qkv_sum = over_sections(grads[0][1], late_qkv).astype(BF)
-    out_all = lax.all_gather(out_sum, "dp", axis=0).reshape(4, 8, 112, 384)
-    qkv_all = lax.all_gather(qkv_sum, "dp", axis=0).reshape(4, 8, 56, 1280)
-    query_sum, key_sum, value_sum = qkv_rows(qkv_all)
-    out_full = out_rows(out_all)
-    router_sum = jnp.transpose(out_all[:, :, 96:98], (1, 2, 0, 3)).reshape(EXPERTS, D)
-    router_sum = tensor_sum(router_sum)
-    gain_two_sum = jnp.sum(out_all[:, :, 98].astype(F32), axis=1).reshape(1, D)
-    gain_one_sum = jnp.sum(out_all[:, :, 99].astype(F32) + qkv_all[:, :, 48, :384].astype(F32), axis=1).reshape(1, D)
-    expert_sum = over_sections(grads[0][3], grads[1][3]).reshape(3, 2, 384, 256)
+    first_part, late = grads[0][1], late.astype(F32)
+
+    def extras(block):
+        return block.reshape(-1, 128)[480:].reshape(3, 112, 128)[:, 96:98].reshape(6, 128)
+
+    straight = swapped(jnp.concatenate([extras(first_part), extras(late)], axis=0).astype(BF), "tensor").astype(F32)
+    across = lax.ppermute(
+        own_of(extras(late), extras(first_part)).astype(BF), ("section", "tensor"), [(0, 3), (1, 2), (2, 1), (3, 0)]
+    ).astype(F32)
+    block = over_sections(first_part, late)
+    more = own_of(straight[:6], straight[6:]) + across
+    wide = block[480:].reshape(3, 112, 128)
+    wide = wide + jnp.pad(more.reshape(3, 2, 128), ((0, 0), (96, 14), (0, 0)))
+    block = jnp.concatenate([block[:480], wide.reshape(336, 128)], axis=0).astype(BF)
+    everything = lax.all_gather(block, "dp", axis=0).reshape(4, 8, 816, 128)
+    query_sum, key_sum, value_sum, out_full, router_sum, gains = dense_rows(everything)
+    expert_sum = over_sections(grads[0][2], grads[1][2]).reshape(3, 2, 384, 256)
     return (
         results,
         input_grads,
-        gain_one_sum,
+        gains[3:4],
         query_sum[None],
         key_sum[None],
         value_sum[None],
         out_full[None],
-        gain_two_sum,
-        router_sum.T[None],
+        gains[2:3],
+        router_sum[None],
         expert_sum[0][None],
         expert_sum[1][None],
         jnp.swapaxes(expert_sum[2], 1, 2)[None],

time: 678 us -> 621 us (0.916)
  starting transfers between devices: 182 us -> 147 us
  local copies, waits for them, and re-layouts: 65.3 us -> 36.3 us
  Pallas kernels: 109 us -> 132 us
  waiting for transfers between devices: 212 us -> 231 us
  matrix products: 18.6 us -> 2.63 us
  other arithmetic: 53.8 us -> 39.4 us
    pallas_call x8 -> x15, Pallas kernels: 49.8 us -> 81.3 us  [the longest x1 13.4 us: last_experts(): pl.pallas_call(ignoring(len(earlier), last_expert_kernel), grid=(1,), in_...]
    ppermute x94 -> x84, waiting for transfers between devices: 99.5 us -> 131 us  [moved(): return lax.ppermute(value, 'dp', route)]
    ppermute x1, waiting for transfers between devices: 21.9 us -> 2.23 us  [per_device(): qkv_sent = lax.ppermute(qkv_both[rows:], 'section', [(0, 1)])]
    ppermute x16 -> x15, starting transfers between devices: 36.3 us -> 17.5 us  [swapped(): return lax.ppermute(value, axis, [(0, 1), (1, 0)])]
    unnamed x324 -> x212, local copies, waits for them, and re-layouts: 31.8 us -> 14.9 us
    ppermute x94 -> x84, starting transfers between devices: 134 us -> 119 us  [moved(): return lax.ppermute(value, 'dp', route)]
    pallas_call x2 -> x1, Pallas kernels: 18.2 us -> 9 us  [experts_backward(): pl.pallas_call(ignoring(len(earlier), expert_back_kernel), grid=(1,), in_...]
    dot_general x4 -> x0, matrix products: 8.74 us -> none  [against(): lax.dot_general(left, right, (((1,), (1,)), ((), ())), preferred_element_...]
  transfers between devices with their start and end apart: 126 -> 115, of which waited for: 57 -> 56; matrix products, arithmetic and copies ran while one was open for 18% -> 8% of each run, Pallas kernels for 15% -> 17%
where the time goes in v3:
time: 621 us; the launch traced here: 610 us
  waiting for transfers between devices  231 us (37%)
  starting transfers between devices  147 us (24%)
  Pallas kernels  132 us (21%)
  other arithmetic  39.4 us (6%)
  local copies, waits for them, and re-layouts  36.3 us (6%)
  between operations  21.5 us (3%)
    ppermute x84, waiting for transfers between devices, moved(): return lax.ppermute(value, 'dp', route)  131 us
    ppermute x84, starting transfers between devices, moved(): return lax.ppermute(value, 'dp', route)  119 us
    ppermute x15, waiting for transfers between devices, swapped(): return lax.ppermute(value, axis, [(0, 1), (1, 0)])  67.2 us
    ppermute x15, starting transfers between devices, swapped(): return lax.ppermute(value, axis, [(0, 1), (1, 0)])  17.5 us
    all_gather x1, waiting for transfers between devices, per_device(): everything = lax.all_gather(block, 'dp', axis=0).reshape(4, 8, 816, 128)  17.2 us
    pallas_call x2, Pallas kernels, attend_backward(): pl.pallas_call(ignoring(len(earlier), attend_back_kernel), grid=(2,), in_...  16.5 us
    unnamed x212, local copies, waits for them, and re-layouts  14.9 us
    pallas_call x2, Pallas kernels, expert_weight_grads(): pl.pallas_call(ignoring(len(earlier), expert_weight_kernel), grid=(4,), i...  13.6 us
  transfers between devices with their start and end apart: 115, of which 56 were waited for; matrix products, arithmetic and copies ran while one was open for 8% of the time, Pallas kernels for 17%

profile of v3, /device:TPU:1, one launch (start us, length us, event | category | flops | bytes accessed | tf_op | source)
XLA Modules:
  0.0 610.5 jit_solution(16390876645902471140)
XLA Ops:
  44.1 5.6 collective-permute-start.7
  51.3 7.5 %collective-permute-start.10 = (bf16[256,512]{1,0:T(8,128)(2,1)S(1)}, bf16[256,512]{1,0:T(8,128)(2,1)S(1)}, u32[]{:S(2)}, u32[]{:S(2)}) collective-permute-start(bf16[256,512]{1,0:T(8,128)(2,1)S(1)} %collective-permute-done.6.refs_6_.refs_14_.refs_8_.refs_16_), channel_id=1, source_target_pairs={{0,2},{2,0},{4,6},{6,4},{8,10},{10,8},{12,14},{14,12},{16,18},{18,... | collective-permute-start | bytes 786440 | tf_op jit(solution)/shard_map/ppermute | solution.py:28
  64.0 5.7 attend_forward.2
  109.9 5.9 collective-permute-start.30
  131.8 8.6 %experts_forward.1 = (bf16[256,1536]{1,0:T(8,128)(2,1)}, bf16[256,1536]{1,0:T(8,128)(2,1)}, bf16[512,1024]{1,0:T(8,128)(2,1)}, bf16[512,512]{1,0:T(8,128)(2,1)},...) custom-call(bf16[6,384,256]{2,1,0:T(8,128)(2,1)} %choose.2.refs_0_, s32[5]{0:T(128)} %stack.41.refs_0_.refs_1_.where_ref.refs_2_, ...), custom_call_target="tpu_custom_call" | custom-call | flops 2415919104 | bytes 10485760 | tf_op jit(solution)/shard_map/experts_forward/pallas_call | solution.py:494
  161.1 5.1 collective-permute-done.37
  193.5 4.9 collective-permute-start.45
  198.6 11.6 %collective-permute-start.47 = (bf16[256,512]{1,0:T(8,128)(2,1)S(1)}, bf16[256,512]{1,0:T(8,128)(2,1)S(1)}, u32[]{:S(2)}, u32[]{:S(2)}) collective-permute-start(bf16[256,512]{1,0:T(8,128)(2,1)S(1)} %collective-permute-done.43.refs_6_.refs_14_.refs_8_.refs_16_), channel_id=1, source_target_pairs={{0,2},{2,0},{4,6},{6,4},{8,10},{10,8},{12,14},{14,12},{16,18},{18,... | collective-permute-start | bytes 786440 | tf_op jit(solution)/shard_map/ppermute | solution.py:28
  213.3 5.6 attend_forward.3
  224.6 6.2 %collective-permute-done.48 = bf16[64,1536]{1,0:T(8,128)(2,1)S(1)} collective-permute-done((bf16[64,1536]{1,0:T(8,128)(2,1)}, bf16[64,1536]{1,0:T(8,128)(2,1)S(1)}, u32[]{:S(2)}, u32[]{:S(2)}) %collective-permute-start.48) | collective-permute-done | bytes 196640 | tf_op jit(solution)/shard_map/ppermute | solution.py:32
  248.5 13.4 %last_experts.1 = (bf16[512,1536]{1,0:T(8,128)(2,1)}, bf16[512,1536]{1,0:T(8,128)(2,1)}, bf16[512,512]{1,0:T(8,128)(2,1)}, bf16[512,1024]{1,0:T(8,128)(2,1)}, f3...) custom-call(s32[5]{0:T(128)} %stack.41.refs_0_.refs_1_.where_ref.refs_2_, ...), custom_call_target="tpu_custom_call" | custom-call | flops 4831838208 | bytes 16777216 | tf_op jit(solution)/shard_map/last_experts/pallas_call | solution.py:615
  270.0 8.0 %collective-permute-done.57 = bf16[128,1536]{1,0:T(8,128)(2,1)S(1)} collective-permute-done((bf16[128,1536]{1,0:T(8,128)(2,1)S(1)}, bf16[128,1536]{1,0:T(8,128)(2,1)S(1)}, u32[]{:S(2)}, u32[]{:S(2)}) %collective-permute-start.57) | collective-permute-done | bytes 393248 | tf_op jit(solution)/shard_map/ppermute | solution.py:28
  281.1 8.7 %collective-permute-done.59 = bf16[128,1536]{1,0:T(8,128)(2,1)S(1)} collective-permute-done((bf16[128,1536]{1,0:T(8,128)(2,1)S(1)}, bf16[128,1536]{1,0:T(8,128)(2,1)S(1)}, u32[]{:S(2)}, u32[]{:S(2)}) %collective-permute-start.59) | collective-permute-done | bytes 393248 | tf_op jit(solution)/shard_map/ppermute | solution.py:28
  292.8 6.8 %expert_weight_grads.2 = bf16[4,6,384,256]{3,2,1,0:T(8,128)(2,1)} custom-call(bf16[64,4608]{1,0:T(8,128)(2,1)} %side_by_side.3.refs_0_, bf16[512,1024]{1,0:T(8,128)(2,1)} %get-tuple-element.65.refs_1_, bf16[512,512]{1,0:T(8,128)(2,1)} %get-tuple-element.66.refs_2_, bf16[512,1536]{1,0:T(8,128)(2,1)} %get-tuple-element.67.refs_3_.refs_6_, ...), custom_call_target="tpu_custom_call" | custom-call | flops 2415919104 | bytes 10485760 | tf_op jit(solution)/shard_map/expert_weight_grads/pallas_call | solution.py:637
  304.8 7.3 %collective-permute-done.60 = bf16[128,1536]{1,0:T(8,128)(2,1)S(1)} collective-permute-done((bf16[128,1536]{1,0:T(8,128)(2,1)S(1)}, bf16[128,1536]{1,0:T(8,128)(2,1)S(1)}, u32[]{:S(2)}, u32[]{:S(2)}) %collective-permute-start.60) | collective-permute-done | bytes 393248 | tf_op jit(solution)/shard_map/ppermute | solution.py:32
  323.9 8.3 %attend_backward.2 = (bf16[64,768]{1,0:T(8,128)(2,1)}, bf16[1024,512]{1,0:T(8,128)(2,1)}, bf16[1024,512]{1,0:T(8,128)(2,1)}) custom-call(s32[5]{0:T(128)} %stack.41.refs_0_.refs_1_.where_ref.refs_2_, s32[1,128]{1,0:T(1,128)} %add_bitcast_fusion.refs_1_, bf16[64,768]{1,0:T(8,128)(2,1)} %slice.263.refs_2_, bf16[64,768]{1,0:T(8,128)(2,1)} %get-tuple-element.70.refs_3_, ...), custom_call_target="tpu_custom_call" | custom-call | flops 1006632960 | bytes 4194304 | tf_op jit(solution)/shard_map/attend_backward/pallas_call | solution.py:242
  340.8 5.7 collective-permute-done.63
  347.9 6.7 %collective-permute-done.65 = bf16[256,512]{1,0:T(8,128)(2,1)S(1)} collective-permute-done((bf16[256,512]{1,0:T(8,128)(2,1)S(1)}, bf16[256,512]{1,0:T(8,128)(2,1)S(1)}, u32[]{:S(2)}, u32[]{:S(2)}) %collective-permute-start.65) | collective-permute-done | bytes 262176 | tf_op jit(solution)/shard_map/ppermute | solution.py:28
  365.9 5.1 act_back.2
  386.7 5.7 collective-permute-done.70.refs_8_
  397.4 9.0 %experts_backward.1 = (bf16[512,1536]{1,0:T(8,128)(2,1)}, bf16[256,1536]{1,0:T(8,128)(2,1)}, bf16[256,1536]{1,0:T(8,128)(2,1)}, bf16[512,1024]{1,0:T(8,128)(2,1)}, f32[512,16]{1,0:T(8,128)}) custom-call(bf16[64,2944]{1,0:T(8,128)(2,1)} %pad_maximum_fusion.refs_0_, bf16[2304,256]{1,0:T(8,128)(2,1)} %reduce-scatter.4.cloned.1.call-done.refs_1_, ...), custom_call_target="tpu_custom_call" | custom-call | flops 2415919104 | bytes 10485760 | tf_op jit(solution)/shard_map/experts_backward/pallas_call | solution.py:545
  411.1 6.8 %expert_weight_grads.3 = bf16[4,6,384,256]{3,2,1,0:T(8,128)(2,1)} custom-call(bf16[256,1536]{1,0:T(8,128)(2,1)} %add_convert_fusion.3.refs_0_, bf16[512,1024]{1,0:T(8,128)(2,1)} %get-tuple-element.80.refs_1_, bf16[512,512]{1,0:T(8,128)(2,1)} %get-tuple-element.81.refs_2_, bf16[512,1536]{1,0:T(8,128)(2,1)} %get-tuple-element.82.refs_3_.refs_5_, ...), custom_call_target="tpu_custom_call" | custom-call | flops 2415919104 | bytes 10485760 | tf_op jit(solution)/shard_map/expert_weight_grads/pallas_call | solution.py:637
  435.5 6.6 %collective-permute-done.81.got_ref = bf16[64,1536]{1,0:T(8,128)(2,1)S(1)} collective-permute-done((bf16[64,1536]{1,0:T(8,128)(2,1)S(1)}, bf16[64,1536]{1,0:T(8,128)(2,1)S(1)}, u32[]{:S(2)}, u32[]{:S(2)}) %collective-permute-start.81) | collective-permute-done | bytes 196640 | tf_op jit(solution)/shard_map/ppermute | solution.py:32
  447.4 8.3 %attend_backward.3 = (bf16[64,768]{1,0:T(8,128)(2,1)}, bf16[1024,512]{1,0:T(8,128)(2,1)}, bf16[1024,512]{1,0:T(8,128)(2,1)}) custom-call(s32[5]{0:T(128)} %stack.41.refs_0_.refs_1_.where_ref.refs_2_, s32[1,128]{1,0:T(1,128)} %add_bitcast_fusion.refs_1_, bf16[64,768]{1,0:T(8,128)(2,1)} %slice.320.refs_2_, bf16[64,768]{1,0:T(8,128)(2,1)} %get-tuple-element.85.refs_3_, ...), custom_call_target="tpu_custom_call" | custom-call | flops 1006632960 | bytes 4194304 | tf_op jit(solution)/shard_map/attend_backward/pallas_call | solution.py:242
  463.9 6.6 %dense_slice.2 = bf16[4,816,128]{2,1,0:T(8,128)(2,1)} custom-call(bf16[1024,512]{1,0:T(8,128)(2,1)} %copy-done.9, s32[5]{0:T(128)} %stack.41.refs_0_.refs_1_.where_ref.refs_2_, bf16[512,4608]{1,0:T(8,128)(2,1)} %all-gather.22.cloned.1.call-done.refs_0_.refs_2_.refs_1_, f32[512,16]{1,0:T(8,128)} %get-tuple-element.90.refs_3_, ...), custom_call_target="tpu_custom_call" | custom-call | flops 1610612736 | bytes 8388608 | tf_op jit(solution)/shard_map/dense_slice/pallas_call | solution.py:696
  485.8 5.1 act_back.3
  496.7 5.4 collective-permute-done.91.refs_8_
  506.6 6.4 %dense_slice.3 = bf16[4,816,128]{2,1,0:T(8,128)(2,1)} custom-call(s32[5]{0:T(128)} %stack.41.refs_0_.refs_1_.where_ref.refs_2_, bf16[512,4608]{1,0:T(8,128)(2,1)} %all-gather.22.cloned.1.call-done.refs_0_.refs_2_.refs_1_, f32[512,16]{1,0:T(8,128)} %get-tuple-element.93.refs_2_, f32[512,16]{1,0:T(8,128)} %get-tuple-element.76.refs_6_.refs_3_, ...), custom_call_target="tpu_custom_call" | custom-call | flops 1610612736 | bytes 8388608 | tf_op jit(solution)/shard_map/dense_slice/pallas_call | solution.py:696
  517.3 9.3 %collective-permute-done.100 = bf16[816,128]{1,0:T(8,128)(2,1)S(1)} collective-permute-done((bf16[816,128]{1,0:T(8,128)(2,1)S(1)}, bf16[816,128]{1,0:T(8,128)(2,1)S(1)}, u32[]{:S(2)}, u32[]{:S(2)}) %collective-permute-start.100) | collective-permute-done | bytes 208928 | tf_op jit(solution)/shard_map/ppermute | solution.py:28
  542.1 26.9 %collective-permute-done.90 = bf16[64,1536]{1,0:T(8,128)(2,1)S(1)} collective-permute-done((bf16[64,1536]{1,0:T(8,128)(2,1)S(1)}, bf16[64,1536]{1,0:T(8,128)(2,1)S(1)}, u32[]{:S(2)}, u32[]{:S(2)}) %collective-permute-start.90) | collective-permute-done | bytes 196640 | tf_op jit(solution)/shard_map/ppermute | solution.py:32
  572.9 17.2 %all-gather.14.cloned.1.call-done = bf16[32,816,128]{2,1,0:T(8,128)(2,1)} async-done(((bf16[1,816,128]{2,1,0:T(8,128)(2,1)}), bf16[32,816,128]{2,1,0:T(8,128)(2,1)}) %all-gather.14.cloned.1.call-update) | async-done | bytes 6684688 | tf_op jit(solution)/shard_map/all_gather | solution.py:990
  590.1 9.7 %dense_rows.1 = (f32[1536,768]{1,0:T(8,128)}, f32[1536,256]{1,0:T(8,128)}, f32[1536,256]{1,0:T(8,128)}, f32[768,1536]{1,0:T(8,128)}, f32[1536,16]{1,0:T(8,128)}, /*index=5*/f32[16,1536]{1,0:T(8,128)}) custom-call(bf16[4,8,816,128]{3,2,1,0:T(8,128)(2,1)} %bitcast.126), custom_call_target="tpu_custom_call" | custom-call | bytes 20971520 | tf_op jit(solution)/shard_map/dense_rows/pallas_call | solution.py:734
  (559 shorter events, 329.4 us)
Async XLA Ops:
  7.2 66.9 %all-gather.16.cloned.1.call-start = ((), (), s32[]{:S(2)}) async-start(), calls=%async_computation.7 | async-start | bytes 6488064 | tf_op jit(solution)/shard_map/all_gather | solution.py:832
  20.6 111.1 %all-gather.18.cloned.1.call-start = ((), (), s32[]{:S(2)}) async-start(), calls=%async_computation.8 | async-start | bytes 5898240 | tf_op jit(solution)/shard_map/all_gather | solution.py:762
  34.7 15.0 %collective-permute-start.6 = (bf16[256,512]{1,0:T(8,128)(2,1)S(1)}, bf16[256,512]{1,0:T(8,128)(2,1)S(1)}, u32[]{:S(2)}, u32[]{:S(2)}) collective-permute-start(bf16[256,512]{1,0:T(8,128)(2,1)S(1)} %pad_maximum_fusion.2.refs_3_.refs_11_.refs_5_.refs_13_), channel_id=1, source_target_pairs={{0,12},{2,14},{4,0},{6,2},{8,4},{10,6},{12,8},{14,10},{16,28},{18,... | collective-permute-start | bytes 786440 | tf_op jit(solution)/shard_map/ppermute | solution.py:28
  40.6 29.1 %collective-permute-start.17 = (bf16[4,384,256]{2,1,0:T(8,128)(2,1)}, bf16[4,384,256]{2,1,0:T(8,128)(2,1)S(1)}, u32[]{:S(2)}, u32[]{:S(2)}) collective-permute-start(bf16[4,384,256]{2,1,0:T(8,128)(2,1)} %side_by_side.2), channel_id=1, source_target_pairs={{0,64},{64,0},{1,65},{65,1},{2,66},{66,2},{3,67},{67,3},{4,68},{68... | collective-permute-start | bytes 2359304 | tf_op jit(solution)/shard_map/ppermute | solution.py:32
  42.5 16.3 %collective-permute-start.5 = (bf16[256,512]{1,0:T(8,128)(2,1)S(1)}, bf16[256,512]{1,0:T(8,128)(2,1)S(1)}, u32[]{:S(2)}, u32[]{:S(2)}) collective-permute-start(bf16[256,512]{1,0:T(8,128)(2,1)S(1)} %pad_maximum_fusion.2.refs_3_.refs_11_.refs_5_.refs_13_), channel_id=1, source_target_pairs={{0,8},{2,10},{4,12},{6,14},{8,0},{10,2},{12,4},{14,6},{16,24},{18,... | collective-permute-start | bytes 786440 | tf_op jit(solution)/shard_map/ppermute | solution.py:28
  44.1 14.8 %collective-permute-start.7 = (bf16[256,512]{1,0:T(8,128)(2,1)S(1)}, bf16[256,512]{1,0:T(8,128)(2,1)S(1)}, u32[]{:S(2)}, u32[]{:S(2)}) collective-permute-start(bf16[256,512]{1,0:T(8,128)(2,1)S(1)} %pad_maximum_fusion.2.refs_3_.refs_11_.refs_5_.refs_13_), channel_id=1, source_target_pairs={{0,2},{2,0},{4,6},{6,4},{8,10},{10,8},{12,14},{14,12},{16,18},{18,... | collective-permute-start | bytes 786440 | tf_op jit(solution)/shard_map/ppermute | solution.py:28
  49.7 20.0 %collective-permute-start.16 = (bf16[2,384,256]{2,1,0:T(8,128)(2,1)S(1)}, bf16[2,384,256]{2,1,0:T(8,128)(2,1)}, u32[]{:S(2)}, u32[]{:S(2)}) collective-permute-start(bf16[2,384,256]{2,1,0:T(8,128)(2,1)S(1)} %bitcast.140), channel_id=1, source_target_pairs={{0,64},{64,0},{1,65},{65,1},{2,66},{66,2},{3,67},{67,3},{4,68},{68... | collective-permute-start | bytes 1179656 | tf_op jit(solution)/shard_map/ppermute | solution.py:32
  76.7 171.0 %all-gather.20.cloned.1.call-start = ((), (), s32[]{:S(2)}) async-start(), calls=%async_computation.9 | async-start | bytes 5898240 | tf_op jit(solution)/shard_map/all_gather | solution.py:762
  101.2 264.6 %all-gather.22.cloned.1.call-start = ((), (), s32[]{:S(2)}) async-start(), calls=%async_computation.10 | async-start | bytes 5308416 | tf_op jit(solution)/shard_map/all_gather | solution.py:906
  102.4 13.4 %collective-permute-start.27 = (bf16[64,1664]{1,0:T(8,128)(2,1)S(1)}, bf16[64,1664]{1,0:T(8,128)(2,1)S(1)}, u32[]{:S(2)}, u32[]{:S(2)}) collective-permute-start(bf16[64,1664]{1,0:T(8,128)(2,1)S(1)} %fusion.21.refs_12_.refs_11_), channel_id=1, source_target_pairs={{0,8},{2,10},{4,12},{6,14},{8,0},{10,2},{12,4},{14,6},{16,24},{18,... | collective-permute-start | bytes 638984 | tf_op jit(solution)/shard_map/ppermute | solution.py:28
  105.0 13.0 %collective-permute-start.29 = (bf16[64,1664]{1,0:T(8,128)(2,1)S(1)}, bf16[64,1664]{1,0:T(8,128)(2,1)S(1)}, u32[]{:S(2)}, u32[]{:S(2)}) collective-permute-start(bf16[64,1664]{1,0:T(8,128)(2,1)S(1)} %fusion.21.refs_12_.refs_11_), channel_id=1, source_target_pairs={{0,2},{2,0},{4,6},{6,4},{8,10},{10,8},{12,14},{14,12},{16,18},{18,... | collective-permute-start | bytes 638984 | tf_op jit(solution)/shard_map/ppermute | solution.py:28
  116.2 12.7 %collective-permute-start.20 = (bf16[64,1536]{1,0:T(8,128)(2,1)S(1)}, bf16[64,1536]{1,0:T(8,128)(2,1)S(1)}, u32[]{:S(2)}, u32[]{:S(2)}) collective-permute-start(bf16[64,1536]{1,0:T(8,128)(2,1)S(1)} %copy-done.32), channel_id=1, source_target_pairs={{0,8},{2,10},{4,12},{6,14},{8,0},{10,2},{12,4},{14,6},{16,24},{18,... | collective-permute-start | bytes 589832 | tf_op jit(solution)/shard_map/ppermute | solution.py:28
  182.9 15.5 %collective-permute-start.42 = (bf16[256,512]{1,0:T(8,128)(2,1)S(1)}, bf16[256,512]{1,0:T(8,128)(2,1)S(1)}, u32[]{:S(2)}, u32[]{:S(2)}) collective-permute-start(bf16[256,512]{1,0:T(8,128)(2,1)S(1)} %pad_maximum_fusion.3.refs_3_.refs_11_.refs_5_.refs_13_), channel_id=1, source_target_pairs={{0,8},{2,10},{4,12},{6,14},{8,0},{10,2},{12,4},{14,6},{16,24},{18,... | collective-permute-start | bytes 786440 | tf_op jit(solution)/shard_map/ppermute | solution.py:28
  184.0 14.5 %collective-permute-start.43 = (bf16[256,512]{1,0:T(8,128)(2,1)S(1)}, bf16[256,512]{1,0:T(8,128)(2,1)S(1)}, u32[]{:S(2)}, u32[]{:S(2)}) collective-permute-start(bf16[256,512]{1,0:T(8,128)(2,1)S(1)} %pad_maximum_fusion.3.refs_3_.refs_11_.refs_5_.refs_13_), channel_id=1, source_target_pairs={{0,12},{2,14},{4,0},{6,2},{8,4},{10,6},{12,8},{14,10},{16,28},{18,... | collective-permute-start | bytes 786440 | tf_op jit(solution)/shard_map/ppermute | solution.py:28
  186.0 25.6 %collective-permute-start.44 = (bf16[256,512]{1,0:T(8,128)(2,1)S(1)}, bf16[256,512]{1,0:T(8,128)(2,1)S(1)}, u32[]{:S(2)}, u32[]{:S(2)}) collective-permute-start(bf16[256,512]{1,0:T(8,128)(2,1)S(1)} %pad_maximum_fusion.3.refs_3_.refs_11_.refs_5_.refs_13_), channel_id=1, source_target_pairs={{0,2},{2,0},{4,6},{6,4},{8,10},{10,8},{12,14},{14,12},{16,18},{18,... | collective-permute-start | bytes 786440 | tf_op jit(solution)/shard_map/ppermute | solution.py:28
  193.5 18.1 %collective-permute-start.45 = (bf16[256,512]{1,0:T(8,128)(2,1)S(1)}, bf16[256,512]{1,0:T(8,128)(2,1)S(1)}, u32[]{:S(2)}, u32[]{:S(2)}) collective-permute-start(bf16[256,512]{1,0:T(8,128)(2,1)S(1)} %collective-permute-done.41.refs_4_.refs_12_.refs_6_.refs_14_), channel_id=1, source_target_pairs={{0,2},{2,0},{4,6},{6,4},{8,10},{10,8},{12,14},{14,12},{16,18},{18,... | collective-permute-start | bytes 786440 | tf_op jit(solution)/shard_map/ppermute | solution.py:28
  198.5 13.2 %collective-permute-start.46 = (bf16[256,512]{1,0:T(8,128)(2,1)S(1)}, bf16[256,512]{1,0:T(8,128)(2,1)S(1)}, u32[]{:S(2)}, u32[]{:S(2)}) collective-permute-start(bf16[256,512]{1,0:T(8,128)(2,1)S(1)} %collective-permute-done.42.refs_5_.refs_13_.refs_7_.refs_15_), channel_id=1, source_target_pairs={{0,2},{2,0},{4,6},{6,4},{8,10},{10,8},{12,14},{14,12},{16,18},{18,... | collective-permute-start | bytes 786440 | tf_op jit(solution)/shard_map/ppermute | solution.py:28
  198.6 13.1 %collective-permute-start.47 = (bf16[256,512]{1,0:T(8,128)(2,1)S(1)}, bf16[256,512]{1,0:T(8,128)(2,1)S(1)}, u32[]{:S(2)}, u32[]{:S(2)}) collective-permute-start(bf16[256,512]{1,0:T(8,128)(2,1)S(1)} %collective-permute-done.43.refs_6_.refs_14_.refs_8_.refs_16_), channel_id=1, source_target_pairs={{0,2},{2,0},{4,6},{6,4},{8,10},{10,8},{12,14},{14,12},{16,18},{18,... | collective-permute-start | bytes 786440 | tf_op jit(solution)/shard_map/ppermute | solution.py:28
  269.4 20.4 %collective-permute-start.59 = (bf16[128,1536]{1,0:T(8,128)(2,1)S(1)}, bf16[128,1536]{1,0:T(8,128)(2,1)S(1)}, u32[]{:S(2)}, u32[]{:S(2)}) collective-permute-start(bf16[128,1536]{1,0:T(8,128)(2,1)S(1)} %get-tuple-element.190), channel_id=1, source_target_pairs={{0,4},{2,6},{4,8},{6,10},{8,12},{10,14},{12,0},{14,2},{16,20},{18,... | collective-permute-start | bytes 1179656 | tf_op jit(solution)/shard_map/ppermute | solution.py:28
  292.7 103.9 %reduce-scatter.4.cloned.1.call-start = ((), (), s32[]{:S(2)}) async-start(), calls=%async_computation.3 | async-start | bytes 5898240 | tf_op jit(solution)/shard_map/reduce_scatter | solution.py:767
  299.7 164.2 %all-gather.24.cloned.1.call-start = ((), (), s32[]{:S(2)}) async-start(), calls=%async_computation.11 | async-start | bytes 3391488 | tf_op jit(solution)/shard_map/all_gather | solution.py:961
  340.0 14.6 %collective-permute-start.65 = (bf16[256,512]{1,0:T(8,128)(2,1)S(1)}, bf16[256,512]{1,0:T(8,128)(2,1)S(1)}, u32[]{:S(2)}, u32[]{:S(2)}) collective-permute-start(bf16[256,512]{1,0:T(8,128)(2,1)S(1)} %get-tuple-element.196), channel_id=1, source_target_pairs={{0,4},{2,6},{4,8},{6,10},{8,12},{10,14},{12,0},{14,2},{16,20},{18,... | collective-permute-start | bytes 786440 | tf_op jit(solution)/shard_map/ppermute | solution.py:28
  365.1 120.7 %reduce-scatter.6.cloned.1.call-start = ((), (), s32[]{:S(2)}) async-start(), calls=%async_computation.4 | async-start | bytes 5898240 | tf_op jit(solution)/shard_map/reduce_scatter | solution.py:767
  381.3 12.7 %collective-permute-start.71 = (bf16[64,1536]{1,0:T(8,128)(2,1)S(1)}, bf16[64,1536]{1,0:T(8,128)(2,1)S(1)}, u32[]{:S(2)}, u32[]{:S(2)}) collective-permute-start(bf16[64,1536]{1,0:T(8,128)(2,1)S(1)} %get-tuple-element.174.refs_7_), channel_id=1, source_target_pairs={{0,8},{2,10},{4,12},{6,14},{8,0},{10,2},{12,4},{14,6},{16,24},{18,... | collective-permute-start | bytes 589832 | tf_op jit(solution)/shard_map/ppermute | solution.py:28
  417.9 87.9 %all-gather.26.cloned.1.call-start = ((), (), s32[]{:S(2)}) async-start(), calls=%async_computation.12 | async-start | bytes 1916928 | tf_op jit(solution)/shard_map/all_gather | solution.py:965
  447.4 69.9 %reduce-scatter.8.cloned.1.call-start = ((), (), s32[]{:S(2)}) async-start(), calls=%async_computation.5 | async-start | bytes 1044480 | tf_op jit(solution)/shard_map/reduce_scatter | solution.py:767
  462.4 14.8 %collective-permute-start.85 = (bf16[256,512]{1,0:T(8,128)(2,1)S(1)}, bf16[256,512]{1,0:T(8,128)(2,1)S(1)}, u32[]{:S(2)}, u32[]{:S(2)}) collective-permute-start(bf16[256,512]{1,0:T(8,128)(2,1)S(1)} %get-tuple-element.193), channel_id=1, source_target_pairs={{0,4},{2,6},{4,8},{6,10},{8,12},{10,14},{12,0},{14,2},{16,20},{18,... | collective-permute-start | bytes 786440 | tf_op jit(solution)/shard_map/ppermute | solution.py:28
  479.9 110.1 %all-gather.14.cloned.1.call-start = ((), (), s32[]{:S(2)}) async-start(), calls=%async_computation.6 | async-start | bytes 6893568 | tf_op jit(solution)/shard_map/all_gather | solution.py:990
  490.9 12.9 %collective-permute-start.89 = (bf16[64,1536]{1,0:T(8,128)(2,1)}, bf16[64,1536]{1,0:T(8,128)(2,1)S(1)}, u32[]{:S(2)}, u32[]{:S(2)}) collective-permute-start(bf16[64,1536]{1,0:T(8,128)(2,1)} %act_back.3), channel_id=1, source_target_pairs={{0,1},{1,0},{2,3},{3,2},{4,5},{5,4},{6,7},{7,6},{8,9},{9,8},{10,11... | collective-permute-start | bytes 589832 | tf_op jit(solution)/shard_map/ppermute | solution.py:32
  514.1 12.5 %collective-permute-start.100 = (bf16[816,128]{1,0:T(8,128)(2,1)S(1)}, bf16[816,128]{1,0:T(8,128)(2,1)S(1)}, u32[]{:S(2)}, u32[]{:S(2)}) collective-permute-start(bf16[816,128]{1,0:T(8,128)(2,1)S(1)} %get-tuple-element.201), channel_id=1, source_target_pairs={{0,16},{2,18},{4,20},{6,22},{8,24},{10,26},{12,28},{14,30},{16,32}... | collective-permute-start | bytes 626696 | tf_op jit(solution)/shard_map/ppermute | solution.py:28
  539.3 30.7 %collective-permute-start.104 = (bf16[2304,256]{1,0:T(8,128)(2,1)S(1)}, bf16[2304,256]{1,0:T(8,128)(2,1)S(1)}, u32[]{:S(2)}, u32[]{:S(2)}) collective-permute-start(bf16[2304,256]{1,0:T(8,128)(2,1)S(1)} %broadcast_select_fusion), channel_id=1, source_target_pairs={{0,64},{64,0},{1,65},{65,1},{2,66},{66,2},{3,67},{67,3},{4,68},{68... | collective-permute-start | bytes 3538952 | tf_op jit(solution)/shard_map/ppermute | solution.py:32
  540.6 28.4 %collective-permute-start.90 = (bf16[64,1536]{1,0:T(8,128)(2,1)S(1)}, bf16[64,1536]{1,0:T(8,128)(2,1)S(1)}, u32[]{:S(2)}, u32[]{:S(2)}) collective-permute-start(bf16[64,1536]{1,0:T(8,128)(2,1)S(1)} %get-tuple-element.172), channel_id=1, source_target_pairs={{0,64},{64,0},{1,65},{65,1},{2,66},{66,2},{3,67},{67,3},{4,68},{68... | collective-permute-start | bytes 589832 | tf_op jit(solution)/shard_map/ppermute | solution.py:32
  (189 other events, 1680.4 us)
Sparse Core Ops, SparseCore 0:
  20.7 53.3 all-gather.15
  76.8 50.1 all-gather.17
  129.2 55.8 all-gather.19
  292.9 30.5 all-gather.21
  326.3 53.4 reduce-scatter.3
  381.4 27.6 all-gather.23
  418.0 48.3 reduce-scatter.5
  468.7 24.6 all-gather.25
  495.8 21.4 reduce-scatter.7
  539.2 50.8 all-gather.13

commit v4 on v3

--- a/solution.py
+++ b/solution.py
@@ -111,15 +111,15 @@
 SMEM = pl.BlockSpec(memory_space=pltpu.SMEM)
 VMEM = pl.BlockSpec(memory_space=pltpu.VMEM)
 ANY = pl.BlockSpec(memory_space=pl.ANY)
+HBM = pl.BlockSpec(memory_space=pltpu.HBM)
 
 
 def shaped(*shape, dtype=BF):
     return jax.ShapeDtypeStruct(shape, dtype)
 
 
-def params(mib):
-    del mib
-    return pltpu.CompilerParams(vmem_limit_bytes=58 << 20)
+def params(mib=58):
+    return pltpu.CompilerParams(vmem_limit_bytes=mib << 20)
 
 
 def cost(flops, bytes_accessed, exps=0):
@@ -169,10 +169,20 @@
     return jnp.concatenate([bias, bias, bias], axis=1)
 
 
-def attend_kernel(place_ref, st_ref, q_ref, *refs):
+def attend_kernel(layer, place_ref, st_ref, q_ref, *refs):
+    j = pl.program_id(0)
     keys = [stacked(refs[0:4]), stacked(refs[4:8])]
     values = [stacked(refs[8:12]), stacked(refs[12:16])]
-    out_ref, lse_ref = refs[16:]
+    if layer == 1:
+        earlier_refs, act_ref, out_w_ref, sent_ref = refs[16:18], refs[18], refs[19], refs[20]
+        out_ref, lse_ref, near_ref, far_ref, partial_ref, lefts_ref, held, sems = refs[21:]
+        start, wait = fetch_out(layer, place_ref, out_w_ref, sent_ref, held, sems)
+        pl.when(j == 0)(start)
+    else:
+        out_ref, lse_ref, near_ref, far_ref = refs[16:]
+    for k, v, to_ref in zip(keys, values, (near_ref, far_ref)):
+        to_ref[:, pl.ds(pl.multiple_of(j * 128, 128), 128)] = k
+        to_ref[:, pl.ds(pl.multiple_of(256 + j * 128, 128), 128)] = v
     query = (spread(q_ref[...]) * 0.125).astype(BF)
     scores = [nt(k, query) + bias_of(place_ref, h, st_ref) for h, k in enumerate(keys)]
     top = jnp.maximum(*[jnp.max(s, axis=0, keepdims=True) for s in scores])
@@ -182,8 +192,16 @@
         raised = jnp.exp(s - top)
         total = total + jnp.sum(raised, axis=0, keepdims=True)
         mixed = mixed + tn(v, raised.astype(BF))
-    out_ref[...] = gathered(mixed / total).astype(BF)
+    out_ref[:, pl.ds(pl.multiple_of(j * 384, 128), 384)] = gathered(mixed / total).astype(BF)
     lse_ref[0] = top + jnp.log(total)
+    if layer == 1:
+
+        @pl.when(j == 1)
+        def _():
+            wait()
+            partial_ref[...] = nn(out_ref[...], held[...]).astype(BF)
+            lefts_ref[:, 0:1536], lefts_ref[:, 1536:2304] = earlier_refs[0][...], earlier_refs[1][...]
+            lefts_ref[:, 2304:3840], lefts_ref[:, 3840:4608] = act_ref[...], out_ref[...]
 
 
 def column(rows, width, base):
@@ -198,26 +216,32 @@
     return lambda *refs: kernel(*refs[count:])
 
 
-def attend_forward(masks, query, pieces, *earlier):
-    return pl.pallas_call(
-        ignoring(len(earlier), attend_kernel),
+def fixed(*shape):
+    return pl.BlockSpec(shape, lambda j: (0,) * len(shape))
+
+
+def attend_forward(layer, masks, query, pieces, factors=(), weights=()):
+    last = layer == 1
+    return pl.pallas_call(
+        functools.partial(attend_kernel, layer),
         grid=(2,),
-        in_specs=[ANY] * len(earlier) + PAIRS[0] + [column(64, 384, 0)] + PAIRS[1],
-        out_specs=[column(64, 384, 0), LSE],
-        out_shape=[shaped(64, 768), shaped(2, 1, 384, dtype=F32)],
-        compiler_params=params(40),
+        in_specs=PAIRS[0] + [column(64, 384, 0)] + PAIRS[1] + [fixed(*f.shape) for f in factors] + [HBM] * len(weights),
+        out_specs=[fixed(64, 768), LSE, fixed(1024, 512), fixed(1024, 512)] + [fixed(64, D), fixed(64, 4608)] * last,
+        out_shape=[shaped(64, 768), shaped(2, 1, 384, dtype=F32), shaped(1024, 512), shaped(1024, 512)]
+        + [shaped(64, D), shaped(64, 4608)] * last,
+        scratch_shapes=OUT_HELD if last else [],
+        compiler_params=params(),
         cost_estimate=cost(12 * 64 * 2048 * 64 * 4, 2 << 20, 12 * 64 * 2048),
         name="attend_forward",
-    )(*earlier, *masks, query, *pieces, *pieces)
+    )(*masks, query, *pieces, *pieces, *factors, *weights)
 
 
 def attend_back_kernel(place_ref, st_ref, q_ref, do_ref, lse_ref, *refs):
     j = pl.program_id(0)
     key_columns = pl.ds(pl.multiple_of(j * 128, 128), 128)
     value_columns = pl.ds(pl.multiple_of(256 + j * 128, 128), 128)
-    keys = [stacked(refs[0:4]), stacked(refs[4:8])]
-    values = [stacked(refs[8:12]), stacked(refs[12:16])]
-    dq_ref, near_ref, far_ref = refs[16:]
+    keys, values = [ref[...] for ref in refs[0:2]], [ref[...] for ref in refs[2:4]]
+    dq_ref, near_ref, far_ref = refs[4:]
     query = (spread(q_ref[...]) * 0.125).astype(BF)
     grad = spread(do_ref[...]).astype(BF)
     weights, raws = [], []
@@ -238,17 +262,17 @@
     dq_ref[...] = gathered(turned * 0.125).astype(BF)
 
 
-def attend_backward(masks, query, grad, lse, pieces, *earlier):
+def attend_backward(masks, query, grad, lse, near, far, *earlier):
     return pl.pallas_call(
         ignoring(len(earlier), attend_back_kernel),
         grid=(2,),
-        in_specs=[ANY] * len(earlier) + PAIRS[0] + [column(64, 384, 0)] * 2 + [LSE] + PAIRS[1],
+        in_specs=[ANY] * len(earlier) + PAIRS[0] + [column(64, 384, 0)] * 2 + [LSE] + [column(1024, 128, 0)] * 2 + [column(1024, 128, 2)] * 2,
         out_specs=[column(64, 384, 0)] + [pl.BlockSpec((1024, 512), lambda j: (0, 0))] * 2,
         out_shape=[shaped(64, 768), shaped(1024, 512), shaped(1024, 512)],
-        compiler_params=params(48),
+        compiler_params=params(),
         cost_estimate=cost(12 * 64 * 2048 * 64 * 10, 4 << 20, 12 * 64 * 2048),
         name="attend_backward",
-    )(*earlier, *masks, query, grad, lse, *pieces, *pieces)
+    )(*earlier, *masks, query, grad, lse, near, far, near, far)
 
 
 def choose_kernel(layer, section_ref, gate_ref, up_ref, down_ref, sent_gate_ref, sent_ref, out_ref, sems):
@@ -277,7 +301,7 @@
         out_specs=VMEM,
         out_shape=shaped(6, 384, 256),
         scratch_shapes=[pltpu.SemaphoreType.DMA((3,))],
-        compiler_params=params(16),
+        compiler_params=params(),
         cost_estimate=cost(0, 3 << 20),
         name="choose",
     )(*earlier, section, *parts)
@@ -294,12 +318,23 @@
         in_specs=[ANY] * len(earlier) + [VMEM] * len(parts),
         out_specs=VMEM,
         out_shape=jax.ShapeDtypeStruct(tuple(shape), parts[0].dtype),
-        compiler_params=params(16),
+        compiler_params=params(),
         cost_estimate=cost(0, 2 << 20),
         name="side_by_side",
     )(*earlier, *parts)
 
 
+def held_until(value, *earlier):
+    return pl.pallas_call(
+        lambda *refs: None,
+        in_specs=[ANY] * (1 + len(earlier)),
+        out_specs=ANY,
+        out_shape=jax.ShapeDtypeStruct(value.shape, value.dtype),
+        input_output_aliases={0: 0},
+        name="held_until",
+    )(value, *earlier)
+
+
 def fetched(own, refs, held, sems, where_ref, others):
     def copies(pairs):
         return [pltpu.make_async_copy(a, b, sems.at[i]) for i, (a, b) in enumerate(pairs)]
@@ -307,15 +342,16 @@
     mine, sent = copies(refs), copies(others)
     is_own = where_ref[4] == own
 
-    @pl.when(is_own)
-    def _():
-        for copy in mine:
-            copy.start()
-
-    @pl.when(jnp.logical_not(is_own))
-    def _():
-        for copy in sent:
-            copy.start()
+    def start():
+        @pl.when(is_own)
+        def _():
+            for copy in mine:
+                copy.start()
+
+        @pl.when(jnp.logical_not(is_own))
+        def _():
+            for copy in sent:
+                copy.start()
 
     def wait():
         @pl.when(is_own)
@@ -328,23 +364,32 @@
             for copy in sent:
                 copy.wait()
 
-    return wait
+    return start, wait
 
 
 def fetch_qkv(layer, where_ref, q_ref, k_ref, v_ref, sent_ref, held, sems):
-    own = [(q_ref, held.at[:, 0:768]), (k_ref, held.at[:, 768:1024]), (v_ref, held.at[:, 1024:1280])]
-    return fetched(layer, own, held, sems, where_ref, [(sent_ref.at[:, 0:1280], held)])
+    own, sent = [], []
+    for i in range(4):
+        rows = slice(i * 384, (i + 1) * 384)
+        own += [(q_ref.at[rows], held.at[rows, 0:768]), (k_ref.at[rows], held.at[rows, 768:1024])]
+        own += [(v_ref.at[rows], held.at[rows, 1024:1280])]
+        sent += [(sent_ref.at[rows, 0:640], held.at[rows, 0:640]), (sent_ref.at[rows, 640:1280], held.at[rows, 640:1280])]
+    return fetched(layer, own, held, sems, where_ref, sent)
 
 
 def fetch_out(layer, where_ref, out_ref, sent_ref, held, sems):
-    halves = [
-        (sent_ref.at[h * 768 : (h + 1) * 768, 1280:2048], held.at[:, h * 768 : (h + 1) * 768]) for h in range(2)
-    ]
-    return fetched(layer, [(out_ref, held)], held, sems, where_ref, halves)
-
-
-QKV_HELD = [pltpu.VMEM((1536, 1280), BF), pltpu.SemaphoreType.DMA((3,))]
-OUT_HELD = [pltpu.VMEM((768, 1536), BF), pltpu.SemaphoreType.DMA((2,))]
+    own, sent = [], []
+    for i in range(4):
+        rows = slice(i * 192, (i + 1) * 192)
+        own.append((out_ref.at[rows], held.at[rows]))
+        for h in range(2):
+            from_rows = slice(h * 768 + i * 192, h * 768 + (i + 1) * 192)
+            sent.append((sent_ref.at[from_rows, 1280:2048], held.at[rows, h * 768 : (h + 1) * 768]))
+    return fetched(layer, own, held, sems, where_ref, sent)
+
+
+QKV_HELD = [pltpu.VMEM((1536, 1280), BF), pltpu.SemaphoreType.DMA((12,))]
+OUT_HELD = [pltpu.VMEM((768, 1536), BF), pltpu.SemaphoreType.DMA((8,))]
 
 
 def normed(value, gain):
@@ -353,7 +398,8 @@
 
 
 def qkv_kernel(layer, where_ref, hidden_ref, gain_ref, q_ref, k_ref, v_ref, sent_ref, act_ref, out_ref, held, sems):
-    wait = fetch_qkv(layer, where_ref, q_ref, k_ref, v_ref, sent_ref, held, sems)
+    start, wait = fetch_qkv(layer, where_ref, q_ref, k_ref, v_ref, sent_ref, held, sems)
+    start()
     act = normed(hidden_ref[...], gain_ref[...])[1].astype(BF)
     act_ref[...] = act
     wait()
@@ -367,32 +413,16 @@
         out_specs=[VMEM, VMEM],
         out_shape=[shaped(64, D), shaped(64, 1280)],
         scratch_shapes=QKV_HELD,
-        compiler_params=params(40),
+        compiler_params=params(20),
         cost_estimate=cost(64 * 1536 * 1280 * 2, 4 << 20),
         name="qkv_of",
     )(where, hidden, gain, *weights, sent)
 
 
-def out_kernel(layer, where_ref, mixed_ref, out_w_ref, sent_ref, out_ref, held, sems):
-    fetch_out(layer, where_ref, out_w_ref, sent_ref, held, sems)()
-    out_ref[...] = nn(mixed_ref[...], held[...]).astype(BF)
-
-
-def out_of(layer, where, mixed, weight, sent):
-    return pl.pallas_call(
-        functools.partial(out_kernel, layer),
-        in_specs=[SMEM, VMEM] + [ANY] * 2,
-        out_specs=VMEM,
-        out_shape=shaped(64, D),
-        scratch_shapes=OUT_HELD,
-        compiler_params=params(40),
-        cost_estimate=cost(64 * 1536 * 768 * 2, 3 << 20),
-        name="out_of",
-    )(where, mixed, weight, sent)
-
-
 def act_back_kernel(layer, where_ref, grad_ref, q_ref, k_ref, v_ref, sent_ref, out_ref, held, sems):
-    fetch_qkv(layer, where_ref, q_ref, k_ref, v_ref, sent_ref, held, sems)()
+    start, wait = fetch_qkv(layer, where_ref, q_ref, k_ref, v_ref, sent_ref, held, sems)
+    start()
+    wait()
     out_ref[...] = nt(grad_ref[...], held[...]).astype(BF)
 
 
@@ -403,7 +433,7 @@
         out_specs=VMEM,
         out_shape=shaped(64, D),
         scratch_shapes=QKV_HELD,
-        compiler_params=params(40),
+        compiler_params=params(),
         cost_estimate=cost(64 * 1536 * 1280 * 2, 4 << 20),
         name="act_back",
     )(*earlier, where, grad, *weights, sent)
@@ -413,7 +443,8 @@
     layer, where_ref, low_ref, got_ref, grad_ref, branch_ref, middle_ref, gain_ref, router_ref, routed_ref, out_w_ref, sent_ref,
     grad_middle_ref, right_ref, mixed_ref, gain_grad_ref, held, sems,
 ):
-    wait = fetch_out(layer, where_ref, out_w_ref, sent_ref, held, sems)
+    start, wait = fetch_out(layer, where_ref, out_w_ref, sent_ref, held, sems)
+    start()
     grad, middle, gain = grad_ref[...], middle_ref[...], gain_ref[...]
     inverse, second = normed(middle, gain)
     routed = routed_ref[...] > 0
@@ -449,7 +480,7 @@
         out_specs=[VMEM] * 4,
         out_shape=[shaped(64, D, dtype=F32), shaped(64, 1664), shaped(64, 768), shaped(1, D, dtype=F32)],
         scratch_shapes=OUT_HELD,
-        compiler_params=params(40),
+        compiler_params=params(),
         cost_estimate=cost(64 * 1536 * 768 * 2, 5 << 20),
         name="middle_back",
     )(where, low, got, grad, branch, middle, gain, router, routed, weight, sent)
@@ -459,7 +490,19 @@
     return pl.BlockSpec(shape, lambda j: (0,) * len(shape))
 
 
-def expert_kernel(where_ref, weight_ref, router_ref, *refs):
+class Quarters:
+    def __init__(self, refs):
+        self.refs = refs
+
+    def __getitem__(self, index):
+        return self.refs[index[0]][0, index[1]]
+
+
+QUARTERS = [pl.BlockSpec((1, 6, 384, 256), functools.partial(lambda r, j: (r, 0, 0, 0), r)) for r in range(4)]
+
+
+def expert_kernel(where_ref, router_ref, *refs):
+    weight_ref, refs = Quarters(refs[:4]), refs[4:]
     token_refs, routed_refs, (pa_ref, pb_ref, pre_ref, mid_ref, gates_ref, all_ref) = refs[:8], refs[8:16], refs[16:]
     for h, out_ref in enumerate((pa_ref, pb_ref)):
         rows = pl.ds(h * 256, 256)
@@ -495,18 +538,29 @@
         ignoring(len(earlier), expert_kernel),
         grid=(1,),
         in_specs=[ANY] * len(earlier)
-        + [SMEM, whole(4, 6, 384, 256), whole(16, D)] + [whole(64, D)] * 8 + [routed] * 8,
+        + [SMEM, whole(16, D)] + QUARTERS + [whole(64, D)] * 8 + [routed] * 8,
         out_specs=[whole(256, D)] * 2 + [whole(512, 1024), whole(512, 512), whole(512, 16), whole(512, D)],
         out_shape=[shaped(256, D), shaped(256, D), shaped(512, 1024), shaped(512, 512)]
         + [shaped(512, 16, dtype=F32), shaped(512, D)],
-        compiler_params=params(48),
+        compiler_params=params(),
         cost_estimate=cost(512 * 1536 * 1536 * 2, 10 << 20, 512 * 512),
         name="experts_forward",
-    )(*earlier, where, weights, router, *tokens, *given)
-
-
-def expert_back_kernel(order_ref, weight_ref, router_ref, pre_ref, gates_ref, *refs):
-    grad_refs, (all_ref, pa_ref, pb_ref, gpre_ref, gated_ref) = refs[:8], refs[8:]
+    )(*earlier, where, router, *[weights] * 4, *tokens, *given)
+
+
+def weight_products(out_ref, tokens_ref, grads_ref, gpre_ref, mid_ref):
+    for r in range(4):
+        lanes = slice(r * 384, (r + 1) * 384)
+        for left_ref, right_ref, base in ((tokens_ref, gpre_ref, 0), (grads_ref, mid_ref, 4)):
+            total = tn(left_ref[:, lanes], right_ref[...]).astype(BF)
+            for n in range(total.shape[1] // 256):
+                out_ref[r, base + n] = total[:, n * 256 : (n + 1) * 256]
+
+
+def expert_back_kernel(order_ref, router_ref, *refs):
+    weight_ref, pre_ref, gates_ref, refs = Quarters(refs[:4]), refs[4], refs[5], refs[6:]
+    tokens_ref, mid_ref, grad_refs = refs[0], refs[1], refs[2:10]
+    pa_ref, pb_ref, gated_ref, weight_grad_ref, all_ref, gpre_ref = refs[10:]
     for h, out_ref in enumerate((pa_ref, pb_ref)):
         rows = pl.ds(h * 256, 256)
         grad_out = stacked(grad_refs[4 * h : 4 * h + 4])
@@ -539,26 +593,29 @@
             for e in range(2):
                 made = made + nt(grads[e][0], weight_ref[r, e]) + nt(grads[e][1], weight_ref[r, 2 + e])
             out_ref[:, r * 384 : (r + 1) * 384] = made.astype(BF)
-
-
-def experts_backward(where, grads, pre, gates, router, weights, *earlier):
+    weight_products(weight_grad_ref, tokens_ref, all_ref, gpre_ref, mid_ref)
+
+
+def experts_backward(where, grads, pre, gates, tokens, mid, router, weights, *earlier):
     return pl.pallas_call(
         ignoring(len(earlier), expert_back_kernel),
         grid=(1,),
         in_specs=[ANY] * len(earlier)
-        + [SMEM, whole(4, 6, 384, 256), whole(16, D), whole(512, 1024), whole(512, 16)]
-        + [whole(64, D)] * 8,
-        out_specs=[whole(512, D), whole(256, D), whole(256, D), whole(512, 1024), whole(512, 16)],
-        out_shape=[shaped(512, D), shaped(256, D), shaped(256, D), shaped(512, 1024), shaped(512, 16, dtype=F32)],
-        compiler_params=params(48),
+        + [SMEM, whole(16, D)] + QUARTERS + [whole(512, 1024), whole(512, 16)]
+        + [whole(512, D), whole(512, 512)] + [whole(64, D)] * 8,
+        out_specs=[whole(256, D), whole(256, D), whole(512, 16), whole(4, 6, 384, 256)],
+        out_shape=[shaped(256, D), shaped(256, D), shaped(512, 16, dtype=F32), shaped(4, 6, 384, 256)],
+        scratch_shapes=[pltpu.VMEM((512, D), BF), pltpu.VMEM((512, 1024), BF)],
+        compiler_params=params(),
         cost_estimate=cost(512 * 1536 * 1536 * 2, 10 << 20, 512 * 512),
         name="experts_backward",
-    )(*earlier, where, weights, router, pre, gates, *grads)
-
-
-def last_expert_kernel(where_ref, weight_ref, router_ref, *refs):
+    )(*earlier, where, router, *[weights] * 4, pre, gates, tokens, mid, *grads)
+
+
+def last_expert_kernel(where_ref, router_ref, *refs):
+    weight_ref, refs = Quarters(refs[:4]), refs[4:]
     token_refs, given_refs = refs[:8], refs[8:16]
-    pa_ref, pb_ref, mid_ref, gpre_ref, gates_ref, gated_ref, tokens_ref, all_ref = refs[16:]
+    pa_ref, pb_ref, gates_ref, gated_ref, tokens_ref, weight_grad_ref, mid_ref, gpre_ref, all_ref = refs[16:]
     for h, out_ref in enumerate((pa_ref, pb_ref)):
         rows = pl.ds(h * 256, 256)
         tokens = stacked(token_refs[4 * h : 4 * h + 4])
@@ -609,6 +666,7 @@
             for j in range(4):
                 out_ref[j * 128 : j * 128 + 64, lanes] = made[j * 64 : (j + 1) * 64]
                 out_ref[j * 128 + 64 : (j + 1) * 128, lanes] = back[j * 64 : (j + 1) * 64]
+    weight_products(weight_grad_ref, tokens_ref, all_ref, gpre_ref, mid_ref)
 
 
 def last_experts(where, tokens, given, router, weights, *earlier):
@@ -616,34 +674,15 @@
         ignoring(len(earlier), last_expert_kernel),
         grid=(1,),
         in_specs=[ANY] * len(earlier)
-        + [SMEM, whole(4, 6, 384, 256), whole(16, D)] + [whole(64, D)] * 8 + [whole(64, 1664)] * 8,
-        out_specs=[whole(512, D)] * 2
-        + [whole(512, 512), whole(512, 1024), whole(512, 16), whole(512, 16), whole(512, D), whole(512, D)],
-        out_shape=[shaped(512, D), shaped(512, D), shaped(512, 512), shaped(512, 1024)]
-        + [shaped(512, 16, dtype=F32), shaped(512, 16, dtype=F32), shaped(512, D), shaped(512, D)],
-        compiler_params=params(48),
+        + [SMEM, whole(16, D)] + QUARTERS + [whole(64, D)] * 8 + [whole(64, 1664)] * 8,
+        out_specs=[whole(512, D)] * 2 + [whole(512, 16)] * 2 + [whole(512, D), whole(4, 6, 384, 256)],
+        out_shape=[shaped(512, D), shaped(512, D), shaped(512, 16, dtype=F32), shaped(512, 16, dtype=F32)]
+        + [shaped(512, D), shaped(4, 6, 384, 256)],
+        scratch_shapes=[pltpu.VMEM((512, 512), BF), pltpu.VMEM((512, 1024), BF), pltpu.VMEM((512, D), BF)],
+        compiler_params=params(),
         cost_estimate=cost(512 * 1536 * 1536 * 4, 16 << 20, 512 * 512),
         name="last_experts",
-    )(*earlier, where, weights, router, *tokens, *given)
-
-
-def expert_weight_kernel(gpre_ref, mid_ref, tokens_ref, grads_ref, out_ref):
-    for n in range(6):
-        left_ref, right_ref = (tokens_ref, gpre_ref) if n < 4 else (grads_ref, mid_ref)
-        out_ref[0, n] = tn(left_ref[...], right_ref[:, (n % 4) * 256 : (n % 4 + 1) * 256]).astype(BF)
-
-
-def expert_weight_grads(tokens, grads, gpre, mid, *earlier):
-    return pl.pallas_call(
-        ignoring(len(earlier), expert_weight_kernel),
-        grid=(4,),
-        in_specs=[ANY] * len(earlier) + [whole(512, 1024), whole(512, 512)] + [column(512, 384, 0)] * 2,
-        out_specs=pl.BlockSpec((1, 6, 384, 256), lambda r: (r, 0, 0, 0)),
-        out_shape=shaped(4, 6, 384, 256),
-        compiler_params=params(40),
-        cost_estimate=cost(512 * 1536 * 1536 * 2, 10 << 20),
-        name="expert_weight_grads",
-    )(*earlier, gpre, mid, tokens, grads)
+    )(*earlier, where, router, *[weights] * 4, *tokens, *given)
 
 
 def chosen(size, width, me):
@@ -656,8 +695,10 @@
     return ((where_ref[1] - (b & 3)) & 3) * 2 + (where_ref[2] if b < 4 else 1 - where_ref[2])
 
 
-def dense_slice_kernel(pieces, where_ref, left_ref, gated_ref, gates_ref, gains_ref, tokens_ref, right_ref, *refs):
+def dense_slice_kernel(pieces, where_ref, gated_ref, gates_ref, gains_ref, *refs):
     me = where_ref[3]
+    left, tokens, right_all = stacked(refs[0:4]), stacked(refs[4:8]), stacked(refs[8:12])
+    lane_refs, refs = refs[12], refs[13:]
     out_ref = refs[8 if pieces else 0]
     if pieces:
         right = refs[9]
@@ -665,26 +706,25 @@
             right[pl.ds(pl.multiple_of(source(where_ref, b) * 64, 64), 64), :] = refs[b][...]
         right = right[...]
     else:
-        right = right_ref[:, 1664:2944]
-    left = nn(left_ref[:, 0:1536], chosen(1536, 192, me)).astype(BF)
-    rows = tn(left, right).astype(BF)
-    left = nn(left_ref[:, 1536:2304], chosen(768, 96, me)).astype(BF)
+        right = right_all[:, 1664:2944]
+    rows = tn(nn(left[:, 0:1536], chosen(1536, 192, me)).astype(BF), right).astype(BF)
+    left = nn(left[:, 1536:2304], chosen(768, 96, me)).astype(BF)
     lane = lax.broadcasted_iota(jnp.int32, (64, 16), 1)
     logits = []
     for b in range(8):
         block = slice(b * 64, (b + 1) * 64)
         start = pl.multiple_of(source(where_ref, b) * 64, 64)
-        lanes = right_ref[pl.ds(start, 64), 1536:1664].astype(F32)
+        lanes = lane_refs[pl.ds(start, 64), :].astype(F32)
         inner = lanes[:, 0:1] + lanes[:, 1:2]
         grad = gated_ref[block] - 0.5 * gates_ref[block] * inner
         one = [jnp.sum(jnp.where(lane == 2 * me + e, grad, 0.0), axis=1, keepdims=True) for e in range(2)]
         logits.append(jnp.where(lane == 0, one[0], jnp.where(lane == 1, one[1], 0.0)).astype(BF))
-    extra = tn(jnp.concatenate(logits, axis=0), tokens_ref[...])
+    extra = tn(jnp.concatenate(logits, axis=0), tokens)
     row = lax.broadcasted_iota(jnp.int32, (16, D), 0)
-    extra = jnp.where(row == 2, gains_ref[0:1], jnp.where(row == 3, gains_ref[1:2], extra))
-    wide = jnp.concatenate([tn(left, right_ref[:, 0:1536]), extra], axis=0).astype(BF)
+    extra = jnp.where(row == 2, gains_ref[...], extra)
+    wide = jnp.concatenate([tn(left, right_all[:, 0:1536]), extra], axis=0).astype(BF)
     for r in range(4):
-        to = (where_ref[0] - r) & 3 if pieces else r
+        to = (where_ref[0] - r) & 3
         for c in range(10):
             out_ref[to, c * 48 : (c + 1) * 48] = rows[r * 48 : (r + 1) * 48, c * 128 : (c + 1) * 128]
         for c in range(3):
@@ -692,24 +732,31 @@
             out_ref[to, 480 + c * 112 : 480 + (c + 1) * 112] = wide[:, lanes]
 
 
+def quarters(width, base):
+    return [pl.BlockSpec((128, width), functools.partial(lambda i, j: (i, base), i)) for i in range(4)]
+
+
 def dense_slice(layer, where, left, gated, gates, gains, tokens, right, pieces, *earlier):
     return pl.pallas_call(
         ignoring(len(earlier), functools.partial(dense_slice_kernel, len(pieces) > 0)),
         grid=(1,),
         in_specs=[ANY] * len(earlier)
-        + [SMEM, pl.BlockSpec((512, 2304), lambda j: (0, layer)), whole(512, 16), whole(512, 16), whole(2, D)]
-        + [whole(512, D), whole(*right.shape)]
+        + [SMEM, whole(512, 16), whole(512, 16), whole(1, D)]
+        + quarters(2304, layer)
+        + quarters(D, 0)
+        + quarters(right.shape[1], 0)
+        + [pl.BlockSpec((512, 128), lambda j: (0, 12))]
         + [whole(64, 1280)] * len(pieces),
         out_specs=whole(4, 816, 128),
         out_shape=shaped(4, 816, 128),
         scratch_shapes=[pltpu.VMEM((512, 1280), BF)] if pieces else [],
-        compiler_params=params(40),
+        compiler_params=params(),
         cost_estimate=cost(512 * 1536 * 1024 * 2, 8 << 20),
         name="dense_slice",
-    )(*earlier, where, left, gated, gates, gains, tokens, right, *pieces)
-
-
-def dense_rows_kernel(in_ref, q_ref, k_ref, v_ref, out_ref, router_ref, gains_ref, held_ref):
+    )(*earlier, where, gated, gates, gains, *[left] * 4, *[tokens] * 4, *[right] * 5, *pieces)
+
+
+def dense_rows_kernel(in_ref, q_ref, k_ref, v_ref, out_ref, router_ref, gains_ref, first_ref, held_ref):
     j = pl.program_id(0)
     for x in range(4):
         rows = slice(x * 48, (x + 1) * 48)
@@ -721,11 +768,23 @@
             out_ref[:, lanes] = in_ref[x, 0, 480 + c * 112 : 576 + c * 112].astype(F32)
             held_ref[j, :, lanes] = in_ref[x, 0, 576 + c * 112 : 592 + c * 112].astype(F32)
 
+    own = in_ref[0, 0, 816:832].astype(F32)
+    for x in range(1, 4):
+        own = own + in_ref[x, 0, 816:832].astype(F32)
+
+    @pl.when(j == 0)
+    def _():
+        first_ref[...] = own
+
+    @pl.when(j != 0)
+    def _():
+        first_ref[...] = first_ref[...] + own
+
     @pl.when(j == 7)
     def _():
         held = held_ref[...]
         router = jnp.concatenate([held[i, 0:2] for i in range(8)], axis=0)
-        router_ref[...] = router.T
+        router_ref[...] = router
         gains_ref[...] = jnp.sum(held, axis=0)
 
 
@@ -734,12 +793,13 @@
     return pl.pallas_call(
         dense_rows_kernel,
         grid=(8,),
-        in_specs=[pl.BlockSpec((4, 1, 816, 128), lambda j: (0, j, 0, 0))],
-        out_specs=[rows(192, 768), rows(192, 256), rows(192, 256), rows(96, D), whole(D, 16), whole(16, D)],
+        in_specs=[pl.BlockSpec((4, 1, 832, 128), lambda j: (0, j, 0, 0))],
+        out_specs=[rows(192, 768), rows(192, 256), rows(192, 256), rows(96, D), whole(16, D), whole(16, D), whole(16, 128)],
         out_shape=[shaped(D, 768, dtype=F32), shaped(D, 256, dtype=F32), shaped(D, 256, dtype=F32)]
-        + [shaped(768, D, dtype=F32), shaped(D, 16, dtype=F32), shaped(16, D, dtype=F32)],
+        + [shaped(768, D, dtype=F32), shaped(16, D, dtype=F32), shaped(16, D, dtype=F32)]
+        + [shaped(16, 128, dtype=F32)],
         scratch_shapes=[pltpu.VMEM((8, 16, D), F32)],
-        compiler_params=params(40),
+        compiler_params=params(28),
         cost_estimate=cost(0, 20 << 20),
         name="dense_rows",
     )(everything)
@@ -866,7 +926,12 @@
         slab = jnp.concatenate([pair] + around, axis=0)
         near = [slab] + [moved(slab, 0, j, 0) for j in (1, 2, 3)]
         pieces = near + [moved(piece, 0, 0, 1) for piece in near]
-        mixed, log_total = attend_forward(masks, query, pieces)
+        if layer == 0:
+            mixed, log_total, *pieces = attend_forward(0, masks, query, pieces)
+        else:
+            mixed, log_total, *pieces, partial, lefts = attend_forward(
+                1, masks, query, pieces, (*saved[0][8], activation), (w_out[0], dense_all)
+            )
         if layer == 0:
             mixed_sent = lax.ppermute(mixed, "section", [(1, 0)])
             partial = dot(jnp.concatenate([mixed, mixed_sent], axis=0), w_out[0]).astype(BF)
@@ -874,18 +939,17 @@
             straight = lax.ppermute(partial[rows:], both_axes, [(0, 2), (1, 3)])
             across = lax.ppermute(partial[rows:], both_axes, [(0, 3), (1, 2)])
             turned = lax.ppermute(partial[:rows], both_axes, [(0, 1), (1, 0)])
-            experts_first = choose(0, section[None].astype(jnp.int32), halves, dense_all, mixed)
+            experts_first = choose(0, section[None].astype(jnp.int32), halves, mixed)
             expert_weights[0] = replica_gather(experts_first)
             middle = hidden + (
                 jnp.where(first, partial[:rows], straight).astype(F32) + jnp.where(first, turned, across).astype(F32)
             )
         else:
-            partial = out_of(1, where, mixed, w_out[0], dense_all)
             middle = hidden + (partial.astype(F32) + swapped(partial, "tensor").astype(F32))
         second = norm_apply(middle, gain_two).astype(BF)
         tokens = group_pieces(second)
         if layer == 0:
-            experts_second = choose(1, section[None].astype(jnp.int32), halves, second)
+            experts_second = choose(1, section[None].astype(jnp.int32), halves, second, dense_all)
             expert_weights[1] = replica_gather(experts_second)
         cut = (activation, mixed)
         if layer == 0:
@@ -894,20 +958,19 @@
             )
             made = group_sum(made_near, made_far).reshape(rows, D).astype(BF)
             branch = tensor_sum(made)
-            rest = (mid, gates, pre)
+            rest = (gates, (pre, mid))
         else:
-            near, far, mid, grad_pre, gates, gated, tokens, grad_all = last_experts(
+            near, far, gates, gated, tokens, weight_grads = last_experts(
                 where, tokens, given_all, routers[1], expert_weights[1]
             )
             both = (near.astype(F32) + moved(far, 0, 0, 1).astype(F32)).astype(BF)
             low = back_y(both).reshape(2 * rows, D).astype(BF)
-            lefts = side_by_side([*saved[0][8], *cut], 1, low)
-            weight_grads = expert_weight_grads(tokens, grad_all, grad_pre, mid, lefts)
+            lefts = held_until(lefts, low)
             lefts = lax.all_gather(lefts, "dp", axis=0, axis_index_groups=Y_GROUPS).reshape(8 * rows, 4608)
-            got = behind(swapped(low, "tensor"), weight_grads)
+            got = swapped(low, "tensor")
             branch = low[:rows].astype(F32) + got[:rows].astype(F32)
             low, got = low[rows:], got[rows:]
-            rest = (mid, gates, gated)
+            rest = (gates, gated)
         result = middle + branch
         saved.append((hidden, query, pieces, log_total, middle, second, tokens, branch, cut, result, rest))
         hidden = result
@@ -927,22 +990,21 @@
         hidden, query, pieces, log_total, middle, second, tokens, branch, _, _, rest = saved[layer]
         gain_one, gain_two = packs[layer][0:1], packs[layer][1:2]
         router = routers[layer]
-        mid, gates, rest = rest
+        gates, rest = rest
         if layer == 1:
             gated = rest
         else:
-            grad_all, back_near, back_far, grad_pre, gated = experts_backward(
-                where, group_pieces(grad_output.astype(BF)), rest, gates, router, expert_weights[0], *earlier
+            back_near, back_far, gated, weight_grads = experts_backward(
+                where, group_pieces(grad_output.astype(BF)), rest[0], gates, tokens, rest[1], router, expert_weights[0], *earlier
             )
             both = (back_near.astype(F32) + moved(back_far, 0, 0, 1).astype(F32)).astype(BF)
-            weight_grads = expert_weight_grads(tokens, grad_all, grad_pre, mid, both)
-            low = behind(back_y(both), weight_grads).reshape(rows, D).astype(BF)
+            low = back_y(both).reshape(rows, D).astype(BF)
             got = swapped(low, "tensor")
         expert_part = replica_scatter(weight_grads)
         grad_middle, right, grad_mixed, gain_two_grad = middle_back(
             layer, where, low, got, grad_output, branch, middle, gain_two, router, routed_own, w_out[0], dense_all
         )
-        grad_query, back_near, back_far = attend_backward(masks, query, grad_mixed, log_total, pieces)
+        grad_query, back_near, back_far = attend_backward(masks, query, grad_mixed, log_total, *pieces)
         both = (back_near.astype(F32) + moved(back_far, 0, 0, 1).astype(F32)).astype(BF)
         half = back_y(both)
         if layer == 0:
@@ -950,21 +1012,23 @@
             half = behind(half, late)
         grad_pair = back_x(half.astype(BF)).reshape(rows, 512).astype(BF)
         grad_qkv = jnp.concatenate([grad_query, grad_pair], axis=1)
-        partial = act_back(layer, where, grad_qkv, weights_in, dense_all, lefts if layer == 1 else expert_part)
+        if layer == 0:
+            grad_qkv = held_until(grad_qkv, expert_part)
+            right_pieces = group_pieces(grad_qkv)
+        partial = act_back(layer, where, grad_qkv, weights_in, dense_all, lefts if layer == 1 else right_pieces[1])
         grad_activation = partial.astype(F32) + swapped(partial, "tensor").astype(F32)
         grad_from_first, gain_one_grad = norm_back(hidden, gain_one, grad_activation)
         grad_input = grad_middle + grad_from_first
-        gains = jnp.concatenate([gain_two_grad, gain_one_grad[None]], axis=0)
         if layer == 1:
             right = jnp.concatenate([right, grad_qkv], axis=1)
             earlier = [right, expert_part]
             right = lax.all_gather(right, "dp", axis=0, axis_index_groups=Y_GROUPS).reshape(8 * rows, 2944)
-            grads.append((grad_input, (where, lefts, gated, gates, gains, tokens, right), expert_part))
+            grads.append((grad_input, (where, lefts, gated, gates, gain_two_grad, tokens, right), expert_part, gain_one_grad))
         else:
-            late = replica_scatter(late)
             right = lax.all_gather(right, "dp", axis=0, axis_index_groups=Y_GROUPS).reshape(8 * rows, 1664)
-            blocks = dense_slice(0, where, lefts, gated, gates, gains, tokens, right, group_pieces(grad_qkv))
-            grads.append((grad_input, back_x(blocks.reshape(4 * 816, 128)).reshape(816, 128), expert_part))
+            blocks = dense_slice(0, where, lefts, gated, gates, gain_two_grad, tokens, right, right_pieces, partial)
+            late = back_x(late.reshape(4 * 816, 128)).reshape(816, 128)
+            grads.append((grad_input, back_x(blocks.reshape(4 * 816, 128)).reshape(816, 128), expert_part, gain_one_grad))
         grad_output = grad_input
     grads = grads[::-1]
 
@@ -973,33 +1037,34 @@
 
     results = by_batch(own_of(saved[0][9], saved[1][9]), from_other(saved[0][9], saved[1][9]))
     input_grads = by_batch(own_of(grads[0][0], grads[1][0]), from_other(grads[0][0], grads[1][0]))
-    first_part, late = grads[0][1], late.astype(F32)
+    first_part = grads[0][1]
 
     def extras(block):
-        return block.reshape(-1, 128)[480:].reshape(3, 112, 128)[:, 96:98].reshape(6, 128)
+        return block[480:816].reshape(3, 112, 128)[:, 96:98].reshape(6, 128)
 
     straight = swapped(jnp.concatenate([extras(first_part), extras(late)], axis=0).astype(BF), "tensor").astype(F32)
     across = lax.ppermute(
         own_of(extras(late), extras(first_part)).astype(BF), ("section", "tensor"), [(0, 3), (1, 2), (2, 1), (3, 0)]
     ).astype(F32)
-    block = over_sections(first_part, late)
+    gain_rows = [jnp.pad(g[3].reshape(12, 128), ((0, 4), (0, 0))) for g in grads]
+    block = over_sections(*[jnp.concatenate(pair, axis=0) for pair in ((first_part, gain_rows[0]), (late, gain_rows[1]))])
     more = own_of(straight[:6], straight[6:]) + across
-    wide = block[480:].reshape(3, 112, 128)
+    wide = block[480:816].reshape(3, 112, 128)
     wide = wide + jnp.pad(more.reshape(3, 2, 128), ((0, 0), (96, 14), (0, 0)))
-    block = jnp.concatenate([block[:480], wide.reshape(336, 128)], axis=0).astype(BF)
-    everything = lax.all_gather(block, "dp", axis=0).reshape(4, 8, 816, 128)
-    query_sum, key_sum, value_sum, out_full, router_sum, gains = dense_rows(everything)
+    block = jnp.concatenate([block[:480], wide.reshape(336, 128), block[816:]], axis=0).astype(BF)
+    everything = lax.all_gather(block, "dp", axis=0).reshape(4, 8, 832, 128)
+    query_sum, key_sum, value_sum, out_full, router_sum, gains, gain_one_sum = dense_rows(everything)
     expert_sum = over_sections(grads[0][2], grads[1][2]).reshape(3, 2, 384, 256)
     return (
         results,
         input_grads,
-        gains[3:4],
+        gain_one_sum[:12].reshape(1, D),
         query_sum[None],
         key_sum[None],
         value_sum[None],
         out_full[None],
         gains[2:3],
-        router_sum[None],
+        router_sum.T[None],
         expert_sum[0][None],
         expert_sum[1][None],
         jnp.swapaxes(expert_sum[2], 1, 2)[None],

time: 621 us -> 609 us (0.981)
  Pallas kernels: 132 us -> 116 us
  starting transfers between devices: 147 us -> 156 us
    pallas_call x5 -> x4, Pallas kernels: 28.8 us -> 14.3 us  [the longest x2 14.3 us: attend_forward(): pl.pallas_call(functools.partial(attend_kernel, layer), grid=(2,), in_spe...]
    ppermute x84 -> x87, starting transfers between devices: 119 us -> 126 us  [moved(): return lax.ppermute(value, 'dp', route)]
    unnamed x212 -> x193, local copies, waits for them, and re-layouts: 14.9 us -> 18.1 us
    ppermute x84 -> x87, waiting for transfers between devices: 131 us -> 131 us  [moved(): return lax.ppermute(value, 'dp', route)]
  transfers between devices with their start and end apart: 115 -> 117, of which waited for: 56 -> 57; matrix products, arithmetic and copies ran while one was open for 8% -> 9% of each run, Pallas kernels for 17% -> 16%
where the time goes in v4:
time: 609 us; the launch traced here: 604 us
  waiting for transfers between devices  230 us (38%)
  starting transfers between devices  156 us (26%)
  Pallas kernels  116 us (19%)
  other arithmetic  39.9 us (7%)
  local copies, waits for them, and re-layouts  38.8 us (6%)
  between operations  18.1 us (3%)
    ppermute x87, waiting for transfers between devices, moved(): return lax.ppermute(value, 'dp', route)  131 us
    ppermute x87, starting transfers between devices, moved(): return lax.ppermute(value, 'dp', route)  126 us
    ppermute x15, waiting for transfers between devices, swapped(): return lax.ppermute(value, axis, [(0, 1), (1, 0)])  69.1 us
    unnamed x193, local copies, waits for them, and re-layouts  18.1 us
    ppermute x15, starting transfers between devices, swapped(): return lax.ppermute(value, axis, [(0, 1), (1, 0)])  18 us
    all_gather x1, waiting for transfers between devices, per_device(): everything = lax.all_gather(block, 'dp', axis=0).reshape(4, 8, 832, 128)  16.9 us
    pallas_call x1, Pallas kernels, last_experts(): pl.pallas_call(ignoring(len(earlier), last_expert_kernel), grid=(1,), in_...  16.6 us
    pallas_call x2, Pallas kernels, attend_backward(): pl.pallas_call(ignoring(len(earlier), attend_back_kernel), grid=(2,), in_...  16.3 us
  transfers between devices with their start and end apart: 117, of which 57 were waited for; matrix products, arithmetic and copies ran while one was open for 9% of the time, Pallas kernels for 16%

profile of v4, /device:TPU:1, one launch (start us, length us, event | category | flops | bytes accessed | tf_op | source)
XLA Modules:
  0.0 604.0 jit_solution(3188979590296095730)
XLA Ops:
  57.1 6.5 %collective-permute-start.10 = (bf16[256,512]{1,0:T(8,128)(2,1)}, bf16[256,512]{1,0:T(8,128)(2,1)}, u32[]{:S(2)}, u32[]{:S(2)}) collective-permute-start(bf16[256,512]{1,0:T(8,128)(2,1)} %collective-permute-done.6.refs_3_.refs_11_), channel_id=1, source_target_pairs={{0,2},{2,0},{4,6},{6,4},{8,10},{10,8},{12,14},{14,12},{16,18},{18,... | collective-permute-start | bytes 786440 | tf_op jit(solution)/shard_map/ppermute | solution.py:28
  68.8 6.4 %attend_forward.2 = (bf16[64,768]{1,0:T(8,128)(2,1)}, f32[2,1,384]{2,1,0:T(1,128)}, bf16[1024,512]{1,0:T(8,128)(2,1)}, bf16[1024,512]{1,0:T(8,128)(2,1)}) custom-call(s32[5]{0:T(128)} %stack.41.place_ref.refs_1_.where_ref.refs_0_.refs_2_, s32[1,128]{1,0:T(1,128)} %add_bitcast_fusion.st_ref.refs_1_, bf16[64,768]{1,0:T(8,128)(2,1)} %slice.333.q_ref.refs_2_, ...), custom_call_target="tpu_custom_call" | custom-call | flops 402653184 | bytes 2097152 | tf_op jit(solution)/shard_map/attend_forward/pallas_call | solution.py:225
  116.1 6.1 %collective-permute-start.30 = (bf16[64,1664]{1,0:T(8,128)(2,1)S(1)}, bf16[64,1664]{1,0:T(8,128)(2,1)S(1)}, u32[]{:S(2)}, u32[]{:S(2)}) collective-permute-start(bf16[64,1664]{1,0:T(8,128)(2,1)S(1)} %collective-permute-done.26.refs_16_.refs_15_), channel_id=1, source_target_pairs={{0,2},{2,0},{4,6},{6,4},{8,10},{10,8},{12,14},{14,12},{16,18},{18,... | collective-permute-start | bytes 638984 | tf_op jit(solution)/shard_map/ppermute | solution.py:28
  122.3 12.3 %collective-permute-start.19 = (bf16[64,1536]{1,0:T(8,128)(2,1)}, bf16[64,1536]{1,0:T(8,128)(2,1)S(1)}, u32[]{:S(2)}, u32[]{:S(2)}) collective-permute-start(bf16[64,1536]{1,0:T(8,128)(2,1)} %multiply_convert_fusion.1.refs_0_.refs_7_), channel_id=1, source_target_pairs={{0,4},{2,6},{4,8},{6,10},{8,12},{10,14},{12,0},{14,2},{16,20},{18,... | collective-permute-start | bytes 589832 | tf_op jit(solution)/shard_map/ppermute | solution.py:28
  139.0 7.5 %collective-permute-done.19.refs_8_ = bf16[64,1536]{1,0:T(8,128)(2,1)S(1)} collective-permute-done((bf16[64,1536]{1,0:T(8,128)(2,1)}, bf16[64,1536]{1,0:T(8,128)(2,1)S(1)}, u32[]{:S(2)}, u32[]{:S(2)}) %collective-permute-start.19) | collective-permute-done | bytes 196640 | tf_op jit(solution)/shard_map/ppermute | solution.py:28
  151.8 8.5 %experts_forward.1 = (bf16[256,1536]{1,0:T(8,128)(2,1)}, bf16[256,1536]{1,0:T(8,128)(2,1)}, bf16[512,1024]{1,0:T(8,128)(2,1)}, bf16[512,512]{1,0:T(8,128)(2,1)},...) custom-call(bf16[6,384,256]{2,1,0:T(8,128)(2,1)} %choose.2.refs_0_, s32[5]{0:T(128)} %stack.41.place_ref.refs_1_.where_ref.refs_0_.refs_2_, ...), custom_call_target="tpu_custom_call" | custom-call | flops 2415919104 | bytes 10485760 | tf_op jit(solution)/shard_map/experts_forward/pallas_call | solution.py:537
  167.5 7.6 %collective-permute-done.34 = bf16[64,1536]{1,0:T(8,128)(2,1)S(1)} collective-permute-done((bf16[64,1536]{1,0:T(8,128)(2,1)S(1)}, bf16[64,1536]{1,0:T(8,128)(2,1)S(1)}, u32[]{:S(2)}, u32[]{:S(2)}) %collective-permute-start.34) | collective-permute-done | bytes 196640 | tf_op jit(solution)/shard_map/ppermute | solution.py:28
  209.7 5.0 collective-permute-start.45
  217.4 7.9 %attend_forward.3 = (bf16[64,768]{1,0:T(8,128)(2,1)}, f32[2,1,384]{2,1,0:T(1,128)}, bf16[1024,512]{1,0:T(8,128)(2,1)}, bf16[1024,512]{1,0:T(8,128)(2,1)}, bf16[6...) custom-call(s32[5]{0:T(128)} %stack.41.place_ref.refs_1_.where_ref.refs_0_.refs_2_, ...), custom_call_target="tpu_custom_call" | custom-call | flops 402653184 | bytes 2097152 | tf_op jit(solution)/shard_map/attend_forward/pallas_call | solution.py:225
  226.9 6.2 %collective-permute-done.48 = bf16[64,1536]{1,0:T(8,128)(2,1)S(1)} collective-permute-done((bf16[64,1536]{1,0:T(8,128)(2,1)}, bf16[64,1536]{1,0:T(8,128)(2,1)S(1)}, u32[]{:S(2)}, u32[]{:S(2)}) %collective-permute-start.48) | collective-permute-done | bytes 196640 | tf_op jit(solution)/shard_map/ppermute | solution.py:32
  250.9 16.6 %last_experts.1 = (bf16[512,1536]{1,0:T(8,128)(2,1)}, bf16[512,1536]{1,0:T(8,128)(2,1)}, f32[512,16]{1,0:T(8,128)}, f32[512,16]{1,0:T(8,128)}, bf16[512,1536]{1,...) custom-call(s32[5]{0:T(128)} %stack.41.place_ref.refs_1_.where_ref.refs_0_.refs_2_, ...), custom_call_target="tpu_custom_call" | custom-call | flops 4831838208 | bytes 16777216 | tf_op jit(solution)/shard_map/last_experts/pallas_call | solution.py:673
  275.9 8.4 %collective-permute-done.57 = bf16[128,1536]{1,0:T(8,128)(2,1)S(1)} collective-permute-done((bf16[128,1536]{1,0:T(8,128)(2,1)S(1)}, bf16[128,1536]{1,0:T(8,128)(2,1)S(1)}, u32[]{:S(2)}, u32[]{:S(2)}) %collective-permute-start.57) | collective-permute-done | bytes 393248 | tf_op jit(solution)/shard_map/ppermute | solution.py:28
  287.1 8.6 %collective-permute-done.59 = bf16[128,1536]{1,0:T(8,128)(2,1)S(1)} collective-permute-done((bf16[128,1536]{1,0:T(8,128)(2,1)S(1)}, bf16[128,1536]{1,0:T(8,128)(2,1)S(1)}, u32[]{:S(2)}, u32[]{:S(2)}) %collective-permute-start.59) | collective-permute-done | bytes 393248 | tf_op jit(solution)/shard_map/ppermute | solution.py:28
  299.5 9.7 %collective-permute-done.60 = bf16[128,1536]{1,0:T(8,128)(2,1)S(1)} collective-permute-done((bf16[128,1536]{1,0:T(8,128)(2,1)S(1)}, bf16[128,1536]{1,0:T(8,128)(2,1)S(1)}, u32[]{:S(2)}, u32[]{:S(2)}) %collective-permute-start.60) | collective-permute-done | bytes 393248 | tf_op jit(solution)/shard_map/ppermute | solution.py:32
  320.8 8.2 %attend_backward.2 = (bf16[64,768]{1,0:T(8,128)(2,1)}, bf16[1024,512]{1,0:T(8,128)(2,1)}, bf16[1024,512]{1,0:T(8,128)(2,1)}) custom-call(s32[5]{0:T(128)} %stack.41.place_ref.refs_1_.where_ref.refs_0_.refs_2_, s32[1,128]{1,0:T(1,128)} %add_bitcast_fusion.st_ref.refs_1_, bf16[64,768]{1,0:T(8,128)(2,1)} %slice.273.q_ref.refs_2_, ...), custom_call_target="tpu_custom_call" | custom-call | flops 1006632960 | bytes 4194304 | tf_op jit(solution)/shard_map/attend_backward/pallas_call | solution.py:266
  337.3 6.0 collective-permute-done.63
  344.5 6.7 %collective-permute-done.65 = bf16[256,512]{1,0:T(8,128)(2,1)S(1)} collective-permute-done((bf16[256,512]{1,0:T(8,128)(2,1)S(1)}, bf16[256,512]{1,0:T(8,128)(2,1)S(1)}, u32[]{:S(2)}, u32[]{:S(2)}) %collective-permute-start.65) | collective-permute-done | bytes 262176 | tf_op jit(solution)/shard_map/ppermute | solution.py:28
  363.4 5.2 act_back.2
  369.6 6.0 collective-permute-done.69
  384.5 5.2 collective-permute-done.70.refs_13_
  393.9 13.5 %experts_backward.1 = (bf16[256,1536]{1,0:T(8,128)(2,1)}, bf16[256,1536]{1,0:T(8,128)(2,1)}, f32[512,16]{1,0:T(8,128)}, bf16[4,6,384,256]{3,2,1,0:T(8,128)(2,1)}) custom-call(bf16[64,2944]{1,0:T(8,128)(2,1)} %pad_maximum_fusion.refs_0_, bf16[2304,256]{1,0:T(8,128)(2,1)} %reduce-scatter.3.cloned.1.call-done.refs_1_, ...), custom_call_target="tpu_custom_call" | custom-call | flops 2415919104 | bytes 10485760 | tf_op jit(solution)/shard_map/experts_backward/pallas_call | solution.py:600
  427.0 6.4 %collective-permute-done.81.got_ref = bf16[64,1536]{1,0:T(8,128)(2,1)S(1)} collective-permute-done((bf16[64,1536]{1,0:T(8,128)(2,1)S(1)}, bf16[64,1536]{1,0:T(8,128)(2,1)S(1)}, u32[]{:S(2)}, u32[]{:S(2)}) %collective-permute-start.81) | collective-permute-done | bytes 196640 | tf_op jit(solution)/shard_map/ppermute | solution.py:32
  438.6 8.2 %attend_backward.3 = (bf16[64,768]{1,0:T(8,128)(2,1)}, bf16[1024,512]{1,0:T(8,128)(2,1)}, bf16[1024,512]{1,0:T(8,128)(2,1)}) custom-call(s32[5]{0:T(128)} %stack.41.place_ref.refs_1_.where_ref.refs_0_.refs_2_, s32[1,128]{1,0:T(1,128)} %add_bitcast_fusion.st_ref.refs_1_, bf16[64,768]{1,0:T(8,128)(2,1)} %slice.333.q_ref.refs_2_, ...), custom_call_target="tpu_custom_call" | custom-call | flops 1006632960 | bytes 4194304 | tf_op jit(solution)/shard_map/attend_backward/pallas_call | solution.py:266
  454.3 6.5 %dense_slice.2 = bf16[4,816,128]{2,1,0:T(8,128)(2,1)} custom-call(bf16[1024,512]{1,0:T(8,128)(2,1)} %copy-done.12, s32[5]{0:T(128)} %stack.41.place_ref.refs_1_.where_ref.refs_0_.refs_2_, f32[512,16]{1,0:T(8,128)} %get-tuple-element.93.refs_2_, f32[512,16]{1,0:T(8,128)} %get-tuple-element.94.refs_3_, f32[1,1536]{1,0:T(1,128)} %get-tuple-element.95.refs_4_, ...), custom_call_target="tpu_custom_call" | custom-call | flops 1610612736 | bytes 8388608 | tf_op jit(solution)/shard_map/dense_slice/pallas_call | solution.py:740
  463.5 4.9 collective-permute-done.85
  482.1 5.3 collective-permute-done.89.refs_0_.refs_19_
  490.5 5.2 act_back.3.refs_0_
  501.8 6.4 %dense_slice.3 = bf16[4,816,128]{2,1,0:T(8,128)(2,1)} custom-call(bf16[64,1536]{1,0:T(8,128)(2,1)} %act_back.3.refs_0_, s32[5]{0:T(128)} %stack.41.place_ref.refs_1_.where_ref.refs_0_.refs_2_, f32[512,16]{1,0:T(8,128)} %get-tuple-element.98.refs_2_, f32[512,16]{1,0:T(8,128)} %get-tuple-element.78.refs_9_.refs_3_, f32[1,1536]{1,0:T(1,128)} %get-tuple-element.99.refs_4_, ...), custom_call_target="tpu_custom_call" | custom-call | flops 1610612736 | bytes 8388608 | tf_op jit(solution)/shard_map/dense_slice/pallas_call | solution.py:740
  517.2 5.4 collective-permute-done.99
  540.9 25.5 %collective-permute-done.91 = bf16[64,1536]{1,0:T(8,128)(2,1)S(1)} collective-permute-done((bf16[64,1536]{1,0:T(8,128)(2,1)S(1)}, bf16[64,1536]{1,0:T(8,128)(2,1)S(1)}, u32[]{:S(2)}, u32[]{:S(2)}) %collective-permute-start.91) | collective-permute-done | bytes 196640 | tf_op jit(solution)/shard_map/ppermute | solution.py:32
  570.4 16.9 %all-gather.14.cloned.1.call-done = bf16[32,832,128]{2,1,0:T(8,128)(2,1)} async-done(((bf16[1,832,128]{2,1,0:T(8,128)(2,1)}), bf16[32,832,128]{2,1,0:T(8,128)(2,1)}) %all-gather.14.cloned.1.call-update) | async-done | bytes 6815760 | tf_op jit(solution)/shard_map/all_gather | solution.py:1055
  590.2 5.8 dense_rows.1
  (537 shorter events, 321.5 us)
Async XLA Ops:
  7.2 96.0 %all-gather.16.cloned.1.call-start = ((), (), s32[]{:S(2)}) async-start(), calls=%async_computation.5 | async-start | bytes 6488064 | tf_op jit(solution)/shard_map/all_gather | solution.py:892
  21.7 130.1 %all-gather.18.cloned.1.call-start = ((), (), s32[]{:S(2)}) async-start(), calls=%async_computation.6 | async-start | bytes 5898240 | tf_op jit(solution)/shard_map/all_gather | solution.py:822
  37.2 16.0 %collective-permute-start.6 = (bf16[256,512]{1,0:T(8,128)(2,1)S(1)}, bf16[256,512]{1,0:T(8,128)(2,1)}, u32[]{:S(2)}, u32[]{:S(2)}) collective-permute-start(bf16[256,512]{1,0:T(8,128)(2,1)S(1)} %pad_maximum_fusion.2.refs_0_.refs_8_), channel_id=1, source_target_pairs={{0,12},{2,14},{4,0},{6,2},{8,4},{10,6},{12,8},{14,10},{16,28},{18,... | collective-permute-start | bytes 786440 | tf_op jit(solution)/shard_map/ppermute | solution.py:28
  44.4 30.9 %collective-permute-start.18 = (bf16[4,384,256]{2,1,0:T(8,128)(2,1)}, bf16[4,384,256]{2,1,0:T(8,128)(2,1)}, u32[]{:S(2)}, u32[]{:S(2)}) collective-permute-start(bf16[4,384,256]{2,1,0:T(8,128)(2,1)} %side_by_side.1), channel_id=1, source_target_pairs={{0,64},{64,0},{1,65},{65,1},{2,66},{66,2},{3,67},{67,3},{4,68},{68... | collective-permute-start | bytes 2359304 | tf_op jit(solution)/shard_map/ppermute | solution.py:32
  47.0 16.5 %collective-permute-start.5 = (bf16[256,512]{1,0:T(8,128)(2,1)S(1)}, bf16[256,512]{1,0:T(8,128)(2,1)}, u32[]{:S(2)}, u32[]{:S(2)}) collective-permute-start(bf16[256,512]{1,0:T(8,128)(2,1)S(1)} %pad_maximum_fusion.2.refs_0_.refs_8_), channel_id=1, source_target_pairs={{0,8},{2,10},{4,12},{6,14},{8,0},{10,2},{12,4},{14,6},{16,24},{18,... | collective-permute-start | bytes 786440 | tf_op jit(solution)/shard_map/ppermute | solution.py:28
  48.7 17.0 %collective-permute-start.7 = (bf16[256,512]{1,0:T(8,128)(2,1)S(1)}, bf16[256,512]{1,0:T(8,128)(2,1)}, u32[]{:S(2)}, u32[]{:S(2)}) collective-permute-start(bf16[256,512]{1,0:T(8,128)(2,1)S(1)} %pad_maximum_fusion.2.refs_0_.refs_8_), channel_id=1, source_target_pairs={{0,2},{2,0},{4,6},{6,4},{8,10},{10,8},{12,14},{14,12},{16,18},{18,... | collective-permute-start | bytes 786440 | tf_op jit(solution)/shard_map/ppermute | solution.py:28
  53.2 22.0 %collective-permute-start.17 = (bf16[2,384,256]{2,1,0:T(8,128)(2,1)}, bf16[2,384,256]{2,1,0:T(8,128)(2,1)}, u32[]{:S(2)}, u32[]{:S(2)}) collective-permute-start(bf16[2,384,256]{2,1,0:T(8,128)(2,1)} %bitcast.166), channel_id=1, source_target_pairs={{0,64},{64,0},{1,65},{65,1},{2,66},{66,2},{3,67},{67,3},{4,68},{68... | collective-permute-start | bytes 1179656 | tf_op jit(solution)/shard_map/ppermute | solution.py:32
  77.7 172.4 %all-gather.20.cloned.1.call-start = ((), (), s32[]{:S(2)}) async-start(), calls=%async_computation.7 | async-start | bytes 5898240 | tf_op jit(solution)/shard_map/all_gather | solution.py:822
  105.6 257.8 %all-gather.22.cloned.1.call-start = ((), (), s32[]{:S(2)}) async-start(), calls=%async_computation.8 | async-start | bytes 5308416 | tf_op jit(solution)/shard_map/all_gather | solution.py:969
  111.1 23.4 %collective-permute-start.28 = (bf16[64,1664]{1,0:T(8,128)(2,1)S(1)}, bf16[64,1664]{1,0:T(8,128)(2,1)S(1)}, u32[]{:S(2)}, u32[]{:S(2)}) collective-permute-start(bf16[64,1664]{1,0:T(8,128)(2,1)S(1)} %fusion.23.refs_15_.refs_14_), channel_id=1, source_target_pairs={{0,12},{2,14},{4,0},{6,2},{8,4},{10,6},{12,8},{14,10},{16,28},{18,... | collective-permute-start | bytes 638984 | tf_op jit(solution)/shard_map/ppermute | solution.py:28
  113.1 22.9 %collective-permute-start.29 = (bf16[64,1664]{1,0:T(8,128)(2,1)S(1)}, bf16[64,1664]{1,0:T(8,128)(2,1)S(1)}, u32[]{:S(2)}, u32[]{:S(2)}) collective-permute-start(bf16[64,1664]{1,0:T(8,128)(2,1)S(1)} %fusion.23.refs_15_.refs_14_), channel_id=1, source_target_pairs={{0,2},{2,0},{4,6},{6,4},{8,10},{10,8},{12,14},{14,12},{16,18},{18,... | collective-permute-start | bytes 638984 | tf_op jit(solution)/shard_map/ppermute | solution.py:28
  116.1 21.6 %collective-permute-start.30 = (bf16[64,1664]{1,0:T(8,128)(2,1)S(1)}, bf16[64,1664]{1,0:T(8,128)(2,1)S(1)}, u32[]{:S(2)}, u32[]{:S(2)}) collective-permute-start(bf16[64,1664]{1,0:T(8,128)(2,1)S(1)} %collective-permute-done.26.refs_16_.refs_15_), channel_id=1, source_target_pairs={{0,2},{2,0},{4,6},{6,4},{8,10},{10,8},{12,14},{14,12},{16,18},{18,... | collective-permute-start | bytes 638984 | tf_op jit(solution)/shard_map/ppermute | solution.py:28
  122.2 16.7 %collective-permute-start.31 = (bf16[64,1664]{1,0:T(8,128)(2,1)S(1)}, bf16[64,1664]{1,0:T(8,128)(2,1)S(1)}, u32[]{:S(2)}, u32[]{:S(2)}) collective-permute-start(bf16[64,1664]{1,0:T(8,128)(2,1)S(1)} %collective-permute-done.27.refs_17_.refs_16_), channel_id=1, source_target_pairs={{0,2},{2,0},{4,6},{6,4},{8,10},{10,8},{12,14},{14,12},{16,18},{18,... | collective-permute-start | bytes 638984 | tf_op jit(solution)/shard_map/ppermute | solution.py:28
  122.3 24.2 %collective-permute-start.19 = (bf16[64,1536]{1,0:T(8,128)(2,1)}, bf16[64,1536]{1,0:T(8,128)(2,1)S(1)}, u32[]{:S(2)}, u32[]{:S(2)}) collective-permute-start(bf16[64,1536]{1,0:T(8,128)(2,1)} %multiply_convert_fusion.1.refs_0_.refs_7_), channel_id=1, source_target_pairs={{0,4},{2,6},{4,8},{6,10},{8,12},{10,14},{12,0},{14,2},{16,20},{18,... | collective-permute-start | bytes 589832 | tf_op jit(solution)/shard_map/ppermute | solution.py:28
  199.2 15.5 %collective-permute-start.42 = (bf16[256,512]{1,0:T(8,128)(2,1)S(1)}, bf16[256,512]{1,0:T(8,128)(2,1)S(1)}, u32[]{:S(2)}, u32[]{:S(2)}) collective-permute-start(bf16[256,512]{1,0:T(8,128)(2,1)S(1)} %pad_maximum_fusion.3.refs_0_.refs_8_), channel_id=1, source_target_pairs={{0,8},{2,10},{4,12},{6,14},{8,0},{10,2},{12,4},{14,6},{16,24},{18,... | collective-permute-start | bytes 786440 | tf_op jit(solution)/shard_map/ppermute | solution.py:28
  200.2 14.6 %collective-permute-start.43 = (bf16[256,512]{1,0:T(8,128)(2,1)S(1)}, bf16[256,512]{1,0:T(8,128)(2,1)S(1)}, u32[]{:S(2)}, u32[]{:S(2)}) collective-permute-start(bf16[256,512]{1,0:T(8,128)(2,1)S(1)} %pad_maximum_fusion.3.refs_0_.refs_8_), channel_id=1, source_target_pairs={{0,12},{2,14},{4,0},{6,2},{8,4},{10,6},{12,8},{14,10},{16,28},{18,... | collective-permute-start | bytes 786440 | tf_op jit(solution)/shard_map/ppermute | solution.py:28
  202.2 13.8 %collective-permute-start.44 = (bf16[256,512]{1,0:T(8,128)(2,1)S(1)}, bf16[256,512]{1,0:T(8,128)(2,1)S(1)}, u32[]{:S(2)}, u32[]{:S(2)}) collective-permute-start(bf16[256,512]{1,0:T(8,128)(2,1)S(1)} %pad_maximum_fusion.3.refs_0_.refs_8_), channel_id=1, source_target_pairs={{0,2},{2,0},{4,6},{6,4},{8,10},{10,8},{12,14},{14,12},{16,18},{18,... | collective-permute-start | bytes 786440 | tf_op jit(solution)/shard_map/ppermute | solution.py:28
  275.3 20.4 %collective-permute-start.59 = (bf16[128,1536]{1,0:T(8,128)(2,1)S(1)}, bf16[128,1536]{1,0:T(8,128)(2,1)S(1)}, u32[]{:S(2)}, u32[]{:S(2)}) collective-permute-start(bf16[128,1536]{1,0:T(8,128)(2,1)S(1)} %get-tuple-element.136), channel_id=1, source_target_pairs={{0,4},{2,6},{4,8},{6,10},{8,12},{10,14},{12,0},{14,2},{16,20},{18,... | collective-permute-start | bytes 1179656 | tf_op jit(solution)/shard_map/ppermute | solution.py:28
  296.6 95.6 %reduce-scatter.3.cloned.1.call-start = ((), (), s32[]{:S(2)}) async-start(), calls=%async_computation.2 | async-start | bytes 5898240 | tf_op jit(solution)/shard_map/reduce_scatter | solution.py:827
  297.2 157.0 %all-gather.24.cloned.1.call-start = ((), (), s32[]{:S(2)}) async-start(), calls=%async_computation.9 | async-start | bytes 3391488 | tf_op jit(solution)/shard_map/all_gather | solution.py:1025
  336.5 14.7 %collective-permute-start.65 = (bf16[256,512]{1,0:T(8,128)(2,1)S(1)}, bf16[256,512]{1,0:T(8,128)(2,1)S(1)}, u32[]{:S(2)}, u32[]{:S(2)}) collective-permute-start(bf16[256,512]{1,0:T(8,128)(2,1)S(1)} %get-tuple-element.142), channel_id=1, source_target_pairs={{0,4},{2,6},{4,8},{6,10},{8,12},{10,14},{12,0},{14,2},{16,20},{18,... | collective-permute-start | bytes 786440 | tf_op jit(solution)/shard_map/ppermute | solution.py:28
  362.7 114.3 %reduce-scatter.5.cloned.1.call-start = ((), (), s32[]{:S(2)}) async-start(), calls=%async_computation.3 | async-start | bytes 5898240 | tf_op jit(solution)/shard_map/reduce_scatter | solution.py:827
  407.5 93.6 %all-gather.26.cloned.1.call-start = ((), (), s32[]{:S(2)}) async-start(), calls=%async_computation.10 | async-start | bytes 1916928 | tf_op jit(solution)/shard_map/all_gather | solution.py:1028
  448.7 138.6 %all-gather.14.cloned.1.call-start = ((), (), s32[]{:S(2)}) async-start(), calls=%async_computation.4 | async-start | bytes 7028736 | tf_op jit(solution)/shard_map/all_gather | solution.py:1055
  453.4 15.0 %collective-permute-start.85 = (bf16[256,512]{1,0:T(8,128)(2,1)S(1)}, bf16[256,512]{1,0:T(8,128)(2,1)S(1)}, u32[]{:S(2)}, u32[]{:S(2)}) collective-permute-start(bf16[256,512]{1,0:T(8,128)(2,1)S(1)} %get-tuple-element.139), channel_id=1, source_target_pairs={{0,4},{2,6},{4,8},{6,10},{8,12},{10,14},{12,0},{14,2},{16,20},{18,... | collective-permute-start | bytes 786440 | tf_op jit(solution)/shard_map/ppermute | solution.py:28
  479.8 15.9 %collective-permute-start.94 = (bf16[64,1280]{1,0:T(8,128)(2,1)}, bf16[64,1280]{1,0:T(8,128)(2,1)S(1)}, u32[]{:S(2)}, u32[]{:S(2)}) collective-permute-start(bf16[64,1280]{1,0:T(8,128)(2,1)} %held_until.3.refs_2_.refs_18_), channel_id=1, source_target_pairs={{0,2},{2,0},{4,6},{6,4},{8,10},{10,8},{12,14},{14,12},{16,18},{18,... | collective-permute-start | bytes 491528 | tf_op jit(solution)/shard_map/ppermute | solution.py:28
  489.8 20.9 %collective-permute-start.101 = (bf16[816,128]{1,0:T(8,128)(2,1)S(1)}, bf16[816,128]{1,0:T(8,128)(2,1)S(1)}, u32[]{:S(2)}, u32[]{:S(2)}) collective-permute-start(bf16[816,128]{1,0:T(8,128)(2,1)S(1)} %get-tuple-element.146), channel_id=1, source_target_pairs={{0,48},{2,50},{4,52},{6,54},{8,56},{10,58},{12,60},{14,62},{16,0},... | collective-permute-start | bytes 626696 | tf_op jit(solution)/shard_map/ppermute | solution.py:28
  495.7 16.5 %collective-permute-start.102 = (bf16[816,128]{1,0:T(8,128)(2,1)S(1)}, bf16[816,128]{1,0:T(8,128)(2,1)S(1)}, u32[]{:S(2)}, u32[]{:S(2)}) collective-permute-start(bf16[816,128]{1,0:T(8,128)(2,1)S(1)} %get-tuple-element.148), channel_id=1, source_target_pairs={{0,32},{2,34},{4,36},{6,38},{8,40},{10,42},{12,44},{14,46},{16,48}... | collective-permute-start | bytes 626696 | tf_op jit(solution)/shard_map/ppermute | solution.py:28
  496.0 17.8 %collective-permute-start.103 = (bf16[816,128]{1,0:T(8,128)(2,1)S(1)}, bf16[816,128]{1,0:T(8,128)(2,1)S(1)}, u32[]{:S(2)}, u32[]{:S(2)}) collective-permute-start(bf16[816,128]{1,0:T(8,128)(2,1)S(1)} %get-tuple-element.147), channel_id=1, source_target_pairs={{0,16},{2,18},{4,20},{6,22},{8,24},{10,26},{12,28},{14,30},{16,32}... | collective-permute-start | bytes 626696 | tf_op jit(solution)/shard_map/ppermute | solution.py:28
  496.9 17.0 %collective-permute-start.90 = (bf16[64,1536]{1,0:T(8,128)(2,1)}, bf16[64,1536]{1,0:T(8,128)(2,1)S(1)}, u32[]{:S(2)}, u32[]{:S(2)}) collective-permute-start(bf16[64,1536]{1,0:T(8,128)(2,1)} %act_back.3.refs_0_), channel_id=1, source_target_pairs={{0,1},{1,0},{2,3},{3,2},{4,5},{5,4},{6,7},{7,6},{8,9},{9,8},{10,11... | collective-permute-start | bytes 589832 | tf_op jit(solution)/shard_map/ppermute | solution.py:32
  537.2 30.2 %collective-permute-start.107 = (bf16[2304,256]{1,0:T(8,128)(2,1)S(1)}, bf16[2304,256]{1,0:T(8,128)(2,1)S(1)}, u32[]{:S(2)}, u32[]{:S(2)}) collective-permute-start(bf16[2304,256]{1,0:T(8,128)(2,1)S(1)} %broadcast_select_fusion), channel_id=1, source_target_pairs={{0,64},{64,0},{1,65},{65,1},{2,66},{66,2},{3,67},{67,3},{4,68},{68... | collective-permute-start | bytes 3538952 | tf_op jit(solution)/shard_map/ppermute | solution.py:32
  539.2 27.2 %collective-permute-start.91 = (bf16[64,1536]{1,0:T(8,128)(2,1)S(1)}, bf16[64,1536]{1,0:T(8,128)(2,1)S(1)}, u32[]{:S(2)}, u32[]{:S(2)}) collective-permute-start(bf16[64,1536]{1,0:T(8,128)(2,1)S(1)} %get-tuple-element.118), channel_id=1, source_target_pairs={{0,64},{64,0},{1,65},{65,1},{2,66},{66,2},{3,67},{67,3},{4,68},{68... | collective-permute-start | bytes 589832 | tf_op jit(solution)/shard_map/ppermute | solution.py:32
  (180 other events, 1485.6 us)
Sparse Core Ops, SparseCore 0:
  21.9 55.4 all-gather.15
  79.6 51.0 all-gather.17
  132.9 53.0 all-gather.19
  296.7 31.8 all-gather.21
  331.5 54.2 reduce-scatter.2
  387.3 27.3 all-gather.23
  417.6 54.3 reduce-scatter.4
  474.3 26.7 all-gather.25
  537.2 50.0 all-gather.13

commit v5 on v4

--- a/solution.py
+++ b/solution.py
@@ -756,7 +756,7 @@
     )(*earlier, where, gated, gates, gains, *[left] * 4, *[tokens] * 4, *[right] * 5, *pieces)
 
 
-def dense_rows_kernel(in_ref, q_ref, k_ref, v_ref, out_ref, router_ref, gains_ref, first_ref, held_ref):
+def dense_rows_kernel(in_ref, q_ref, k_ref, v_ref, out_ref, router_ref, gains_ref, held_ref):
     j = pl.program_id(0)
     for x in range(4):
         rows = slice(x * 48, (x + 1) * 48)
@@ -768,18 +768,6 @@
             out_ref[:, lanes] = in_ref[x, 0, 480 + c * 112 : 576 + c * 112].astype(F32)
             held_ref[j, :, lanes] = in_ref[x, 0, 576 + c * 112 : 592 + c * 112].astype(F32)
 
-    own = in_ref[0, 0, 816:832].astype(F32)
-    for x in range(1, 4):
-        own = own + in_ref[x, 0, 816:832].astype(F32)
-
-    @pl.when(j == 0)
-    def _():
-        first_ref[...] = own
-
-    @pl.when(j != 0)
-    def _():
-        first_ref[...] = first_ref[...] + own
-
     @pl.when(j == 7)
     def _():
         held = held_ref[...]
@@ -793,11 +781,10 @@
     return pl.pallas_call(
         dense_rows_kernel,
         grid=(8,),
-        in_specs=[pl.BlockSpec((4, 1, 832, 128), lambda j: (0, j, 0, 0))],
-        out_specs=[rows(192, 768), rows(192, 256), rows(192, 256), rows(96, D), whole(16, D), whole(16, D), whole(16, 128)],
+        in_specs=[pl.BlockSpec((4, 1, 816, 128), lambda j: (0, j, 0, 0))],
+        out_specs=[rows(192, 768), rows(192, 256), rows(192, 256), rows(96, D), whole(16, D), whole(16, D)],
         out_shape=[shaped(D, 768, dtype=F32), shaped(D, 256, dtype=F32), shaped(D, 256, dtype=F32)]
-        + [shaped(768, D, dtype=F32), shaped(16, D, dtype=F32), shaped(16, D, dtype=F32)]
-        + [shaped(16, 128, dtype=F32)],
+        + [shaped(768, D, dtype=F32), shaped(16, D, dtype=F32), shaped(16, D, dtype=F32)],
         scratch_shapes=[pltpu.VMEM((8, 16, D), F32)],
         compiler_params=params(28),
         cost_estimate=cost(0, 20 << 20),
@@ -960,12 +947,13 @@
             branch = tensor_sum(made)
             rest = (gates, (pre, mid))
         else:
+            lefts = held_until(lefts, *tokens[1:])
             near, far, gates, gated, tokens, weight_grads = last_experts(
                 where, tokens, given_all, routers[1], expert_weights[1]
             )
             both = (near.astype(F32) + moved(far, 0, 0, 1).astype(F32)).astype(BF)
             low = back_y(both).reshape(2 * rows, D).astype(BF)
-            lefts = held_until(lefts, low)
+            weight_grads = held_until(weight_grads, low)
             lefts = lax.all_gather(lefts, "dp", axis=0, axis_index_groups=Y_GROUPS).reshape(8 * rows, 4608)
             got = swapped(low, "tensor")
             branch = low[:rows].astype(F32) + got[:rows].astype(F32)
@@ -984,6 +972,7 @@
     def over_sections(a, b):
         return own_of(a, b).astype(F32) + from_other(a, b)
 
+    early_sent = own_of(saved[1][9], saved[0][9]).astype(BF)
     grad_output = given.astype(F32)
     grads = []
     for layer in (1, 0):
@@ -1010,12 +999,16 @@
         if layer == 0:
             late = dense_slice(1, *grads[0][1], [], both)
             half = behind(half, late)
+            late = back_x(late.reshape(4 * 816, 128)).reshape(816, 128)
         grad_pair = back_x(half.astype(BF)).reshape(rows, 512).astype(BF)
         grad_qkv = jnp.concatenate([grad_query, grad_pair], axis=1)
         if layer == 0:
-            grad_qkv = held_until(grad_qkv, expert_part)
+            grad_qkv = held_until(grad_qkv, expert_part, late)
             right_pieces = group_pieces(grad_qkv)
-        partial = act_back(layer, where, grad_qkv, weights_in, dense_all, lefts if layer == 1 else right_pieces[1])
+            right = lax.all_gather(right, "dp", axis=0, axis_index_groups=Y_GROUPS).reshape(8 * rows, 1664)
+            results_sent = swapped(held_until(early_sent, both), "section")
+            blocks = dense_slice(0, where, lefts, gated, gates, gain_two_grad, tokens, right, right_pieces, results_sent)
+        partial = act_back(layer, where, grad_qkv, weights_in, dense_all, *([lefts] if layer == 1 else []))
         grad_activation = partial.astype(F32) + swapped(partial, "tensor").astype(F32)
         grad_from_first, gain_one_grad = norm_back(hidden, gain_one, grad_activation)
         grad_input = grad_middle + grad_from_first
@@ -1025,9 +1018,6 @@
             right = lax.all_gather(right, "dp", axis=0, axis_index_groups=Y_GROUPS).reshape(8 * rows, 2944)
             grads.append((grad_input, (where, lefts, gated, gates, gain_two_grad, tokens, right), expert_part, gain_one_grad))
         else:
-            right = lax.all_gather(right, "dp", axis=0, axis_index_groups=Y_GROUPS).reshape(8 * rows, 1664)
-            blocks = dense_slice(0, where, lefts, gated, gates, gain_two_grad, tokens, right, right_pieces, partial)
-            late = back_x(late.reshape(4 * 816, 128)).reshape(816, 128)
             grads.append((grad_input, back_x(blocks.reshape(4 * 816, 128)).reshape(816, 128), expert_part, gain_one_grad))
         grad_output = grad_input
     grads = grads[::-1]
@@ -1035,7 +1025,7 @@
     def by_batch(own, other):
         return jnp.stack([jnp.where(first, own, other), jnp.where(first, other, own)])[None]
 
-    results = by_batch(own_of(saved[0][9], saved[1][9]), from_other(saved[0][9], saved[1][9]))
+    results = by_batch(own_of(saved[0][9], saved[1][9]), results_sent.astype(F32))
     input_grads = by_batch(own_of(grads[0][0], grads[1][0]), from_other(grads[0][0], grads[1][0]))
     first_part = grads[0][1]
 
@@ -1046,19 +1036,23 @@
     across = lax.ppermute(
         own_of(extras(late), extras(first_part)).astype(BF), ("section", "tensor"), [(0, 3), (1, 2), (2, 1), (3, 0)]
     ).astype(F32)
-    gain_rows = [jnp.pad(g[3].reshape(12, 128), ((0, 4), (0, 0))) for g in grads]
-    block = over_sections(*[jnp.concatenate(pair, axis=0) for pair in ((first_part, gain_rows[0]), (late, gain_rows[1]))])
+    block = over_sections(first_part, late)
     more = own_of(straight[:6], straight[6:]) + across
-    wide = block[480:816].reshape(3, 112, 128)
+    wide = block[480:].reshape(3, 112, 128)
     wide = wide + jnp.pad(more.reshape(3, 2, 128), ((0, 0), (96, 14), (0, 0)))
-    block = jnp.concatenate([block[:480], wide.reshape(336, 128), block[816:]], axis=0).astype(BF)
-    everything = lax.all_gather(block, "dp", axis=0).reshape(4, 8, 832, 128)
-    query_sum, key_sum, value_sum, out_full, router_sum, gains, gain_one_sum = dense_rows(everything)
-    expert_sum = over_sections(grads[0][2], grads[1][2]).reshape(3, 2, 384, 256)
+    block = jnp.concatenate([block[:480], wide.reshape(336, 128)], axis=0).astype(BF)
+    everything = lax.all_gather(block, "dp", axis=0).reshape(4, 8, 816, 128)
+    query_sum, key_sum, value_sum, out_full, router_sum, gains = dense_rows(everything)
+    gain_sent = from_other(grads[0][3], grads[1][3])
+    gain_one_sum = (own_of(grads[0][3], grads[1][3]) + gain_sent).astype(BF)
+    gain_one_sum = jnp.sum(lax.all_gather(gain_one_sum, "dp", axis=0).astype(F32), axis=0)[None]
+    expert_sent = swapped(behind(own_of(grads[1][2], grads[0][2]), gain_sent), "section")
+    expert_sum = own_of(grads[0][2], grads[1][2]).astype(F32) + expert_sent.astype(F32)
+    expert_sum = expert_sum.reshape(3, 2, 384, 256)
     return (
         results,
         input_grads,
-        gain_one_sum[:12].reshape(1, D),
+        gain_one_sum,
         query_sum[None],
         key_sum[None],
         value_sum[None],

time: 609 us -> 610 us (level)
  waiting for transfers between devices: 230 us -> 178 us
  blocking collectives: 0 us -> 27.6 us
  starting transfers between devices: 156 us -> 178 us
    ppermute x15 -> x16, waiting for transfers between devices: 69.1 us -> 37.1 us  [swapped(): return lax.ppermute(value, axis, [(0, 1), (1, 0)])]
    all_gather x0 -> x1, blocking collectives: none -> 27.6 us  [per_device(): lax.all_gather(gain_one_sum, 'dp', axis=0).astype(F32)]
    all_gather x1, waiting for transfers between devices: 16.9 us -> 0.01 us  [per_device(): everything = lax.all_gather(block, 'dp', axis=0).reshape(4, 8, 816, 128)]
    ppermute x15 -> x16, starting transfers between devices: 18 us -> 26.5 us  [swapped(): return lax.ppermute(value, axis, [(0, 1), (1, 0)])]
    ppermute x87, starting transfers between devices: 126 us -> 134 us  [moved(): return lax.ppermute(value, 'dp', route)]
    unnamed x193 -> x188, local copies, waits for them, and re-layouts: 18.1 us -> 18 us
  transfers between devices with their start and end apart: 117 -> 118, of which waited for: 57 -> 59; matrix products, arithmetic and copies ran while one was open for 9% -> 10% of each run, Pallas kernels for 16% -> 17%
where the time goes in v5:
time: 610 us; the launch traced here: 604 us
  starting transfers between devices  178 us (29%)
  waiting for transfers between devices  178 us (29%)
  Pallas kernels  116 us (19%)
  local copies, waits for them, and re-layouts  40.6 us (7%)
  other arithmetic  39.8 us (7%)
  blocking collectives  27.6 us (5%)
  between operations  19.3 us (3%)
    ppermute x87, starting transfers between devices, moved(): return lax.ppermute(value, 'dp', route)  134 us
    ppermute x87, waiting for transfers between devices, moved(): return lax.ppermute(value, 'dp', route)  130 us
    ppermute x16, waiting for transfers between devices, swapped(): return lax.ppermute(value, axis, [(0, 1), (1, 0)])  37.1 us
    all_gather x1, blocking collectives, per_device(): lax.all_gather(gain_one_sum, 'dp', axis=0).astype(F32)  27.6 us
    ppermute x16, starting transfers between devices, swapped(): return lax.ppermute(value, axis, [(0, 1), (1, 0)])  26.5 us
    unnamed x188, local copies, waits for them, and re-layouts  18 us
    pallas_call x1, Pallas kernels, last_experts(): pl.pallas_call(ignoring(len(earlier), last_expert_kernel), grid=(1,), in_...  16.6 us
    pallas_call x2, Pallas kernels, attend_backward(): pl.pallas_call(ignoring(len(earlier), attend_back_kernel), grid=(2,), in_...  16.4 us
  transfers between devices with their start and end apart: 118, of which 59 were waited for; matrix products, arithmetic and copies ran while one was open for 10% of the time, Pallas kernels for 17%

profile of v5, /device:TPU:1, one launch (start us, length us, event | category | flops | bytes accessed | tf_op | source)
XLA Modules:
  0.0 604.3 jit_solution(9274527624759778118)
XLA Ops:
  47.9 5.0 collective-permute-start.7
  56.5 7.8 %collective-permute-start.10 = (bf16[256,512]{1,0:T(8,128)(2,1)}, bf16[256,512]{1,0:T(8,128)(2,1)}, u32[]{:S(2)}, u32[]{:S(2)}) collective-permute-start(bf16[256,512]{1,0:T(8,128)(2,1)} %collective-permute-done.6.refs_3_.refs_11_), channel_id=1, source_target_pairs={{0,2},{2,0},{4,6},{6,4},{8,10},{10,8},{12,14},{14,12},{16,18},{18,... | collective-permute-start | bytes 786440 | tf_op jit(solution)/shard_map/ppermute | solution.py:28
  70.4 6.3 %attend_forward.2 = (bf16[64,768]{1,0:T(8,128)(2,1)}, f32[2,1,384]{2,1,0:T(1,128)}, bf16[1024,512]{1,0:T(8,128)(2,1)}, bf16[1024,512]{1,0:T(8,128)(2,1)}) custom-call(s32[5]{0:T(128)} %stack.41.place_ref.refs_1_.where_ref.refs_0_.refs_2_, s32[1,128]{1,0:T(1,128)} %add_bitcast_fusion.st_ref.refs_1_, bf16[64,768]{1,0:T(8,128)(2,1)} %slice.328.q_ref.refs_2_, ...), custom_call_target="tpu_custom_call" | custom-call | flops 402653184 | bytes 2097152 | tf_op jit(solution)/shard_map/attend_forward/pallas_call | solution.py:225
  90.9 7.0 %collective-permute-start.14 = (bf16[64,1536]{1,0:T(8,128)(2,1)S(1)}, bf16[64,1536]{1,0:T(8,128)(2,1)S(1)}, u32[]{:S(2)}, u32[]{:S(2)}) collective-permute-start(bf16[64,1536]{1,0:T(8,128)(2,1)S(1)} %get-tuple-element.161), channel_id=1, source_target_pairs={{0,65},{1,64},{2,67},{3,66},{4,69},{5,68},{6,71},{7,70},{8,73},{9,... | collective-permute-start | bytes 589832 | tf_op jit(solution)/shard_map/ppermute | solution.py:927
  122.5 5.1 collective-permute-start.30
  127.7 12.3 %collective-permute-start.19 = (bf16[64,1536]{1,0:T(8,128)(2,1)}, bf16[64,1536]{1,0:T(8,128)(2,1)S(1)}, u32[]{:S(2)}, u32[]{:S(2)}) collective-permute-start(bf16[64,1536]{1,0:T(8,128)(2,1)} %multiply_convert_fusion.1.refs_0_.refs_7_), channel_id=1, source_target_pairs={{0,4},{2,6},{4,8},{6,10},{8,12},{10,14},{12,0},{14,2},{16,20},{18,... | collective-permute-start | bytes 589832 | tf_op jit(solution)/shard_map/ppermute | solution.py:28
  143.7 8.3 %collective-permute-done.19.refs_8_ = bf16[64,1536]{1,0:T(8,128)(2,1)S(1)} collective-permute-done((bf16[64,1536]{1,0:T(8,128)(2,1)}, bf16[64,1536]{1,0:T(8,128)(2,1)S(1)}, u32[]{:S(2)}, u32[]{:S(2)}) %collective-permute-start.19) | collective-permute-done | bytes 196640 | tf_op jit(solution)/shard_map/ppermute | solution.py:28
  157.3 8.5 %experts_forward.1 = (bf16[256,1536]{1,0:T(8,128)(2,1)}, bf16[256,1536]{1,0:T(8,128)(2,1)}, bf16[512,1024]{1,0:T(8,128)(2,1)}, bf16[512,512]{1,0:T(8,128)(2,1)},...) custom-call(bf16[6,384,256]{2,1,0:T(8,128)(2,1)} %choose.2.refs_0_, s32[5]{0:T(128)} %stack.41.place_ref.refs_1_.where_ref.refs_0_.refs_2_, ...), custom_call_target="tpu_custom_call" | custom-call | flops 2415919104 | bytes 10485760 | tf_op jit(solution)/shard_map/experts_forward/pallas_call | solution.py:537
  215.6 5.5 collective-permute-start.45
  223.7 7.9 %attend_forward.3 = (bf16[64,768]{1,0:T(8,128)(2,1)}, f32[2,1,384]{2,1,0:T(1,128)}, bf16[1024,512]{1,0:T(8,128)(2,1)}, bf16[1024,512]{1,0:T(8,128)(2,1)}, bf16[6...) custom-call(s32[5]{0:T(128)} %stack.41.place_ref.refs_1_.where_ref.refs_0_.refs_2_, ...), custom_call_target="tpu_custom_call" | custom-call | flops 402653184 | bytes 2097152 | tf_op jit(solution)/shard_map/attend_forward/pallas_call | solution.py:225
  233.4 6.1 %collective-permute-done.48 = bf16[64,1536]{1,0:T(8,128)(2,1)S(1)} collective-permute-done((bf16[64,1536]{1,0:T(8,128)(2,1)}, bf16[64,1536]{1,0:T(8,128)(2,1)S(1)}, u32[]{:S(2)}, u32[]{:S(2)}) %collective-permute-start.48) | collective-permute-done | bytes 196640 | tf_op jit(solution)/shard_map/ppermute | solution.py:32
  258.4 16.6 %last_experts.1 = (bf16[512,1536]{1,0:T(8,128)(2,1)}, bf16[512,1536]{1,0:T(8,128)(2,1)}, f32[512,16]{1,0:T(8,128)}, f32[512,16]{1,0:T(8,128)}, bf16[512,1536]{1,...) custom-call(s32[5]{0:T(128)} %stack.41.place_ref.refs_1_.where_ref.refs_0_.refs_2_, ...), custom_call_target="tpu_custom_call" | custom-call | flops 4831838208 | bytes 16777216 | tf_op jit(solution)/shard_map/last_experts/pallas_call | solution.py:673
  283.3 11.3 %collective-permute-done.57 = bf16[128,1536]{1,0:T(8,128)(2,1)S(1)} collective-permute-done((bf16[128,1536]{1,0:T(8,128)(2,1)S(1)}, bf16[128,1536]{1,0:T(8,128)(2,1)S(1)}, u32[]{:S(2)}, u32[]{:S(2)}) %collective-permute-start.57) | collective-permute-done | bytes 393248 | tf_op jit(solution)/shard_map/ppermute | solution.py:28
  295.4 8.3 %collective-permute-done.59 = bf16[128,1536]{1,0:T(8,128)(2,1)S(1)} collective-permute-done((bf16[128,1536]{1,0:T(8,128)(2,1)S(1)}, bf16[128,1536]{1,0:T(8,128)(2,1)S(1)}, u32[]{:S(2)}, u32[]{:S(2)}) %collective-permute-start.59) | collective-permute-done | bytes 393248 | tf_op jit(solution)/shard_map/ppermute | solution.py:28
  309.4 7.8 %collective-permute-done.60 = bf16[128,1536]{1,0:T(8,128)(2,1)S(1)} collective-permute-done((bf16[128,1536]{1,0:T(8,128)(2,1)S(1)}, bf16[128,1536]{1,0:T(8,128)(2,1)S(1)}, u32[]{:S(2)}, u32[]{:S(2)}) %collective-permute-start.60) | collective-permute-done | bytes 393248 | tf_op jit(solution)/shard_map/ppermute | solution.py:32
  318.9 4.6 middle_back.2
  323.5 8.2 %attend_backward.2 = (bf16[64,768]{1,0:T(8,128)(2,1)}, bf16[1024,512]{1,0:T(8,128)(2,1)}, bf16[1024,512]{1,0:T(8,128)(2,1)}) custom-call(s32[5]{0:T(128)} %stack.41.place_ref.refs_1_.where_ref.refs_0_.refs_2_, s32[1,128]{1,0:T(1,128)} %add_bitcast_fusion.st_ref.refs_1_, bf16[64,768]{1,0:T(8,128)(2,1)} %slice.269.q_ref.refs_2_, ...), custom_call_target="tpu_custom_call" | custom-call | flops 1006632960 | bytes 4194304 | tf_op jit(solution)/shard_map/attend_backward/pallas_call | solution.py:266
  340.5 4.7 collective-permute-done.62
  347.9 6.7 %collective-permute-done.64 = bf16[256,512]{1,0:T(8,128)(2,1)S(1)} collective-permute-done((bf16[256,512]{1,0:T(8,128)(2,1)S(1)}, bf16[256,512]{1,0:T(8,128)(2,1)S(1)}, u32[]{:S(2)}, u32[]{:S(2)}) %collective-permute-start.64) | collective-permute-done | bytes 262176 | tf_op jit(solution)/shard_map/ppermute | solution.py:28
  364.5 5.2 act_back.2
  400.1 13.2 %experts_backward.1 = (bf16[256,1536]{1,0:T(8,128)(2,1)}, bf16[256,1536]{1,0:T(8,128)(2,1)}, f32[512,16]{1,0:T(8,128)}, bf16[4,6,384,256]{3,2,1,0:T(8,128)(2,1)}) custom-call(bf16[64,2944]{1,0:T(8,128)(2,1)} %pad_maximum_fusion.refs_0_, bf16[2304,256]{1,0:T(8,128)(2,1)} %reduce-scatter.3.cloned.1.call-done.refs_1_, ...), custom_call_target="tpu_custom_call" | custom-call | flops 2415919104 | bytes 10485760 | tf_op jit(solution)/shard_map/experts_backward/pallas_call | solution.py:600
  425.3 5.3 collective-permute-done.79
  434.0 4.7 collective-permute-done.80.got_ref
  439.5 4.7 middle_back.3
  444.1 8.2 %attend_backward.3 = (bf16[64,768]{1,0:T(8,128)(2,1)}, bf16[1024,512]{1,0:T(8,128)(2,1)}, bf16[1024,512]{1,0:T(8,128)(2,1)}) custom-call(s32[5]{0:T(128)} %stack.41.place_ref.refs_1_.where_ref.refs_0_.refs_2_, s32[1,128]{1,0:T(1,128)} %add_bitcast_fusion.st_ref.refs_1_, bf16[64,768]{1,0:T(8,128)(2,1)} %slice.328.q_ref.refs_2_, ...), custom_call_target="tpu_custom_call" | custom-call | flops 1006632960 | bytes 4194304 | tf_op jit(solution)/shard_map/attend_backward/pallas_call | solution.py:266
  460.1 6.5 %dense_slice.2 = bf16[4,816,128]{2,1,0:T(8,128)(2,1)} custom-call(bf16[1024,512]{1,0:T(8,128)(2,1)} %copy-done.9, s32[5]{0:T(128)} %stack.41.place_ref.refs_1_.where_ref.refs_0_.refs_2_, f32[512,16]{1,0:T(8,128)} %get-tuple-element.92.refs_2_, f32[512,16]{1,0:T(8,128)} %get-tuple-element.93.refs_3_, f32[1,1536]{1,0:T(1,128)} %get-tuple-element.94.refs_4_, ...), custom_call_target="tpu_custom_call" | custom-call | flops 1610612736 | bytes 8388608 | tf_op jit(solution)/shard_map/dense_slice/pallas_call | solution.py:740
  478.7 5.8 collective-permute-done.91
  502.7 6.5 %dense_slice.3 = bf16[4,816,128]{2,1,0:T(8,128)(2,1)} custom-call(bf16[64,1536]{1,0:T(8,128)(2,1)} %copy-done.40, s32[5]{0:T(128)} %stack.41.place_ref.refs_1_.where_ref.refs_0_.refs_2_, f32[512,16]{1,0:T(8,128)} %get-tuple-element.97.refs_2_, f32[512,16]{1,0:T(8,128)} %get-tuple-element.77.refs_9_.refs_3_, f32[1,1536]{1,0:T(1,128)} %get-tuple-element.98.refs_4_, ...), custom_call_target="tpu_custom_call" | custom-call | flops 1610612736 | bytes 8388608 | tf_op jit(solution)/shard_map/dense_slice/pallas_call | solution.py:740
  519.8 4.8 collective-permute-done.104
  536.8 5.2 act_back.3
  555.9 27.6 %all-gather.7 = bf16[32,1,1536]{2,1,0:T(2,128)(2,1)S(1)} all-gather(bf16[1,1,1536]{2,1,0:T(2,128)(2,1)S(1)} %reshape.287), channel_id=7, replica_groups=mesh['section'=2,'dp'=32,'tensor'=2] {'dp'}, dimensions={0}, use_global_device_ids=true | all-gather | bytes 101376 | tf_op jit(solution)/shard_map/all_gather | solution.py:1048
  591.2 5.8 dense_rows.1
  (541 shorter events, 333.5 us)
Async XLA Ops:
  7.2 101.6 %all-gather.18.cloned.1.call-start = ((), (), s32[]{:S(2)}) async-start(), calls=%async_computation.5 | async-start | bytes 6488064 | tf_op jit(solution)/shard_map/all_gather | solution.py:879
  20.1 137.2 %all-gather.20.cloned.1.call-start = ((), (), s32[]{:S(2)}) async-start(), calls=%async_computation.6 | async-start | bytes 5898240 | tf_op jit(solution)/shard_map/all_gather | solution.py:809
  37.5 15.4 %collective-permute-start.6 = (bf16[256,512]{1,0:T(8,128)(2,1)S(1)}, bf16[256,512]{1,0:T(8,128)(2,1)}, u32[]{:S(2)}, u32[]{:S(2)}) collective-permute-start(bf16[256,512]{1,0:T(8,128)(2,1)S(1)} %pad_maximum_fusion.2.refs_0_.refs_8_), channel_id=1, source_target_pairs={{0,12},{2,14},{4,0},{6,2},{8,4},{10,6},{12,8},{14,10},{16,28},{18,... | collective-permute-start | bytes 786440 | tf_op jit(solution)/shard_map/ppermute | solution.py:28
  43.8 32.9 %collective-permute-start.18 = (bf16[4,384,256]{2,1,0:T(8,128)(2,1)}, bf16[4,384,256]{2,1,0:T(8,128)(2,1)}, u32[]{:S(2)}, u32[]{:S(2)}) collective-permute-start(bf16[4,384,256]{2,1,0:T(8,128)(2,1)} %side_by_side.1), channel_id=1, source_target_pairs={{0,64},{64,0},{1,65},{65,1},{2,66},{66,2},{3,67},{67,3},{4,68},{68... | collective-permute-start | bytes 2359304 | tf_op jit(solution)/shard_map/ppermute | solution.py:32
  46.4 17.9 %collective-permute-start.5 = (bf16[256,512]{1,0:T(8,128)(2,1)S(1)}, bf16[256,512]{1,0:T(8,128)(2,1)}, u32[]{:S(2)}, u32[]{:S(2)}) collective-permute-start(bf16[256,512]{1,0:T(8,128)(2,1)S(1)} %pad_maximum_fusion.2.refs_0_.refs_8_), channel_id=1, source_target_pairs={{0,8},{2,10},{4,12},{6,14},{8,0},{10,2},{12,4},{14,6},{16,24},{18,... | collective-permute-start | bytes 786440 | tf_op jit(solution)/shard_map/ppermute | solution.py:28
  47.9 19.2 %collective-permute-start.7 = (bf16[256,512]{1,0:T(8,128)(2,1)S(1)}, bf16[256,512]{1,0:T(8,128)(2,1)}, u32[]{:S(2)}, u32[]{:S(2)}) collective-permute-start(bf16[256,512]{1,0:T(8,128)(2,1)S(1)} %pad_maximum_fusion.2.refs_0_.refs_8_), channel_id=1, source_target_pairs={{0,2},{2,0},{4,6},{6,4},{8,10},{10,8},{12,14},{14,12},{16,18},{18,... | collective-permute-start | bytes 786440 | tf_op jit(solution)/shard_map/ppermute | solution.py:28
  53.0 23.7 %collective-permute-start.17 = (bf16[2,384,256]{2,1,0:T(8,128)(2,1)}, bf16[2,384,256]{2,1,0:T(8,128)(2,1)}, u32[]{:S(2)}, u32[]{:S(2)}) collective-permute-start(bf16[2,384,256]{2,1,0:T(8,128)(2,1)} %bitcast.158), channel_id=1, source_target_pairs={{0,64},{64,0},{1,65},{65,1},{2,66},{66,2},{3,67},{67,3},{4,68},{68... | collective-permute-start | bytes 1179656 | tf_op jit(solution)/shard_map/ppermute | solution.py:32
  79.1 179.4 %all-gather.22.cloned.1.call-start = ((), (), s32[]{:S(2)}) async-start(), calls=%async_computation.7 | async-start | bytes 5898240 | tf_op jit(solution)/shard_map/all_gather | solution.py:809
  90.9 15.3 %collective-permute-start.14 = (bf16[64,1536]{1,0:T(8,128)(2,1)S(1)}, bf16[64,1536]{1,0:T(8,128)(2,1)S(1)}, u32[]{:S(2)}, u32[]{:S(2)}) collective-permute-start(bf16[64,1536]{1,0:T(8,128)(2,1)S(1)} %get-tuple-element.161), channel_id=1, source_target_pairs={{0,65},{1,64},{2,67},{3,66},{4,69},{5,68},{6,71},{7,70},{8,73},{9,... | collective-permute-start | bytes 589832 | tf_op jit(solution)/shard_map/ppermute | solution.py:927
  111.1 253.3 %all-gather.24.cloned.1.call-start = ((), (), s32[]{:S(2)}) async-start(), calls=%async_computation.8 | async-start | bytes 5308416 | tf_op jit(solution)/shard_map/all_gather | solution.py:957
  115.7 24.4 %collective-permute-start.28 = (bf16[64,1664]{1,0:T(8,128)(2,1)S(1)}, bf16[64,1664]{1,0:T(8,128)(2,1)S(1)}, u32[]{:S(2)}, u32[]{:S(2)}) collective-permute-start(bf16[64,1664]{1,0:T(8,128)(2,1)S(1)} %fusion.23.refs_15_.refs_14_), channel_id=1, source_target_pairs={{0,12},{2,14},{4,0},{6,2},{8,4},{10,6},{12,8},{14,10},{16,28},{18,... | collective-permute-start | bytes 638984 | tf_op jit(solution)/shard_map/ppermute | solution.py:28
  117.7 24.0 %collective-permute-start.29 = (bf16[64,1664]{1,0:T(8,128)(2,1)S(1)}, bf16[64,1664]{1,0:T(8,128)(2,1)S(1)}, u32[]{:S(2)}, u32[]{:S(2)}) collective-permute-start(bf16[64,1664]{1,0:T(8,128)(2,1)S(1)} %fusion.23.refs_15_.refs_14_), channel_id=1, source_target_pairs={{0,2},{2,0},{4,6},{6,4},{8,10},{10,8},{12,14},{14,12},{16,18},{18,... | collective-permute-start | bytes 638984 | tf_op jit(solution)/shard_map/ppermute | solution.py:28
  122.5 20.3 %collective-permute-start.30 = (bf16[64,1664]{1,0:T(8,128)(2,1)S(1)}, bf16[64,1664]{1,0:T(8,128)(2,1)S(1)}, u32[]{:S(2)}, u32[]{:S(2)}) collective-permute-start(bf16[64,1664]{1,0:T(8,128)(2,1)S(1)} %collective-permute-done.26.refs_16_.refs_15_), channel_id=1, source_target_pairs={{0,2},{2,0},{4,6},{6,4},{8,10},{10,8},{12,14},{14,12},{16,18},{18,... | collective-permute-start | bytes 638984 | tf_op jit(solution)/shard_map/ppermute | solution.py:28
  127.6 16.0 %collective-permute-start.31 = (bf16[64,1664]{1,0:T(8,128)(2,1)S(1)}, bf16[64,1664]{1,0:T(8,128)(2,1)S(1)}, u32[]{:S(2)}, u32[]{:S(2)}) collective-permute-start(bf16[64,1664]{1,0:T(8,128)(2,1)S(1)} %collective-permute-done.27.refs_17_.refs_16_), channel_id=1, source_target_pairs={{0,2},{2,0},{4,6},{6,4},{8,10},{10,8},{12,14},{14,12},{16,18},{18,... | collective-permute-start | bytes 638984 | tf_op jit(solution)/shard_map/ppermute | solution.py:28
  127.7 24.3 %collective-permute-start.19 = (bf16[64,1536]{1,0:T(8,128)(2,1)}, bf16[64,1536]{1,0:T(8,128)(2,1)S(1)}, u32[]{:S(2)}, u32[]{:S(2)}) collective-permute-start(bf16[64,1536]{1,0:T(8,128)(2,1)} %multiply_convert_fusion.1.refs_0_.refs_7_), channel_id=1, source_target_pairs={{0,4},{2,6},{4,8},{6,10},{8,12},{10,14},{12,0},{14,2},{16,20},{18,... | collective-permute-start | bytes 589832 | tf_op jit(solution)/shard_map/ppermute | solution.py:28
  205.5 15.5 %collective-permute-start.42 = (bf16[256,512]{1,0:T(8,128)(2,1)S(1)}, bf16[256,512]{1,0:T(8,128)(2,1)S(1)}, u32[]{:S(2)}, u32[]{:S(2)}) collective-permute-start(bf16[256,512]{1,0:T(8,128)(2,1)S(1)} %pad_maximum_fusion.3.refs_0_.refs_8_), channel_id=1, source_target_pairs={{0,8},{2,10},{4,12},{6,14},{8,0},{10,2},{12,4},{14,6},{16,24},{18,... | collective-permute-start | bytes 786440 | tf_op jit(solution)/shard_map/ppermute | solution.py:28
  206.9 14.3 %collective-permute-start.43 = (bf16[256,512]{1,0:T(8,128)(2,1)S(1)}, bf16[256,512]{1,0:T(8,128)(2,1)S(1)}, u32[]{:S(2)}, u32[]{:S(2)}) collective-permute-start(bf16[256,512]{1,0:T(8,128)(2,1)S(1)} %pad_maximum_fusion.3.refs_0_.refs_8_), channel_id=1, source_target_pairs={{0,12},{2,14},{4,0},{6,2},{8,4},{10,6},{12,8},{14,10},{16,28},{18,... | collective-permute-start | bytes 786440 | tf_op jit(solution)/shard_map/ppermute | solution.py:28
  256.4 143.0 %reduce-scatter.3.cloned.1.call-start = ((), (), s32[]{:S(2)}) async-start(), calls=%async_computation.2 | async-start | bytes 5898240 | tf_op jit(solution)/shard_map/reduce_scatter | solution.py:814
  282.7 21.0 %collective-permute-start.59 = (bf16[128,1536]{1,0:T(8,128)(2,1)S(1)}, bf16[128,1536]{1,0:T(8,128)(2,1)S(1)}, u32[]{:S(2)}, u32[]{:S(2)}) collective-permute-start(bf16[128,1536]{1,0:T(8,128)(2,1)S(1)} %get-tuple-element.134), channel_id=1, source_target_pairs={{0,4},{2,6},{4,8},{6,10},{8,12},{10,14},{12,0},{14,2},{16,20},{18,... | collective-permute-start | bytes 1179656 | tf_op jit(solution)/shard_map/ppermute | solution.py:28
  304.7 155.4 %all-gather.26.cloned.1.call-start = ((), (), s32[]{:S(2)}) async-start(), calls=%async_computation.9 | async-start | bytes 3391488 | tf_op jit(solution)/shard_map/all_gather | solution.py:1018
  340.5 14.1 %collective-permute-start.64 = (bf16[256,512]{1,0:T(8,128)(2,1)S(1)}, bf16[256,512]{1,0:T(8,128)(2,1)S(1)}, u32[]{:S(2)}, u32[]{:S(2)}) collective-permute-start(bf16[256,512]{1,0:T(8,128)(2,1)S(1)} %get-tuple-element.140), channel_id=1, source_target_pairs={{0,4},{2,6},{4,8},{6,10},{8,12},{10,14},{12,0},{14,2},{16,20},{18,... | collective-permute-start | bytes 786440 | tf_op jit(solution)/shard_map/ppermute | solution.py:28
  363.8 123.3 %reduce-scatter.5.cloned.1.call-start = ((), (), s32[]{:S(2)}) async-start(), calls=%async_computation.3 | async-start | bytes 5898240 | tf_op jit(solution)/shard_map/reduce_scatter | solution.py:814
  379.5 17.0 %collective-permute-start.70 = (bf16[64,1536]{1,0:T(8,128)(2,1)S(1)}, bf16[64,1536]{1,0:T(8,128)(2,1)S(1)}, u32[]{:S(2)}, u32[]{:S(2)}) collective-permute-start(bf16[64,1536]{1,0:T(8,128)(2,1)S(1)} %get-tuple-element.118.refs_12_), channel_id=1, source_target_pairs={{0,8},{2,10},{4,12},{6,14},{8,0},{10,2},{12,4},{14,6},{16,24},{18,... | collective-permute-start | bytes 589832 | tf_op jit(solution)/shard_map/ppermute | solution.py:28
  381.3 16.5 %collective-permute-start.71 = (bf16[64,1536]{1,0:T(8,128)(2,1)S(1)}, bf16[64,1536]{1,0:T(8,128)(2,1)S(1)}, u32[]{:S(2)}, u32[]{:S(2)}) collective-permute-start(bf16[64,1536]{1,0:T(8,128)(2,1)S(1)} %get-tuple-element.118.refs_12_), channel_id=1, source_target_pairs={{0,12},{2,14},{4,0},{6,2},{8,4},{10,6},{12,8},{14,10},{16,28},{18,... | collective-permute-start | bytes 589832 | tf_op jit(solution)/shard_map/ppermute | solution.py:28
  383.4 14.8 %collective-permute-start.72 = (bf16[64,1536]{1,0:T(8,128)(2,1)S(1)}, bf16[64,1536]{1,0:T(8,128)(2,1)S(1)}, u32[]{:S(2)}, u32[]{:S(2)}) collective-permute-start(bf16[64,1536]{1,0:T(8,128)(2,1)S(1)} %get-tuple-element.118.refs_12_), channel_id=1, source_target_pairs={{0,2},{2,0},{4,6},{6,4},{8,10},{10,8},{12,14},{14,12},{16,18},{18,... | collective-permute-start | bytes 589832 | tf_op jit(solution)/shard_map/ppermute | solution.py:28
  413.4 87.6 %all-gather.28.cloned.1.call-start = ((), (), s32[]{:S(2)}) async-start(), calls=%async_computation.10 | async-start | bytes 1916928 | tf_op jit(solution)/shard_map/all_gather | solution.py:1008
  453.6 134.6 %all-gather.16.cloned.1.call-start = ((), (), s32[]{:S(2)}) async-start(), calls=%async_computation.4 | async-start | bytes 6893568 | tf_op jit(solution)/shard_map/all_gather | solution.py:1044
  458.6 14.4 %collective-permute-start.83 = (bf16[256,512]{1,0:T(8,128)(2,1)}, bf16[256,512]{1,0:T(8,128)(2,1)S(1)}, u32[]{:S(2)}, u32[]{:S(2)}) collective-permute-start(bf16[256,512]{1,0:T(8,128)(2,1)} %get-tuple-element.136), channel_id=1, source_target_pairs={{0,12},{2,14},{4,0},{6,2},{8,4},{10,6},{12,8},{14,10},{16,28},{18,... | collective-permute-start | bytes 786440 | tf_op jit(solution)/shard_map/ppermute | solution.py:28
  458.6 15.3 %collective-permute-start.84 = (bf16[256,512]{1,0:T(8,128)(2,1)}, bf16[256,512]{1,0:T(8,128)(2,1)S(1)}, u32[]{:S(2)}, u32[]{:S(2)}) collective-permute-start(bf16[256,512]{1,0:T(8,128)(2,1)} %get-tuple-element.138), channel_id=1, source_target_pairs={{0,8},{2,10},{4,12},{6,14},{8,0},{10,2},{12,4},{14,6},{16,24},{18,... | collective-permute-start | bytes 786440 | tf_op jit(solution)/shard_map/ppermute | solution.py:28
  459.3 14.9 %collective-permute-start.85 = (bf16[256,512]{1,0:T(8,128)(2,1)S(1)}, bf16[256,512]{1,0:T(8,128)(2,1)S(1)}, u32[]{:S(2)}, u32[]{:S(2)}) collective-permute-start(bf16[256,512]{1,0:T(8,128)(2,1)S(1)} %get-tuple-element.137), channel_id=1, source_target_pairs={{0,4},{2,6},{4,8},{6,10},{8,12},{10,14},{12,0},{14,2},{16,20},{18,... | collective-permute-start | bytes 786440 | tf_op jit(solution)/shard_map/ppermute | solution.py:28
  554.1 31.3 %collective-permute-start.108 = (bf16[2304,256]{1,0:T(8,128)(2,1)S(1)}, bf16[2304,256]{1,0:T(8,128)(2,1)S(1)}, u32[]{:S(2)}, u32[]{:S(2)}) collective-permute-start(bf16[2304,256]{1,0:T(8,128)(2,1)S(1)} %select_select_fusion), channel_id=1, source_target_pairs={{0,64},{64,0},{1,65},{65,1},{2,66},{66,2},{3,67},{67,3},{4,68},{68... | collective-permute-start | bytes 3538952 | tf_op jit(solution)/shard_map/ppermute | solution.py:32
  555.2 29.1 %collective-permute-start.93 = (bf16[64,1536]{1,0:T(8,128)(2,1)S(1)}, bf16[64,1536]{1,0:T(8,128)(2,1)S(1)}, u32[]{:S(2)}, u32[]{:S(2)}) collective-permute-start(bf16[64,1536]{1,0:T(8,128)(2,1)S(1)} %get-tuple-element.116), channel_id=1, source_target_pairs={{0,64},{64,0},{1,65},{65,1},{2,66},{66,2},{3,67},{67,3},{4,68},{68... | collective-permute-start | bytes 589832 | tf_op jit(solution)/shard_map/ppermute | solution.py:32
  (179 other events, 1435.0 us)
Sparse Core Ops, SparseCore 0:
  20.2 56.3 all-gather.17
  79.2 55.7 all-gather.19
  137.2 53.0 all-gather.21
  256.6 41.0 all-gather.23
  304.8 51.4 reduce-scatter.2
  363.9 31.2 all-gather.25
  413.5 50.3 reduce-scatter.4
  465.6 24.8 all-gather.27
  535.8 49.1 all-gather.15
